TPU v7x, 512 devices: a whole 4x4x16 slice. The times are simulated.
512 devices in a mesh: dp: 64 (over z, x), tensor: 8 (over y, core).
Axes of the slice: x: 4, y: 4, z: 16, core: 2. Of those that a mesh axis runs over, the one named last changes fastest.
Arguments:
- pool: bfloat16 [65536, 4096], P('dp', 'tensor'), may hold values from -6 to 6
- picks: int32 [256], P('dp'), may hold values from 0 to 1023
- targets: bfloat16 [256, 4096], P(None, 'dp'), may hold values from -6 to 6
- gate_weight: bfloat16 [4096, 7168], P('dp', 'tensor'), may hold values from -0.09375 to 0.09375
- up_weight: bfloat16 [4096, 7168], P('dp', 'tensor'), may hold values from -0.09375 to 0.09375
- down_weight: bfloat16 [7168, 4096], P('tensor', 'dp'), may hold values from -0.0625 to 0.0625
- probe_gate: float32 [4096, 7168], P('dp', 'tensor'), may hold values from -6 to 6
- probe_up: float32 [4096, 7168], P('dp', 'tensor'), may hold values from -6 to 6
- probe_down: float32 [7168, 4096], P('tensor', 'dp'), may hold values from -6 to 6
Outputs:
- final_gate: float32 [4096, 7168], P('dp', 'tensor')
- final_up: float32 [4096, 7168], P('dp', 'tensor')
- final_down: float32 [7168, 4096], P('tensor', 'dp')
- rayleigh: float32 [], replicated
Inputs may be any that keep to these rules, and one draw needn't show every extreme that they name: `picks`: a token's pool row lies in the block of 1024 rows held by the dp index that owns the token.
All inputs are finite; a program needn't handle non-finite values.
Results may differ from a plain program's by a relative error of at most 0.0085.
Values may be sent and summed in bfloat16 or wider, within the bound.
No kernel may reach another device: no remote copies, remote signals or barrier semaphores. Data moves between devices by JAX's collectives and lax.ppermute only.
A program may use at most 64 MiB of HBM per device.

v0:
```python
import jax
import jax.numpy as jnp
from jax import lax
from jax.sharding import PartitionSpec as P

D = 4096
FF = 7168
ITERS = 2


def silu_parts(values):
    sigmoid_val = jax.nn.sigmoid(values)
    activated = values * sigmoid_val
    slope_one = sigmoid_val * (1.0 + values * (1.0 - sigmoid_val))
    slope_two = sigmoid_val * (1.0 - sigmoid_val) * (2.0 + values * (1.0 - 2.0 * sigmoid_val))
    return (activated, slope_one, slope_two)


def matmul_plain(former, latter):
    return jnp.dot(former, latter, preferred_element_type=jnp.float32)


def matmul_tn(former, latter):
    return lax.dot_general(
        former, latter, (((0,), (0,)), ((), ())), preferred_element_type=jnp.float32
    )


def matmul_nt(former, latter):
    return lax.dot_general(
        former, latter, (((1,), (1,)), ((), ())), preferred_element_type=jnp.float32
    )


def body(
    pool, picks, targets, gate_weight, up_weight, down_weight, probe_gate, probe_up, probe_down
):
    chosen = jnp.take(pool, picks, axis=0)
    widened = lax.all_gather(chosen, "tensor", axis=1, tiled=True)
    inputs = lax.all_to_all(widened, "dp", split_axis=1, concat_axis=0, tiled=True)
    tokens = inputs.shape[0]
    gate_part = matmul_plain(inputs, gate_weight)
    upper_part = matmul_plain(inputs, up_weight)
    gate_val, upper_val = (
        lax.psum_scatter(gate_part, "dp", scatter_dimension=0, tiled=True),
        lax.psum_scatter(upper_part, "dp", scatter_dimension=0, tiled=True),
    )
    activated, slope_one, slope_two = silu_parts(gate_val)
    hidden_local = (activated * upper_val).astype(jnp.bfloat16)
    hidden = lax.all_gather(hidden_local, "dp", axis=0, tiled=True)
    output = lax.psum(matmul_plain(hidden, down_weight), "tensor")
    resid_b = ((output - targets.astype(jnp.float32)) / tokens).astype(jnp.bfloat16)
    back_part = matmul_nt(resid_b, down_weight)
    back_val = lax.psum_scatter(back_part, "dp", scatter_dimension=0, tiled=True)
    back_act = back_val * upper_val
    count = 3.0 * D * FF
    vectors = (probe_gate, probe_up, probe_down)
    quotient = jnp.zeros((), jnp.float32)
    for iteration in range(ITERS):
        gate_probe = vectors[0].astype(jnp.bfloat16)
        upper_probe = vectors[1].astype(jnp.bfloat16)
        down_probe = vectors[2].astype(jnp.bfloat16)
        tan_gate_part = matmul_plain(inputs, gate_probe)
        tan_upper_part = matmul_plain(inputs, upper_probe)
        tan_gate, tan_upper = (
            lax.psum_scatter(tan_gate_part, "dp", scatter_dimension=0, tiled=True),
            lax.psum_scatter(tan_upper_part, "dp", scatter_dimension=0, tiled=True),
        )
        tan_act = slope_one * tan_gate
        tan_local = (tan_act * upper_val + activated * tan_upper).astype(jnp.bfloat16)
        tan_hidden = lax.all_gather(tan_local, "dp", axis=0, tiled=True)
        tan_out_part = matmul_plain(tan_hidden, down_weight) + matmul_plain(hidden, down_probe)
        tan_out = lax.psum(tan_out_part, "tensor")
        tan_resid = (tan_out / tokens).astype(jnp.bfloat16)
        hv_down = matmul_tn(tan_hidden, resid_b) + matmul_tn(hidden, tan_resid)
        tan_back_part = matmul_nt(tan_resid, down_weight) + matmul_nt(resid_b, down_probe)
        tan_back = lax.psum_scatter(tan_back_part, "dp", scatter_dimension=0, tiled=True)
        delta_up_local = (tan_back * activated + back_val * tan_act).astype(jnp.bfloat16)
        delta_gate_local = (
            (tan_back * upper_val + back_val * tan_upper) * slope_one
            + back_act * slope_two * tan_gate
        ).astype(jnp.bfloat16)
        delta_gate, delta_up = (
            lax.all_gather(delta_gate_local, "dp", axis=0, tiled=True),
            lax.all_gather(delta_up_local, "dp", axis=0, tiled=True),
        )
        hv_gate = matmul_tn(inputs, delta_gate)
        hv_up = matmul_tn(inputs, delta_up)
        square_local = (
            jnp.sum(hv_gate * hv_gate) + jnp.sum(hv_up * hv_up) + jnp.sum(hv_down * hv_down)
        )
        if iteration + 1 < ITERS:
            square = lax.psum(square_local, ("dp", "tensor"))
        else:
            inner_local = (
                jnp.sum(vectors[0] * hv_gate)
                + jnp.sum(vectors[1] * hv_up)
                + jnp.sum(vectors[2] * hv_down)
            )
            inner, square = lax.psum((inner_local, square_local), ("dp", "tensor"))
            quotient = inner / count
        norm_val = jnp.sqrt(square / count + 1e-06)
        vectors = (hv_gate / norm_val, hv_up / norm_val, hv_down / norm_val)
    return (vectors[0], vectors[1], vectors[2], quotient)


def solution(mesh):
    placed = (
        P("dp", "tensor"),
        P("dp"),
        P(None, "dp"),
        P("dp", "tensor"),
        P("dp", "tensor"),
        P("tensor", "dp"),
        P("dp", "tensor"),
        P("dp", "tensor"),
        P("tensor", "dp"),
    )
    return jax.shard_map(
        body,
        mesh=mesh,
        in_specs=placed,
        out_specs=(P("dp", "tensor"), P("dp", "tensor"), P("tensor", "dp"), P()),
        check_vma=False,
    )
```

profile of v0, /device:TPU:1, one launch (start us, length us, event | category | flops | bytes accessed | tf_op | source)
XLA Modules:
  0.0 2221.6 jit_solution(13146561198980390981)
XLA Ops:
  9.1 19.5 all_gather.24
  28.8 26.7 %all_to_all.19 = bf16[64,2,128]{2,1,0:T(2,128)(2,1)S(1)} all-to-all(bf16[64,2,128]{2,1,0:T(2,128)(2,1)S(1)} %reshape.48), channel_id=1, replica_groups=mesh['dp'=64,'tensor'=8] {'dp'}, dimensions={0} | all-to-all | bytes 65536 | tf_op jit(solution)/shard_map/all_to_all | solution.py:40
  55.6 1.2 fusion.4
  56.8 1.2 fusion.31
  58.0 1.2 fusion.6
  59.2 1.2 fusion.30
  60.5 1.3 dynamic-slice
  62.4 267.3 %all-reduce.29.cloned.1.call-done = (f32[256,896]{1,0:T(8,128)}, f32[256,896]{1,0:T(8,128)}, f32[256,896]{1,0:T(8,128)}, f32[256,896]{1,0:T(8,128)}) async-done(((f32[256,896]{1,0:T(8,128)}, f32[256,896]{1,0:T(8,128)}, f32[256,896]{1,0:T(8,128)}, f32[256,896]{1,0:T(8,128)}), (f32[256,896]{1,0:T(8,128)}, f32[256,896]{1,0:T(8,128)}, f32[256,896]{1,0:T(8,128)}, ...) | async-done | bytes 3670032
  330.6 71.7 %all-gather.1 = bf16[64,4,896]{2,1,0:T(4,128)(2,1)S(1)} all-gather(bf16[1,4,896]{2,1,0:T(4,128)(2,1)S(1)} %get-tuple-element.26), channel_id=1, replica_groups=mesh['dp'=64,'tensor'=8] {'dp'}, dimensions={0}, use_global_device_ids=true | all-gather | bytes 465920 | tf_op jit(solution)/shard_map/all_gather | solution.py:50
  402.4 72.4 %all-gather = bf16[64,4,896]{2,1,0:T(4,128)(2,1)S(1)} all-gather(bf16[1,4,896]{2,1,0:T(4,128)(2,1)S(1)} %get-tuple-element.27), channel_id=1, replica_groups=mesh['dp'=64,'tensor'=8] {'dp'}, dimensions={0}, use_global_device_ids=true | all-gather | bytes 465920 | tf_op jit(solution)/shard_map/all_gather | solution.py:71
  475.7 0.9 fusion.33
  477.5 0.9 convolution_add_fusion.5
  478.5 128.5 %all-reduce.31.cloned.1.call-done = (f32[256,64]{0,1:T(8,128)}, f32[256,64]{0,1:T(8,128)}) async-done(((f32[256,64]{0,1:T(8,128)}, f32[256,64]{0,1:T(8,128)}), (f32[256,64]{0,1:T(8,128)}, f32[256,64]{0,1:T(8,128)})) %all-reduce.31.cloned.1.call-update) | async-done | bytes 131088 | tf_op jit(solution)/shard_map/psum | solution.py:73
  607.1 1.2 fusion.15
  608.3 1.3 fusion.34
  609.5 1.3 convolution_add_fusion.1
  612.5 267.6 %all-reduce.27.cloned.1.call-done = (f32[256,896]{1,0:T(8,128)}, f32[256,896]{1,0:T(8,128)}) async-done(((f32[256,896]{1,0:T(8,128)}, f32[256,896]{1,0:T(8,128)}), (f32[256,896]{1,0:T(8,128)}, f32[256,896]{1,0:T(8,128)})) %all-reduce.27.cloned.1.call-update) | async-done | bytes 1835024
  881.0 72.7 %all-gather.3 = bf16[64,4,896]{2,1,0:T(4,128)(2,1)S(1)} all-gather(bf16[1,4,896]{2,1,0:T(4,128)(2,1)S(1)} %get-tuple-element.24), channel_id=1, replica_groups=mesh['dp'=64,'tensor'=8] {'dp'}, dimensions={0}, use_global_device_ids=true | all-gather | bytes 465920 | tf_op jit(solution)/shard_map/all_gather | solution.py:85
  954.6 72.5 %all-gather.2 = bf16[64,4,896]{2,1,0:T(4,128)(2,1)S(1)} all-gather(bf16[1,4,896]{2,1,0:T(4,128)(2,1)S(1)} %get-tuple-element.25), channel_id=1, replica_groups=mesh['dp'=64,'tensor'=8] {'dp'}, dimensions={0}, use_global_device_ids=true | all-gather | bytes 465920 | tf_op jit(solution)/shard_map/all_gather | solution.py:84
  1030.0 160.2 %psum.44 = f32[]{:T(128)} all-reduce(f32[]{:T(128)S(6)} %add.121), channel_id=1, replica_groups=mesh['dp'=64,'tensor'=8] {'dp','tensor'}, use_global_device_ids=true, to_apply=%region_11.12 | all-reduce | flops 1 | bytes 8 | tf_op jit(solution)/shard_map/psum | solution.py:93
  1190.9 1.2 fusion.2
  1192.1 1.2 fusion
  1193.4 262.0 %all-reduce.25.cloned.1.call-done = (f32[256,896]{1,0:T(8,128)}, f32[256,896]{1,0:T(8,128)}) async-done(((f32[256,896]{1,0:T(8,128)}, f32[256,896]{1,0:T(8,128)}), (f32[256,896]{1,0:T(8,128)}, f32[256,896]{1,0:T(8,128)})) %all-reduce.25.cloned.1.call-update) | async-done | bytes 1835024
  1456.2 72.7 %all-gather.4 = bf16[64,4,896]{2,1,0:T(4,128)(2,1)S(1)} all-gather(bf16[1,4,896]{2,1,0:T(4,128)(2,1)S(1)} %fusion.20), channel_id=1, replica_groups=mesh['dp'=64,'tensor'=8] {'dp'}, dimensions={0}, use_global_device_ids=true | all-gather | bytes 465920 | tf_op jit(solution)/shard_map/all_gather | solution.py:71
  1529.3 0.9 convolution_add_fusion.4
  1530.5 102.6 %all-reduce.21.cloned.1.call-done = f32[256,64]{0,1:T(8,128)} async-done(((f32[256,64]{0,1:T(8,128)}), f32[256,64]{0,1:T(8,128)}) %all-reduce.21.cloned.1.call-update) | async-done | bytes 65552 | tf_op jit(solution)/shard_map/psum | solution.py:73
  1633.0 1.1 fusion.16
  1634.2 1.3 convolution_add_fusion
  1637.2 260.8 %all-reduce.23.cloned.1.call-done = f32[256,896]{1,0:T(8,128)} async-done(((f32[256,896]{1,0:T(8,128)}), f32[256,896]{1,0:T(8,128)}) %all-reduce.23.cloned.1.call-update) | async-done | bytes 917520
  1898.8 72.6 %all-gather.6 = bf16[64,4,896]{2,1,0:T(4,128)(2,1)S(1)} all-gather(bf16[1,4,896]{2,1,0:T(4,128)(2,1)S(1)} %get-tuple-element.22), channel_id=1, replica_groups=mesh['dp'=64,'tensor'=8] {'dp'}, dimensions={0}, use_global_device_ids=true | all-gather | bytes 465920 | tf_op jit(solution)/shard_map/all_gather | solution.py:85
  1972.3 73.5 %all-gather.5 = bf16[64,4,896]{2,1,0:T(4,128)(2,1)S(1)} all-gather(bf16[1,4,896]{2,1,0:T(4,128)(2,1)S(1)} %get-tuple-element.23), channel_id=1, replica_groups=mesh['dp'=64,'tensor'=8] {'dp'}, dimensions={0}, use_global_device_ids=true | all-gather | bytes 465920 | tf_op jit(solution)/shard_map/all_gather | solution.py:84
  2050.5 160.3 %all-reduce.9 = (f32[]{:T(128)}, f32[]{:T(128)}) all-reduce(f32[]{:T(128)S(6)} %add.131, f32[]{:T(128)S(6)} %add.134), channel_id=1, replica_groups=mesh['dp'=64,'tensor'=8] {'dp','tensor'}, use_global_device_ids=true, to_apply=%region_19.20 | all-reduce | flops 2 | bytes 16 | tf_op jit(solution)/shard_map/psum | solution.py:100
  (69 shorter events, 17.1 us)
Async XLA Ops:
  7.2 1.3 copy-start
  7.2 0.8 copy-start.11
  7.2 322.5 %all-reduce.29.cloned.1.call-start = ((), (), s32[]{:S(2)}) async-start(), calls=%async_computation.5 | async-start | bytes 7340032
  28.6 27.1 %copy-start.4 = (f32[64,896]{1,0:T(8,128)S(1)}, f32[64,896]{1,0:T(8,128)}, u32[]{:S(2)}) copy-start(f32[64,896]{1,0:T(8,128)} %param.16) | copy-start | bytes 688132
  55.6 1.2 copy-start.6
  56.8 1.2 copy-start.5
  58.0 1.2 copy-start.7
  60.5 546.6 %all-reduce.31.cloned.1.call-start = ((), (), s32[]{:S(2)}) async-start(), calls=%async_computation.6 | async-start | bytes 262144 | tf_op jit(solution)/shard_map/psum | solution.py:73
  474.8 0.9 copy-start.1
  476.6 0.9 copy-start.2
  478.5 401.6 %all-reduce.27.cloned.1.call-start = ((), (), s32[]{:S(2)}) async-start(), calls=%async_computation.4 | async-start | bytes 3670016
  607.0 1.2 copy-start.9
  607.0 1.2 copy-start.10
  610.8 0.8 copy-start.3
  610.8 844.5 %all-reduce.25.cloned.1.call-start = ((), (), s32[]{:S(2)}) async-start(), calls=%async_computation.3 | async-start | bytes 3670016
  1193.3 439.7 %all-reduce.21.cloned.1.call-start = ((), (), s32[]{:S(2)}) async-start(), calls=%async_computation.1 | async-start | bytes 131072 | tf_op jit(solution)/shard_map/psum | solution.py:73
  1530.2 367.7 %all-reduce.23.cloned.1.call-start = ((), (), s32[]{:S(2)}) async-start(), calls=%async_computation.2 | async-start | bytes 1835008
  1635.5 0.8 copy-start.8
Sparse Core Ops, SparseCore 0:
  60.6 269.0 all-reduce.28
  478.6 128.4 all-reduce.30
  611.0 269.1 all-reduce.26
  1193.4 261.9 all-reduce.24
  1530.3 102.6 all-reduce.20
  1636.6 261.2 all-reduce.22
where the time goes:
time: 2220 us
  waiting for transfers between devices  1290 us (58%)
  blocking collectives  875 us (39%)
  between operations  23.9 us (1%)
    unnamed x10, waiting for transfers between devices  1060 us
    psum x2, waiting for transfers between devices, body(): tan_out = lax.psum(tan_out_part, 'tensor')  231 us
    psum x1, blocking collectives, body(): inner, square = lax.psum((inner_local, square_local), ('dp', 'tensor'))  160 us
    psum x1, blocking collectives, body(): square = lax.psum(square_local, ('dp', 'tensor'))  160 us
    all_gather x2, blocking collectives, body(): lax.all_gather(delta_gate_local, 'dp', axis=0, tiled=True)  146 us
    all_gather x2, blocking collectives, body(): lax.all_gather(delta_up_local, 'dp', axis=0, tiled=True)  145 us
    all_gather x2, blocking collectives, body(): tan_hidden = lax.all_gather(tan_local, 'dp', axis=0, tiled=True)  145 us
    all_gather x1, blocking collectives, body(): hidden = lax.all_gather(hidden_local, 'dp', axis=0, tiled=True)  71.7 us
  transfers between devices with their start and end apart: 6, of which 6 were waited for; matrix products, arithmetic and copies ran while one was open for 0% of the time, Pallas kernels for 0%

commit v1 on v0

v1 whole, which is shorter than its diff:
```python
import jax
import jax.numpy as jnp
from jax import lax
from jax.sharding import Mesh
from jax.sharding import PartitionSpec as P

AXES = ("z", "x", "y", "core")
SIZES = (16, 4, 4, 2)
XYC = ("x", "y", "core")
BF = jnp.bfloat16
F32 = jnp.float32


def dot(a, b, ca, cb):
    return lax.dot_general(a, b, (((ca,), (cb,)), ((), ())), preferred_element_type=F32)


def exchange(v, axes):
    return lax.all_to_all(v, axes, split_axis=0, concat_axis=0, tiled=True)


def gather(v, axes, n):
    return exchange(jnp.broadcast_to(v[None], (n,) + v.shape), axes)


def two_terms(v):
    high = lax.reduce_precision(v, 8, 7)
    return high.astype(BF), (v - high).astype(BF)


def silu_parts(values):
    s = jax.nn.sigmoid(values)
    activated = values * s
    slope_one = s * (1.0 + values * (1.0 - s))
    slope_two = s * (1.0 - s) * (2.0 + values * (1.0 - 2.0 * s))
    return activated, slope_one, slope_two


def make_body(nz, nx, ny, nc):
    nt = ny * nc
    nr = nx * nt

    def body(pool, picks, targets, gate_w, up_w, down_w, probe_g, probe_u, probe_d):
        tok_dev = picks.shape[0]
        tokens = targets.shape[0]
        d_dev, ff_dev = gate_w.shape
        ff = ff_dev // nx
        dz = d_dev * nx
        sub = ff // nz
        rows = dz // nr
        count = 3.0 * (dz * nz) * (ff_dev * nt)

        chosen = pool.at[picks].get(mode="promise_in_bounds")
        wide = gather(chosen, ("y", "core"), nt)
        wide = wide.transpose(1, 0, 2).reshape(tok_dev, nz, dz).transpose(1, 0, 2)
        wide = jnp.broadcast_to(wide[:, None], (nz, nx, tok_dev, dz))
        inputs = exchange(wide.reshape(nz * nx, tok_dev, dz), ("z", "x")).reshape(tokens, dz)

        mats = jnp.stack(
            [
                gate_w,
                up_w,
                probe_g.astype(BF),
                probe_u.astype(BF),
                down_w.T,
                probe_d.T.astype(BF),
            ]
        )
        mats = mats.reshape(6, d_dev, nx, ff).transpose(2, 0, 1, 3)
        mats = exchange(mats, "x").transpose(1, 0, 2, 3).reshape(6, dz, ff)
        down, pdown = mats[4], mats[5]

        first = lax.dot_general(
            mats[:4], inputs, (((1,), (1,)), ((), ())), preferred_element_type=F32
        )
        own = lax.axis_index(XYC)
        gram_rows = tokens // nr
        mine = lax.dynamic_slice_in_dim(inputs, own * gram_rows, gram_rows, 0)
        gram = jnp.concatenate(two_terms(dot(mine, inputs, 1, 1)))
        packed = first.astype(BF).reshape(4, nz, sub, tokens).transpose(1, 0, 2, 3)
        packed = packed.reshape(nz, 4 * sub, tokens)
        packed = jnp.concatenate(
            [packed, jnp.broadcast_to(gram[None], (nz,) + gram.shape)], axis=1
        )
        got = jnp.sum(exchange(packed, "z").astype(F32), axis=0)
        gate_val, upper, tan_gate, tan_upper = (
            got[i * sub : (i + 1) * sub] for i in range(4)
        )
        gram = got[4 * sub : 4 * sub + gram_rows] + got[4 * sub + gram_rows :]
        activated, slope_one, slope_two = silu_parts(gate_val)
        hidden = (activated * upper).astype(BF)
        tan_act = slope_one * tan_gate
        tan_hidden = (tan_act * upper + activated * tan_upper).astype(BF)
        both = gather(jnp.concatenate([hidden, tan_hidden]), "z", nz)
        hidden = both[:, :sub].reshape(ff, tokens)
        tan_hidden = both[:, sub:].reshape(ff, tokens)

        out = dot(down, hidden, 1, 0)
        tan_out = dot(down, tan_hidden, 1, 0) + dot(pdown, hidden, 1, 0)
        packed = jnp.stack([out.astype(BF), tan_out.astype(BF)])
        packed = packed.reshape(2, nr, rows, tokens).transpose(1, 0, 2, 3)
        got = jnp.sum(exchange(packed, XYC).astype(F32), axis=0)
        wanted = lax.dynamic_slice_in_dim(
            targets.T, lax.axis_index(("y", "core")) * rows, rows, 0
        )
        resid = ((got[0] - wanted.astype(F32)) / tokens).astype(BF)
        tan_resid = (got[1] / tokens).astype(BF)
        packed = jnp.concatenate([resid, tan_resid, *two_terms(gram)])
        both = gather(packed, XYC, nr)
        resid = both[:, :rows].reshape(dz, tokens)
        tan_resid = both[:, rows : 2 * rows].reshape(dz, tokens)
        gram_hi = both[:, 2 * rows : 2 * rows + gram_rows].reshape(tokens, tokens)
        gram_lo = both[:, 2 * rows + gram_rows :].reshape(tokens, tokens)

        def by_gram(v):
            return dot(v, gram_hi, 1, 0) + dot(v, gram_lo, 1, 0)

        back = dot(down, resid, 0, 0)
        tan_back = dot(down, tan_resid, 0, 0) + dot(pdown, resid, 0, 0)
        packed = jnp.stack([back.astype(BF), tan_back.astype(BF)])
        packed = packed.reshape(2, nz, sub, tokens).transpose(1, 0, 2, 3)
        got = jnp.sum(exchange(packed, "z").astype(F32), axis=0)
        back, tan_back = got[0], got[1]
        hv_down = dot(resid, tan_hidden, 1, 1) + dot(tan_resid, hidden, 1, 1)

        def deltas(tan_back, tan_gate, tan_upper):
            up = tan_back * activated + back * (slope_one * tan_gate)
            gate = (tan_back * upper + back * tan_upper) * slope_one + (
                back * upper
            ) * slope_two * tan_gate
            return jnp.concatenate([gate.astype(BF), up.astype(BF)])

        delta = deltas(tan_back, tan_gate, tan_upper)

        tangents = by_gram(delta)
        square = jnp.sum(delta.astype(F32) * tangents) + jnp.sum(hv_down * hv_down)
        tan_gate, tan_upper = tangents[:sub], tangents[sub:]
        tan_hidden = ((slope_one * tan_gate) * upper + activated * tan_upper).astype(BF)

        def rows_of(*values):
            terms = [t for v in values for t in two_terms(v)]
            return jnp.stack([jnp.broadcast_to(t, (tokens,)) for t in terms])

        both = gather(jnp.concatenate([tan_hidden, rows_of(square)]), "z", nz)
        tan_hidden = both[:, :sub].reshape(ff, tokens)
        square = jnp.sum(both[:, sub:, 0].astype(F32))

        hv_down_b = hv_down.astype(BF)
        tan_out = dot(down, tan_hidden, 1, 0) + dot(hv_down_b, hidden, 1, 0)
        packed = tan_out.astype(BF).reshape(nr, rows, tokens)
        scal = jnp.broadcast_to(rows_of(square)[None], (nr, 2, tokens))
        got = exchange(jnp.concatenate([packed, scal], axis=1), XYC)
        square = jnp.sum(got[:, rows:, 0].astype(F32))
        got = jnp.sum(got[:, :rows].astype(F32), axis=0)
        scale = 1.0 / jnp.sqrt(square / count + 1e-6)
        tan_resid = (got / tokens).astype(BF)
        tan_resid = gather(tan_resid, XYC, nr).reshape(dz, tokens)

        tan_back = dot(down, tan_resid, 0, 0) + dot(hv_down_b, resid, 0, 0)
        packed = tan_back.astype(BF).reshape(nz, sub, tokens)
        tan_back = jnp.sum(exchange(packed, "z").astype(F32), axis=0)
        hv_down2 = (dot(resid, tan_hidden, 1, 1) + dot(tan_resid, hidden, 1, 1)) * scale

        tangents = tangents * scale
        delta = deltas(tan_back * scale, tangents[:sub], tangents[sub:])
        wide = delta.astype(F32)
        inner = jnp.sum(tangents * wide) + jnp.sum((hv_down * scale) * hv_down2)
        square = jnp.sum(by_gram(delta) * wide) + jnp.sum(hv_down2 * hv_down2)
        both = gather(jnp.concatenate([delta, rows_of(inner, square)]), "z", nz)
        delta_gate = both[:, :sub].reshape(ff, tokens)
        delta_up = both[:, sub : 2 * sub].reshape(ff, tokens)
        inner = jnp.sum(both[:, 2 * sub : 2 * sub + 2, 0].astype(F32))
        square = jnp.sum(both[:, 2 * sub + 2 :, 0].astype(F32))
        sums = jnp.stack([inner, square])
        sums = jnp.broadcast_to(sums[:, None], (2, 128))
        sums = jnp.sum(gather(sums, XYC, nr), axis=0)
        inner, square = sums[0, 0], sums[1, 0]
        scale = 1.0 / jnp.sqrt(square / count + 1e-6)

        hv = jnp.stack(
            [
                dot(inputs, delta_gate, 0, 1).astype(BF),
                dot(inputs, delta_up, 0, 1).astype(BF),
                hv_down2.astype(BF),
            ]
        )
        hv = hv.reshape(3, nx, d_dev, ff).transpose(1, 0, 2, 3)
        hv = exchange(hv, "x").transpose(1, 2, 0, 3).reshape(3, d_dev, ff_dev)
        hv = hv.astype(F32) * scale
        return hv[0], hv[1], hv[2].T, inner / count

    return body


def build(devices, sizes):
    wide = Mesh(devices.reshape(sizes), AXES)
    dp, tensor = ("z", "x"), ("y", "core")
    placed = (
        P(dp, tensor),
        P(dp),
        P(None, dp),
        P(dp, tensor),
        P(dp, tensor),
        P(tensor, dp),
        P(dp, tensor),
        P(dp, tensor),
        P(tensor, dp),
    )
    return jax.shard_map(
        make_body(*sizes),
        mesh=wide,
        in_specs=placed,
        out_specs=(P(dp, tensor), P(dp, tensor), P(tensor, dp), P()),
        check_vma=False,
    )


def solution(mesh):
    return build(mesh.devices, SIZES)
```

time: 2220 us -> 314 us (0.14)
  waiting for transfers between devices: 1290 us -> 93.1 us
  blocking collectives: 875 us -> 99 us
  starting transfers between devices: 0.43 us -> 73.6 us
    unnamed x10 -> x0, waiting for transfers between devices: 1060 us -> none
    all_gather x8 -> x0, blocking collectives: 527 us -> none  [the longest x2 146 us: body(): lax.all_gather(delta_gate_local, 'dp', axis=0, tiled=True)]
    psum x2 -> x0, blocking collectives: 320 us -> none  [the longest x1 160 us: body(): inner, square = lax.psum((inner_local, square_local), ('dp', 'tensor'))]
    psum x2 -> x0, waiting for transfers between devices: 231 us -> none  [body(): tan_out = lax.psum(tan_out_part, 'tensor')]
    all_to_all x0 -> x10, waiting for transfers between devices: none -> 93.1 us  [exchange(): return lax.all_to_all(v, axes, split_axis=0, concat_axis=0, tiled=True)]
    all_to_all x0 -> x10, starting transfers between devices: none -> 73.6 us  [exchange(): return lax.all_to_all(v, axes, split_axis=0, concat_axis=0, tiled=True)]
    all_to_all x1 -> x5, blocking collectives: 26.7 us -> 99 us  [exchange(): return lax.all_to_all(v, axes, split_axis=0, concat_axis=0, tiled=True)]
  transfers between devices with their start and end apart: 6 -> 10, of which waited for: 6 -> 10; matrix products, arithmetic and copies ran while one was open for 0% -> 3% of each run, Pallas kernels for 0% -> 0%
where the time goes in v1:
time: 314 us; the launch traced here: 313 us
  blocking collectives  99 us (32%)
  waiting for transfers between devices  93.1 us (30%)
  starting transfers between devices  73.6 us (23%)
  between operations  16.9 us (5%)
  local copies, waits for them, and re-layouts  16.4 us (5%)
  other arithmetic  7.22 us (2%)
  matrix products  6.8 us (2%)
    all_to_all x5, blocking collectives, exchange(): return lax.all_to_all(v, axes, split_axis=0, concat_axis=0, tiled=True)  99 us
    all_to_all x10, waiting for transfers between devices, exchange(): return lax.all_to_all(v, axes, split_axis=0, concat_axis=0, tiled=True)  93.1 us
    all_to_all x10, starting transfers between devices, exchange(): return lax.all_to_all(v, axes, split_axis=0, concat_axis=0, tiled=True)  73.6 us
    dot_general x21, matrix products, dot(): lax.dot_general(a, b, (((ca,), (cb,)), ((), ())), preferred_element_type=...  6.45 us
  transfers between devices with their start and end apart: 10, of which 10 were waited for; matrix products, arithmetic and copies ran while one was open for 3% of the time, Pallas kernels for 0%

profile of v1, /device:TPU:1, one launch (start us, length us, event | category | flops | bytes accessed | tf_op | source)
XLA Modules:
  0.0 313.0 jit_solution(14199026267879409556)
XLA Ops:
  3.1 10.1 %all-to-all-start = ((bf16[8,4,512]{2,1,0:T(4,128)(2,1)}), bf16[8,4,512]{2,1,0:T(4,128)(2,1)S(1)}, u32[]{:S(2)}, u32[]{:S(2)}) async-start(bf16[8,4,512]{2,1,0:T(4,128)(2,1)} %broadcast_in_dim.21), calls=%async_computation | async-start | bytes 65536 | tf_op jit(solution)/shard_map/all_to_all | solution.py:19
  13.2 1.1 stack.63
  14.4 1.1 stack.64
  16.6 1.3 all-to-all-done
  17.9 13.7 %all_to_all.75 = bf16[4,6,64,224]{3,2,1,0:T(8,128)(2,1)S(1)} all-to-all(bf16[4,6,64,224]{3,2,1,0:T(8,128)(2,1)S(1)} %copy.116), channel_id=1, replica_groups=mesh['z'=16,'x'=4,'y'=4,'core'=2] {'x'}, dimensions={0} | all-to-all | bytes 1376256 | tf_op jit(solution)/shard_map/all_to_all | solution.py:19
  32.4 13.6 %all-to-all-start.1 = ((bf16[64,4,256]{2,1,0:T(4,128)(2,1)}), bf16[64,4,256]{2,1,0:T(4,128)(2,1)S(1)}, u32[]{:S(2)}, u32[]{:S(2)}) async-start(bf16[64,4,256]{2,1,0:T(4,128)(2,1)} %bitcast.3), calls=%async_computation.1 | async-start | bytes 262144 | tf_op jit(solution)/shard_map/all_to_all | solution.py:19
  46.1 14.9 %all-to-all-done.1 = bf16[64,4,256]{2,1,0:T(4,128)(2,1)S(1)} async-done(((bf16[64,4,256]{2,1,0:T(4,128)(2,1)}), bf16[64,4,256]{2,1,0:T(4,128)(2,1)S(1)}, u32[]{:S(2)}, u32[]{:S(2)}) %all-to-all-start.1) | async-done | bytes 131104 | tf_op jit(solution)/shard_map/all_to_all | solution.py:19
  62.3 33.6 %all_to_all.76 = bf16[16,72,256]{2,1,0:T(8,128)(2,1)S(1)} all-to-all(bf16[16,72,256]{2,1,0:T(8,128)(2,1)S(1)} %copy.121), channel_id=1, replica_groups=mesh['z'=16,'x'=4,'y'=4,'core'=2] {'z'}, dimensions={0} | all-to-all | bytes 1179648 | tf_op jit(solution)/shard_map/all_to_all | solution.py:19
  96.8 6.9 %all-to-all-start.4 = ((bf16[16,28,256]{2,1,0:T(8,128)(2,1)}), bf16[16,28,256]{2,1,0:T(8,128)(2,1)S(1)}, u32[]{:S(2)}, u32[]{:S(2)}) async-start(bf16[16,28,256]{2,1,0:T(8,128)(2,1)} %broadcast_in_dim.24), calls=%async_computation.4 | async-start | bytes 524288 | tf_op jit(solution)/shard_map/all_to_all | solution.py:19
  103.7 12.8 %all-to-all-done.4 = bf16[16,28,256]{2,1,0:T(8,128)(2,1)S(1)} async-done(((bf16[16,28,256]{2,1,0:T(8,128)(2,1)}), bf16[16,28,256]{2,1,0:T(8,128)(2,1)S(1)}, u32[]{:S(2)}, u32[]{:S(2)}) %all-to-all-start.4) | async-done | bytes 229408 | tf_op jit(solution)/shard_map/all_to_all | solution.py:19
  117.9 11.0 %all-to-all-start.5 = ((bf16[32,2,8,256]{3,2,1,0:T(8,128)(2,1)}), bf16[32,2,8,256]{3,2,1,0:T(8,128)(2,1)S(1)}, u32[]{:S(2)}, u32[]{:S(2)}) async-start(bf16[32,2,8,256]{3,2,1,0:T(8,128)(2,1)} %maximum_bitcast_fusion.1), calls=%async_computation.5 | async-start | bytes 524288 | tf_op jit(solution)/shard_map/all_to_all | solution.py:19
  128.9 9.0 %all-to-all-done.5 = bf16[32,2,8,256]{3,2,1,0:T(8,128)(2,1)S(1)} async-done(((bf16[32,2,8,256]{3,2,1,0:T(8,128)(2,1)}), bf16[32,2,8,256]{3,2,1,0:T(8,128)(2,1)S(1)}, u32[]{:S(2)}, u32[]{:S(2)}) %all-to-all-start.5) | async-done | bytes 262176 | tf_op jit(solution)/shard_map/all_to_all | solution.py:19
  138.7 15.1 %all_to_all.77 = bf16[32,32,256]{2,1,0:T(8,128)(2,1)S(1)} all-to-all(bf16[32,32,256]{2,1,0:T(8,128)(2,1)S(1)} %broadcast_in_dim.25), channel_id=1, replica_groups=mesh['z'=16,'x'=4,'y'=4,'core'=2] {'x','y','core'}, dimensions={0} | all-to-all | bytes 1048576 | tf_op jit(solution)/shard_map/all_to_all | solution.py:19
  154.6 0.9 copy.124
  155.5 5.3 %all-to-all-start.7 = ((bf16[16,2,14,256]{3,1,2,0:T(2,128)(2,1)}), bf16[16,2,14,256]{3,1,2,0:T(2,128)(2,1)S(1)}, u32[]{:S(2)}, u32[]{:S(2)}) async-start(bf16[16,2,14,256]{3,1,2,0:T(2,128)(2,1)} %copy.124), calls=%async_computation.7 | async-start | bytes 458752 | tf_op jit(solution)/shard_map/all_to_all | solution.py:19
  161.9 12.9 %all-to-all-done.7 = bf16[16,2,14,256]{3,1,2,0:T(2,128)(2,1)S(1)} async-done(((bf16[16,2,14,256]{3,1,2,0:T(2,128)(2,1)}), bf16[16,2,14,256]{3,1,2,0:T(2,128)(2,1)S(1)}, u32[]{:S(2)}, u32[]{:S(2)}) %all-to-all-start.7) | async-done | bytes 229408 | tf_op jit(solution)/shard_map/all_to_all | solution.py:19
  179.3 20.9 %all_to_all.78 = bf16[16,16,256]{2,1,0:T(8,128)(2,1)S(1)} all-to-all(bf16[16,16,256]{2,1,0:T(8,128)(2,1)S(1)} %broadcast_in_dim.26), channel_id=1, replica_groups=mesh['z'=16,'x'=4,'y'=4,'core'=2] {'z'}, dimensions={0} | all-to-all | bytes 262144 | tf_op jit(solution)/shard_map/all_to_all | solution.py:19
  204.6 15.7 %all_to_all.79 = bf16[32,10,256]{2,1,0:T(8,128)(2,1)S(1)} all-to-all(bf16[32,10,256]{2,1,0:T(8,128)(2,1)S(1)} %pad_maximum_fusion.1), channel_id=1, replica_groups=mesh['z'=16,'x'=4,'y'=4,'core'=2] {'x','y','core'}, dimensions={0} | all-to-all | bytes 327680 | tf_op jit(solution)/shard_map/all_to_all | solution.py:19
  220.9 3.7 %all-to-all-start.10 = ((bf16[32,8,256]{2,1,0:T(8,128)(2,1)}), bf16[32,8,256]{2,1,0:T(8,128)(2,1)S(1)}, u32[]{:S(2)}, u32[]{:S(2)}) async-start(bf16[32,8,256]{2,1,0:T(8,128)(2,1)} %broadcast_in_dim.28), calls=%async_computation.10 | async-start | bytes 262144 | tf_op jit(solution)/shard_map/all_to_all | solution.py:19
  226.2 6.3 %all-to-all-done.10 = bf16[32,8,256]{2,1,0:T(8,128)(2,1)S(1)} async-done(((bf16[32,8,256]{2,1,0:T(8,128)(2,1)}), bf16[32,8,256]{2,1,0:T(8,128)(2,1)S(1)}, u32[]{:S(2)}, u32[]{:S(2)}) %all-to-all-start.10) | async-done | bytes 131104 | tf_op jit(solution)/shard_map/all_to_all | solution.py:19
  233.6 3.6 %all-to-all-start.11 = ((bf16[16,14,256]{2,1,0:T(8,128)(2,1)}), bf16[16,14,256]{2,1,0:T(8,128)(2,1)S(1)}, u32[]{:S(2)}, u32[]{:S(2)}) async-start(bf16[16,14,256]{2,1,0:T(8,128)(2,1)} %reshape.145), calls=%async_computation.11 | async-start | bytes 262144 | tf_op jit(solution)/shard_map/all_to_all | solution.py:19
  238.1 11.3 %all-to-all-done.11 = bf16[16,14,256]{2,1,0:T(8,128)(2,1)S(1)} async-done(((bf16[16,14,256]{2,1,0:T(8,128)(2,1)}), bf16[16,14,256]{2,1,0:T(8,128)(2,1)S(1)}, u32[]{:S(2)}, u32[]{:S(2)}) %all-to-all-start.11) | async-done | bytes 114720 | tf_op jit(solution)/shard_map/all_to_all | solution.py:19
  258.1 6.5 %all-to-all-start.12 = ((bf16[16,32,256]{2,1,0:T(8,128)(2,1)}), bf16[16,32,256]{2,1,0:T(8,128)(2,1)S(1)}, u32[]{:S(2)}, u32[]{:S(2)}) async-start(bf16[16,32,256]{2,1,0:T(8,128)(2,1)} %broadcast_in_dim.29), calls=%async_computation.12 | async-start | bytes 524288 | tf_op jit(solution)/shard_map/all_to_all | solution.py:19
  264.6 13.1 %all-to-all-done.12 = bf16[16,32,256]{2,1,0:T(8,128)(2,1)S(1)} async-done(((bf16[16,32,256]{2,1,0:T(8,128)(2,1)}), bf16[16,32,256]{2,1,0:T(8,128)(2,1)S(1)}, u32[]{:S(2)}, u32[]{:S(2)}) %all-to-all-start.12) | async-done | bytes 262176 | tf_op jit(solution)/shard_map/all_to_all | solution.py:19
  278.4 1.4 pad_maximum_fusion.11
  280.5 9.5 %all-to-all-start.14 = ((f32[32,2,128]{2,1,0:T(2,128)}), f32[32,2,128]{2,1,0:T(2,128)S(1)}, u32[]{:S(2)}, u32[]{:S(2)}) async-start(f32[32,2,128]{2,1,0:T(2,128)} %broadcast_in_dim_broadcast_in_dim_broadcast_in_dim.2), calls=%async_computation.14 | async-start | bytes 65536 | tf_op jit(solution)/shard_map/all_to_all | solution.py:19
  291.5 5.8 %all-to-all-done.14 = f32[32,2,128]{2,1,0:T(2,128)S(1)} async-done(((f32[32,2,128]{2,1,0:T(2,128)}), f32[32,2,128]{2,1,0:T(2,128)S(1)}, u32[]{:S(2)}, u32[]{:S(2)}) %all-to-all-start.14) | async-done | bytes 32800 | tf_op jit(solution)/shard_map/all_to_all | solution.py:19
  297.3 3.5 %all-to-all-start.13 = ((bf16[4,3,64,224]{3,2,1,0:T(8,128)(2,1)}), bf16[4,3,64,224]{3,2,1,0:T(8,128)(2,1)S(1)}, u32[]{:S(2)}, u32[]{:S(2)}) async-start(bf16[4,3,64,224]{3,2,1,0:T(8,128)(2,1)} %copy.130), calls=%async_computation.13 | async-start | bytes 786432 | tf_op jit(solution)/shard_map/all_to_all | solution.py:19
  302.7 5.9 %all-to-all-done.13 = bf16[4,3,64,224]{3,2,1,0:T(8,128)(2,1)S(1)} async-done(((bf16[4,3,64,224]{3,2,1,0:T(8,128)(2,1)}), bf16[4,3,64,224]{3,2,1,0:T(8,128)(2,1)S(1)}, u32[]{:S(2)}, u32[]{:S(2)}) %all-to-all-start.13) | async-done | bytes 344096 | tf_op jit(solution)/shard_map/all_to_all | solution.py:19
  308.9 0.9 squeeze.38
  309.9 0.9 squeeze.36
  311.0 0.9 squeeze.37
  (123 shorter events, 23.4 us)
Async XLA Ops:
  0.6 1.2 copy-start
  0.6 14.8 %copy-start.1 = (f32[64,896]{1,0:T(8,128)S(1)}, f32[64,896]{1,0:T(8,128)}, u32[]{:S(2)}) copy-start(f32[64,896]{1,0:T(8,128)} %param.15) | copy-start | bytes 688132
  0.7 15.0 %copy-start.2 = (f32[64,896]{1,0:T(8,128)S(1)}, f32[64,896]{1,0:T(8,128)}, u32[]{:S(2)}) copy-start(f32[64,896]{1,0:T(8,128)} %param.16) | copy-start | bytes 688132
  0.7 15.2 %copy-start.4 = (bf16[896,64]{0,1:T(8,128)(2,1)S(1)}, bf16[896,64]{0,1:T(8,128)(2,1)}, u32[]{:S(2)}) copy-start(bf16[896,64]{0,1:T(8,128)(2,1)} %param.14) | copy-start | bytes 344068
  3.1 14.9 %all-to-all-start = ((bf16[8,4,512]{2,1,0:T(4,128)(2,1)}), bf16[8,4,512]{2,1,0:T(4,128)(2,1)S(1)}, u32[]{:S(2)}, u32[]{:S(2)}) async-start(bf16[8,4,512]{2,1,0:T(4,128)(2,1)} %broadcast_in_dim.21), calls=%async_computation | async-start | bytes 65536 | tf_op jit(solution)/shard_map/all_to_all | solution.py:19
  13.2 2.8 copy-start.3
  32.4 28.6 %all-to-all-start.1 = ((bf16[64,4,256]{2,1,0:T(4,128)(2,1)}), bf16[64,4,256]{2,1,0:T(4,128)(2,1)S(1)}, u32[]{:S(2)}, u32[]{:S(2)}) async-start(bf16[64,4,256]{2,1,0:T(4,128)(2,1)} %bitcast.3), calls=%async_computation.1 | async-start | bytes 262144 | tf_op jit(solution)/shard_map/all_to_all | solution.py:19
  96.8 19.7 %all-to-all-start.4 = ((bf16[16,28,256]{2,1,0:T(8,128)(2,1)}), bf16[16,28,256]{2,1,0:T(8,128)(2,1)S(1)}, u32[]{:S(2)}, u32[]{:S(2)}) async-start(bf16[16,28,256]{2,1,0:T(8,128)(2,1)} %broadcast_in_dim.24), calls=%async_computation.4 | async-start | bytes 524288 | tf_op jit(solution)/shard_map/all_to_all | solution.py:19
  117.9 20.0 %all-to-all-start.5 = ((bf16[32,2,8,256]{3,2,1,0:T(8,128)(2,1)}), bf16[32,2,8,256]{3,2,1,0:T(8,128)(2,1)S(1)}, u32[]{:S(2)}, u32[]{:S(2)}) async-start(bf16[32,2,8,256]{3,2,1,0:T(8,128)(2,1)} %maximum_bitcast_fusion.1), calls=%async_computation.5 | async-start | bytes 524288 | tf_op jit(solution)/shard_map/all_to_all | solution.py:19
  155.5 19.2 %all-to-all-start.7 = ((bf16[16,2,14,256]{3,1,2,0:T(2,128)(2,1)}), bf16[16,2,14,256]{3,1,2,0:T(2,128)(2,1)S(1)}, u32[]{:S(2)}, u32[]{:S(2)}) async-start(bf16[16,2,14,256]{3,1,2,0:T(2,128)(2,1)} %copy.124), calls=%async_computation.7 | async-start | bytes 458752 | tf_op jit(solution)/shard_map/all_to_all | solution.py:19
  220.9 11.5 %all-to-all-start.10 = ((bf16[32,8,256]{2,1,0:T(8,128)(2,1)}), bf16[32,8,256]{2,1,0:T(8,128)(2,1)S(1)}, u32[]{:S(2)}, u32[]{:S(2)}) async-start(bf16[32,8,256]{2,1,0:T(8,128)(2,1)} %broadcast_in_dim.28), calls=%async_computation.10 | async-start | bytes 262144 | tf_op jit(solution)/shard_map/all_to_all | solution.py:19
  233.6 15.8 %all-to-all-start.11 = ((bf16[16,14,256]{2,1,0:T(8,128)(2,1)}), bf16[16,14,256]{2,1,0:T(8,128)(2,1)S(1)}, u32[]{:S(2)}, u32[]{:S(2)}) async-start(bf16[16,14,256]{2,1,0:T(8,128)(2,1)} %reshape.145), calls=%async_computation.11 | async-start | bytes 262144 | tf_op jit(solution)/shard_map/all_to_all | solution.py:19
  258.1 19.7 %all-to-all-start.12 = ((bf16[16,32,256]{2,1,0:T(8,128)(2,1)}), bf16[16,32,256]{2,1,0:T(8,128)(2,1)S(1)}, u32[]{:S(2)}, u32[]{:S(2)}) async-start(bf16[16,32,256]{2,1,0:T(8,128)(2,1)} %broadcast_in_dim.29), calls=%async_computation.12 | async-start | bytes 524288 | tf_op jit(solution)/shard_map/all_to_all | solution.py:19
  280.5 16.9 %all-to-all-start.14 = ((f32[32,2,128]{2,1,0:T(2,128)}), f32[32,2,128]{2,1,0:T(2,128)S(1)}, u32[]{:S(2)}, u32[]{:S(2)}) async-start(f32[32,2,128]{2,1,0:T(2,128)} %broadcast_in_dim_broadcast_in_dim_broadcast_in_dim.2), calls=%async_computation.14 | async-start | bytes 65536 | tf_op jit(solution)/shard_map/all_to_all | solution.py:19
  297.3 11.2 %all-to-all-start.13 = ((bf16[4,3,64,224]{3,2,1,0:T(8,128)(2,1)}), bf16[4,3,64,224]{3,2,1,0:T(8,128)(2,1)S(1)}, u32[]{:S(2)}, u32[]{:S(2)}) async-start(bf16[4,3,64,224]{3,2,1,0:T(8,128)(2,1)} %copy.130), calls=%async_computation.13 | async-start | bytes 786432 | tf_op jit(solution)/shard_map/all_to_all | solution.py:19

commit v2 on v1

v2 whole, which is shorter than its diff:
```python
import jax
import jax.numpy as jnp
from jax import lax
from jax.sharding import Mesh
from jax.sharding import PartitionSpec as P

AXES = ("zh", "zl", "x", "y", "core")
SIZES = (8, 2, 4, 4, 2)
NEAR = ("zl", "x")
REST = ("zl", "x", "y", "core")
BF = jnp.bfloat16
F32 = jnp.float32


def dot(a, b, ca, cb):
    return lax.dot_general(a, b, (((ca,), (cb,)), ((), ())), preferred_element_type=F32)


def exchange(v, axes):
    return lax.all_to_all(v, axes, split_axis=0, concat_axis=0, tiled=True)


def gather(v, axes, n):
    return exchange(jnp.broadcast_to(v[None], (n,) + v.shape), axes)


def two_terms(v):
    high = lax.reduce_precision(v, 8, 7)
    return high.astype(BF), (v - high).astype(BF)


def silu_parts(values):
    s = jax.nn.sigmoid(values)
    activated = values * s
    slope_one = s * (1.0 + values * (1.0 - s))
    slope_two = s * (1.0 - s) * (2.0 + values * (1.0 - 2.0 * s))
    return activated, slope_one, slope_two


def total(v):
    ones = jnp.ones((v.shape[1], 128), F32)
    both = lax.dot_general(
        v, ones, (((1,), (0,)), ((), ())), precision=lax.Precision.HIGHEST, preferred_element_type=F32
    )
    return both[:, :1]


def make_body(nz, nl, nx, ny, nc):
    nt = ny * nc
    nx = nl * nx
    nr = nx * nt

    def body(pool, picks, targets, gate_w, up_w, down_w, probe_g, probe_u, probe_d):
        tok_dev = picks.shape[0]
        tokens = targets.shape[0]
        d_dev, ff_dev = gate_w.shape
        ff = ff_dev // nx
        dz = d_dev * nx
        sub = ff // nz
        rows = dz // nr
        count = 3.0 * (dz * nz) * (ff_dev * nt)

        chosen = pool.at[picks].get(mode="promise_in_bounds")
        wide = gather(chosen, ("y", "core"), nt)
        wide = wide.transpose(1, 0, 2).reshape(tok_dev, nz, dz).transpose(1, 0, 2)
        wide = jnp.broadcast_to(wide[:, None], (nz, nx, tok_dev, dz))
        inputs = exchange(wide.reshape(nz * nx, tok_dev, dz), ("zh", *NEAR)).reshape(tokens, dz)

        mats = jnp.stack(
            [
                gate_w,
                up_w,
                probe_g.astype(BF),
                probe_u.astype(BF),
                down_w.T,
                probe_d.T.astype(BF),
            ]
        )
        mats = mats.reshape(6, d_dev, nx, ff).transpose(2, 0, 1, 3)
        mats = exchange(mats, NEAR).transpose(1, 0, 2, 3).reshape(6, dz, ff)
        down, pdown = mats[4], mats[5]

        first = lax.dot_general(
            mats[:4], inputs, (((1,), (1,)), ((), ())), preferred_element_type=F32
        )
        own = lax.axis_index(REST)
        gram_rows = tokens // nr
        mine = lax.dynamic_slice_in_dim(inputs, own * gram_rows, gram_rows, 0)
        gram = jnp.concatenate(two_terms(dot(mine, inputs, 1, 1)))
        packed = first.astype(BF).reshape(4, nz, sub, tokens).transpose(1, 0, 2, 3)
        packed = packed.reshape(nz, 4 * sub, tokens)
        packed = jnp.concatenate(
            [packed, jnp.broadcast_to(gram[None], (nz,) + gram.shape)], axis=1
        )
        got = jnp.sum(exchange(packed, "zh").astype(F32), axis=0)
        gate_val, upper, tan_gate, tan_upper = (
            got[i * sub : (i + 1) * sub] for i in range(4)
        )
        gram = got[4 * sub : 4 * sub + gram_rows] + got[4 * sub + gram_rows :]
        activated, slope_one, slope_two = silu_parts(gate_val)
        hidden = (activated * upper).astype(BF)
        tan_act = slope_one * tan_gate
        tan_hidden = (tan_act * upper + activated * tan_upper).astype(BF)
        both = gather(jnp.concatenate([hidden, tan_hidden]), "zh", nz)
        hidden = both[:, :sub].reshape(ff, tokens)
        tan_hidden = both[:, sub:].reshape(ff, tokens)

        out = dot(down, hidden, 1, 0)
        tan_out = dot(down, tan_hidden, 1, 0) + dot(pdown, hidden, 1, 0)
        packed = jnp.stack([out.astype(BF), tan_out.astype(BF)])
        packed = packed.reshape(2, nr, rows, tokens).transpose(1, 0, 2, 3)
        got = jnp.sum(exchange(packed, REST).astype(F32), axis=0)
        wanted = lax.dynamic_slice_in_dim(
            targets.T, lax.axis_index(("y", "core")) * rows, rows, 0
        )
        resid = ((got[0] - wanted.astype(F32)) / tokens).astype(BF)
        tan_resid = (got[1] / tokens).astype(BF)
        packed = jnp.concatenate([resid, tan_resid, *two_terms(gram)])
        both = gather(packed, REST, nr)
        resid = both[:, :rows].reshape(dz, tokens)
        tan_resid = both[:, rows : 2 * rows].reshape(dz, tokens)
        gram_hi = both[:, 2 * rows : 2 * rows + gram_rows].reshape(tokens, tokens)
        gram_lo = both[:, 2 * rows + gram_rows :].reshape(tokens, tokens)

        def by_gram(v):
            return dot(v, gram_hi, 1, 0) + dot(v, gram_lo, 1, 0)

        back = dot(down, resid, 0, 0)
        tan_back = dot(down, tan_resid, 0, 0) + dot(pdown, resid, 0, 0)
        packed = jnp.stack([back.astype(BF), tan_back.astype(BF)])
        packed = packed.reshape(2, nz, sub, tokens).transpose(1, 0, 2, 3)
        got = jnp.sum(exchange(packed, "zh").astype(F32), axis=0)
        back, tan_back = got[0], got[1]
        hv_down = dot(resid, tan_hidden, 1, 1) + dot(tan_resid, hidden, 1, 1)

        def deltas(tan_back, tan_gate, tan_upper):
            up = tan_back * activated + back * (slope_one * tan_gate)
            gate = (tan_back * upper + back * tan_upper) * slope_one + (
                back * upper
            ) * slope_two * tan_gate
            return jnp.concatenate([gate.astype(BF), up.astype(BF)])

        delta = deltas(tan_back, tan_gate, tan_upper)

        def lanes(v):
            v = jnp.sum(v, axis=0, keepdims=True)
            return jnp.pad(v, ((0, 0), (0, tokens - v.shape[1])))

        def terms(*values):
            return jnp.concatenate([t for v in values for t in two_terms(v)])

        tangents = by_gram(delta)
        square = lanes(delta.astype(F32) * tangents) + lanes(hv_down * hv_down)
        tan_gate, tan_upper = tangents[:sub], tangents[sub:]
        tan_hidden = ((slope_one * tan_gate) * upper + activated * tan_upper).astype(BF)
        both = gather(jnp.concatenate([tan_hidden, terms(square)]), "zh", nz)
        tan_hidden = both[:, :sub].reshape(ff, tokens)
        square = jnp.sum(both[:, sub:].astype(F32), axis=(0, 1))[None]

        hv_down_b = hv_down.astype(BF)
        tan_out = dot(down, tan_hidden, 1, 0) + dot(hv_down_b, hidden, 1, 0)
        packed = tan_out.astype(BF).reshape(nr, rows, tokens)
        scal = jnp.broadcast_to(terms(square)[None], (nr, 2, tokens))
        got = exchange(jnp.concatenate([packed, scal], axis=1), REST)
        square = jnp.sum(got[:, rows:].astype(F32), axis=(0, 1))[None]
        got = jnp.sum(got[:, :rows].astype(F32), axis=0)
        scale = 1.0 / jnp.sqrt(total(square) / count + 1e-6)
        tan_resid = (got / tokens).astype(BF)
        tan_resid = gather(tan_resid, REST, nr).reshape(dz, tokens)

        tan_back = dot(down, tan_resid, 0, 0) + dot(hv_down_b, resid, 0, 0)
        packed = tan_back.astype(BF).reshape(nz, sub, tokens)
        tan_back = jnp.sum(exchange(packed, "zh").astype(F32), axis=0)
        hv_down2 = (dot(resid, tan_hidden, 1, 1) + dot(tan_resid, hidden, 1, 1)) * scale

        tangents = tangents * scale
        delta = deltas(tan_back * scale, tangents[:sub], tangents[sub:])
        wide = delta.astype(F32)
        inner = lanes(tangents * wide) + lanes((hv_down * scale) * hv_down2)
        square = lanes(by_gram(delta) * wide) + lanes(hv_down2 * hv_down2)
        both = gather(jnp.concatenate([delta, terms(inner, square)]), "zh", nz)
        delta_gate = both[:, :sub].reshape(ff, tokens)
        delta_up = both[:, sub : 2 * sub].reshape(ff, tokens)
        sums = both[:, 2 * sub :].reshape(nz, 2, 2, tokens).astype(F32)
        sums = jnp.sum(gather(jnp.sum(sums, axis=(0, 2)), REST, nr), axis=0)
        scale = 1.0 / jnp.sqrt(total(sums[1:]) / count + 1e-6)

        hv = jnp.stack(
            [
                dot(inputs, delta_gate, 0, 1).astype(BF),
                dot(inputs, delta_up, 0, 1).astype(BF),
                hv_down2.astype(BF),
            ]
        )
        hv = hv.reshape(3, nx, d_dev, ff).transpose(1, 0, 2, 3)
        hv = exchange(hv, NEAR).transpose(1, 2, 0, 3).reshape(3, d_dev, ff_dev)
        hv = hv.astype(F32) * scale
        return hv[0], hv[1], hv[2].T, jnp.sum(sums[0]) / count

    return body


def build(devices, sizes):
    wide = Mesh(devices.reshape(sizes), AXES)
    dp, tensor = ("zh", *NEAR), ("y", "core")
    placed = (
        P(dp, tensor),
        P(dp),
        P(None, dp),
        P(dp, tensor),
        P(dp, tensor),
        P(tensor, dp),
        P(dp, tensor),
        P(dp, tensor),
        P(tensor, dp),
    )
    return jax.shard_map(
        make_body(*sizes),
        mesh=wide,
        in_specs=placed,
        out_specs=(P(dp, tensor), P(dp, tensor), P(tensor, dp), P()),
        check_vma=False,
    )


def solution(mesh):
    return build(mesh.devices, SIZES)
```

time: 314 us -> 289 us (0.920)
  waiting for transfers between devices: 93.1 us -> 106 us
  blocking collectives: 99 us -> 86.2 us
  between operations: 16.9 us -> 4.52 us
  starting transfers between devices: 73.6 us -> 63.5 us
    all_to_all x10, waiting for transfers between devices: 93.1 us -> 106 us  [exchange(): return lax.all_to_all(v, axes, split_axis=0, concat_axis=0, tiled=True)]
    all_to_all x5, blocking collectives: 99 us -> 86.2 us  [exchange(): return lax.all_to_all(v, axes, split_axis=0, concat_axis=0, tiled=True)]
    all_to_all x10, starting transfers between devices: 73.6 us -> 63.5 us  [exchange(): return lax.all_to_all(v, axes, split_axis=0, concat_axis=0, tiled=True)]
where the time goes in v2:
time: 289 us; the launch traced here: 288 us
  waiting for transfers between devices  106 us (37%)
  blocking collectives  86.2 us (30%)
  starting transfers between devices  63.5 us (22%)
  local copies, waits for them, and re-layouts  15.9 us (6%)
  matrix products  7.53 us (3%)
  between operations  4.52 us (2%)
  other arithmetic  4.1 us (1%)
    all_to_all x10, waiting for transfers between devices, exchange(): return lax.all_to_all(v, axes, split_axis=0, concat_axis=0, tiled=True)  106 us
    all_to_all x5, blocking collectives, exchange(): return lax.all_to_all(v, axes, split_axis=0, concat_axis=0, tiled=True)  86.2 us
    all_to_all x10, starting transfers between devices, exchange(): return lax.all_to_all(v, axes, split_axis=0, concat_axis=0, tiled=True)  63.5 us
    dot_general x21, matrix products, dot(): lax.dot_general(a, b, (((ca,), (cb,)), ((), ())), preferred_element_type=...  5.86 us
  transfers between devices with their start and end apart: 10, of which 10 were waited for; matrix products, arithmetic and copies ran while one was open for 3% of the time, Pallas kernels for 0%

profile of v2, /device:TPU:1, one launch (start us, length us, event | category | flops | bytes accessed | tf_op | source)
XLA Modules:
  0.0 287.7 jit_solution(16304492111048146355)
XLA Ops:
  2.5 14.0 %all_to_all.75 = bf16[8,4,512]{2,1,0:T(4,128)(2,1)S(1)} all-to-all(bf16[8,4,512]{2,1,0:T(4,128)(2,1)S(1)} %broadcast_in_dim.35), channel_id=1, replica_groups=mesh['zh'=8,'zl'=2,'x'=4,'y'=4,'core'=2] {'y','core'}, dimensions={0} | all-to-all | bytes 65536 | tf_op jit(solution)/shard_map/all_to_all | solution.py:20
  16.4 0.8 broadcast_in_dim.36
  17.2 14.9 %all-to-all-start.1 = ((bf16[64,4,512]{2,1,0:T(4,128)(2,1)}), bf16[64,4,512]{2,1,0:T(4,128)(2,1)S(1)}, u32[]{:S(2)}, u32[]{:S(2)}) async-start(bf16[64,4,512]{2,1,0:T(4,128)(2,1)} %bitcast), calls=%async_computation.1 | async-start | bytes 524288 | tf_op jit(solution)/shard_map/all_to_all | solution.py:20
  35.5 1.1 copy.116
  36.6 14.8 %all-to-all-done.1 = bf16[64,4,512]{2,1,0:T(4,128)(2,1)S(1)} async-done(((bf16[64,4,512]{2,1,0:T(4,128)(2,1)}), bf16[64,4,512]{2,1,0:T(4,128)(2,1)S(1)}, u32[]{:S(2)}, u32[]{:S(2)}) %all-to-all-start.1) | async-done | bytes 262176 | tf_op jit(solution)/shard_map/all_to_all | solution.py:20
  51.4 4.1 %all-to-all-start.2 = ((bf16[8,6,64,112]{3,2,1,0:T(8,128)(2,1)}), bf16[8,6,64,112]{3,2,1,0:T(8,128)(2,1)S(1)}, u32[]{:S(2)}, u32[]{:S(2)}) async-start(bf16[8,6,64,112]{3,2,1,0:T(8,128)(2,1)} %copy.116), calls=%async_computation.2 | async-start | bytes 1572864 | tf_op jit(solution)/shard_map/all_to_all | solution.py:20
  55.8 8.0 %all-to-all-done.2 = bf16[8,6,64,112]{3,2,1,0:T(8,128)(2,1)S(1)} async-done(((bf16[8,6,64,112]{3,2,1,0:T(8,128)(2,1)}), bf16[8,6,64,112]{3,2,1,0:T(8,128)(2,1)S(1)}, u32[]{:S(2)}, u32[]{:S(2)}) %all-to-all-start.2) | async-done | bytes 688160 | tf_op jit(solution)/shard_map/all_to_all | solution.py:20
  64.5 20.8 %all_to_all.76 = bf16[8,64,256]{2,1,0:T(8,128)(2,1)S(1)} all-to-all(bf16[8,64,256]{2,1,0:T(8,128)(2,1)S(1)} %copy.121), channel_id=1, replica_groups=mesh['zh'=8,'zl'=2,'x'=4,'y'=4,'core'=2] {'zh'}, dimensions={0} | all-to-all | bytes 524288 | tf_op jit(solution)/shard_map/all_to_all | solution.py:20
  86.0 3.4 %all-to-all-start.4 = ((bf16[8,28,256]{2,1,0:T(8,128)(2,1)}), bf16[8,28,256]{2,1,0:T(8,128)(2,1)S(1)}, u32[]{:S(2)}, u32[]{:S(2)}) async-start(bf16[8,28,256]{2,1,0:T(8,128)(2,1)} %broadcast_in_dim.38), calls=%async_computation.4 | async-start | bytes 262144 | tf_op jit(solution)/shard_map/all_to_all | solution.py:20
  89.5 13.0 %all-to-all-done.4 = bf16[8,28,256]{2,1,0:T(8,128)(2,1)S(1)} async-done(((bf16[8,28,256]{2,1,0:T(8,128)(2,1)}), bf16[8,28,256]{2,1,0:T(8,128)(2,1)S(1)}, u32[]{:S(2)}, u32[]{:S(2)}) %all-to-all-start.4) | async-done | bytes 114720 | tf_op jit(solution)/shard_map/all_to_all | solution.py:20
  103.2 0.8 maximum_bitcast_fusion
  104.0 15.3 %all-to-all-start.5 = ((bf16[64,2,8,256]{3,2,1,0:T(8,128)(2,1)}), bf16[64,2,8,256]{3,2,1,0:T(8,128)(2,1)S(1)}, u32[]{:S(2)}, u32[]{:S(2)}) async-start(bf16[64,2,8,256]{3,2,1,0:T(8,128)(2,1)} %maximum_bitcast_fusion), calls=%async_computation.5 | async-start | bytes 1048576 | tf_op jit(solution)/shard_map/all_to_all | solution.py:20
  119.3 12.2 %all-to-all-done.5 = bf16[64,2,8,256]{3,2,1,0:T(8,128)(2,1)S(1)} async-done(((bf16[64,2,8,256]{3,2,1,0:T(8,128)(2,1)}), bf16[64,2,8,256]{3,2,1,0:T(8,128)(2,1)S(1)}, u32[]{:S(2)}, u32[]{:S(2)}) %all-to-all-start.5) | async-done | bytes 524320 | tf_op jit(solution)/shard_map/all_to_all | solution.py:20
  132.3 19.1 %all_to_all.77 = bf16[64,24,256]{2,1,0:T(8,128)(2,1)S(1)} all-to-all(bf16[64,24,256]{2,1,0:T(8,128)(2,1)S(1)} %broadcast_in_dim.39), channel_id=1, replica_groups=mesh['zh'=8,'zl'=2,'x'=4,'y'=4,'core'=2] {'zl','x','y','core'}, dimensions={0} | all-to-all | bytes 1572864 | tf_op jit(solution)/shard_map/all_to_all | solution.py:20
  153.0 3.4 %all-to-all-start.7 = ((bf16[8,2,14,256]{3,1,2,0:T(2,128)(2,1)}), bf16[8,2,14,256]{3,1,2,0:T(2,128)(2,1)S(1)}, u32[]{:S(2)}, u32[]{:S(2)}) async-start(bf16[8,2,14,256]{3,1,2,0:T(2,128)(2,1)} %copy.124), calls=%async_computation.7 | async-start | bytes 229376 | tf_op jit(solution)/shard_map/all_to_all | solution.py:20
  157.1 14.9 %all-to-all-done.7 = bf16[8,2,14,256]{3,1,2,0:T(2,128)(2,1)S(1)} async-done(((bf16[8,2,14,256]{3,1,2,0:T(2,128)(2,1)}), bf16[8,2,14,256]{3,1,2,0:T(2,128)(2,1)S(1)}, u32[]{:S(2)}, u32[]{:S(2)}) %all-to-all-start.7) | async-done | bytes 114720 | tf_op jit(solution)/shard_map/all_to_all | solution.py:20
  172.6 14.6 %all_to_all.78 = bf16[8,16,256]{2,1,0:T(8,128)(2,1)S(1)} all-to-all(bf16[8,16,256]{2,1,0:T(8,128)(2,1)S(1)} %broadcast_in_dim.42), channel_id=1, replica_groups=mesh['zh'=8,'zl'=2,'x'=4,'y'=4,'core'=2] {'zh'}, dimensions={0} | all-to-all | bytes 131072 | tf_op jit(solution)/shard_map/all_to_all | solution.py:20
  188.3 17.8 %all_to_all.79 = bf16[64,10,256]{2,1,0:T(8,128)(2,1)S(1)} all-to-all(bf16[64,10,256]{2,1,0:T(8,128)(2,1)S(1)} %pad_maximum_fusion), channel_id=1, replica_groups=mesh['zh'=8,'zl'=2,'x'=4,'y'=4,'core'=2] {'zl','x','y','core'}, dimensions={0} | all-to-all | bytes 655360 | tf_op jit(solution)/shard_map/all_to_all | solution.py:20
  206.8 4.6 %all-to-all-start.10 = ((bf16[64,8,256]{2,1,0:T(8,128)(2,1)}), bf16[64,8,256]{2,1,0:T(8,128)(2,1)S(1)}, u32[]{:S(2)}, u32[]{:S(2)}) async-start(bf16[64,8,256]{2,1,0:T(8,128)(2,1)} %broadcast_in_dim.44), calls=%async_computation.10 | async-start | bytes 524288 | tf_op jit(solution)/shard_map/all_to_all | solution.py:20
  211.5 1.7 fusion.14
  214.7 6.5 %all-to-all-done.10 = bf16[64,8,256]{2,1,0:T(8,128)(2,1)S(1)} async-done(((bf16[64,8,256]{2,1,0:T(8,128)(2,1)}), bf16[64,8,256]{2,1,0:T(8,128)(2,1)S(1)}, u32[]{:S(2)}, u32[]{:S(2)}) %all-to-all-start.10) | async-done | bytes 262176 | tf_op jit(solution)/shard_map/all_to_all | solution.py:20
  222.3 3.4 %all-to-all-start.11 = ((bf16[8,14,256]{2,1,0:T(8,128)(2,1)}), bf16[8,14,256]{2,1,0:T(8,128)(2,1)S(1)}, u32[]{:S(2)}, u32[]{:S(2)}) async-start(bf16[8,14,256]{2,1,0:T(8,128)(2,1)} %reshape.165), calls=%async_computation.11 | async-start | bytes 131072 | tf_op jit(solution)/shard_map/all_to_all | solution.py:20
  226.0 11.5 %all-to-all-done.11 = bf16[8,14,256]{2,1,0:T(8,128)(2,1)S(1)} async-done(((bf16[8,14,256]{2,1,0:T(8,128)(2,1)}), bf16[8,14,256]{2,1,0:T(8,128)(2,1)S(1)}, u32[]{:S(2)}, u32[]{:S(2)}) %all-to-all-start.11) | async-done | bytes 57376 | tf_op jit(solution)/shard_map/all_to_all | solution.py:20
  238.8 3.4 %all-to-all-start.12 = ((bf16[8,32,256]{2,1,0:T(8,128)(2,1)}), bf16[8,32,256]{2,1,0:T(8,128)(2,1)S(1)}, u32[]{:S(2)}, u32[]{:S(2)}) async-start(bf16[8,32,256]{2,1,0:T(8,128)(2,1)} %broadcast_in_dim.49), calls=%async_computation.12 | async-start | bytes 262144 | tf_op jit(solution)/shard_map/all_to_all | solution.py:20
  242.3 13.3 %all-to-all-done.12 = bf16[8,32,256]{2,1,0:T(8,128)(2,1)S(1)} async-done(((bf16[8,32,256]{2,1,0:T(8,128)(2,1)}), bf16[8,32,256]{2,1,0:T(8,128)(2,1)S(1)}, u32[]{:S(2)}, u32[]{:S(2)}) %all-to-all-start.12) | async-done | bytes 131104 | tf_op jit(solution)/shard_map/all_to_all | solution.py:20
  256.4 7.6 %all-to-all-start.14 = ((f32[64,2,256]{2,1,0:T(2,128)}), f32[64,2,256]{2,1,0:T(2,128)S(1)}, u32[]{:S(2)}, u32[]{:S(2)}) async-start(f32[64,2,256]{2,1,0:T(2,128)} %broadcast_in_dim.100), calls=%async_computation.14 | async-start | bytes 262144 | tf_op jit(solution)/shard_map/all_to_all | solution.py:20
  265.6 7.1 %all-to-all-done.14 = f32[64,2,256]{2,1,0:T(2,128)S(1)} async-done(((f32[64,2,256]{2,1,0:T(2,128)}), f32[64,2,256]{2,1,0:T(2,128)S(1)}, u32[]{:S(2)}, u32[]{:S(2)}) %all-to-all-start.14) | async-done | bytes 131104 | tf_op jit(solution)/shard_map/all_to_all | solution.py:20
  272.7 3.5 %all-to-all-start.13 = ((bf16[8,3,64,112]{3,2,1,0:T(8,128)(2,1)}), bf16[8,3,64,112]{3,2,1,0:T(8,128)(2,1)S(1)}, u32[]{:S(2)}, u32[]{:S(2)}) async-start(bf16[8,3,64,112]{3,2,1,0:T(8,128)(2,1)} %copy.130), calls=%async_computation.13 | async-start | bytes 786432 | tf_op jit(solution)/shard_map/all_to_all | solution.py:20
  278.8 4.6 %all-to-all-done.13 = bf16[8,3,64,112]{3,2,1,0:T(8,128)(2,1)S(1)} async-done(((bf16[8,3,64,112]{3,2,1,0:T(8,128)(2,1)}), bf16[8,3,64,112]{3,2,1,0:T(8,128)(2,1)S(1)}, u32[]{:S(2)}, u32[]{:S(2)}) %all-to-all-start.13) | async-done | bytes 344096 | tf_op jit(solution)/shard_map/all_to_all | solution.py:20
  283.8 0.8 squeeze.33
  284.8 0.8 squeeze.31
  285.7 0.8 squeeze.32
  (139 shorter events, 20.7 us)
Async XLA Ops:
  0.6 1.2 copy-start
  17.2 15.0 %copy-start.8 = (bf16[64,896]{1,0:T(8,128)(2,1)S(1)}, bf16[64,896]{1,0:T(8,128)(2,1)}, u32[]{:S(2)}) copy-start(bf16[64,896]{1,0:T(8,128)(2,1)} %param.12) | copy-start | bytes 344068
  17.2 15.2 %copy-start.9 = (bf16[64,896]{1,0:T(8,128)(2,1)S(1)}, bf16[64,896]{1,0:T(8,128)(2,1)}, u32[]{:S(2)}) copy-start(bf16[64,896]{1,0:T(8,128)(2,1)} %param.13) | copy-start | bytes 344068
  17.2 34.2 %all-to-all-start.1 = ((bf16[64,4,512]{2,1,0:T(4,128)(2,1)}), bf16[64,4,512]{2,1,0:T(4,128)(2,1)S(1)}, u32[]{:S(2)}, u32[]{:S(2)}) async-start(bf16[64,4,512]{2,1,0:T(4,128)(2,1)} %bitcast), calls=%async_computation.1 | async-start | bytes 524288 | tf_op jit(solution)/shard_map/all_to_all | solution.py:20
  32.2 0.9 copy-start.5
  33.1 0.9 copy-start.6
  34.0 0.9 copy-start.10
  34.1 1.1 copy-start.7
  51.4 12.5 %all-to-all-start.2 = ((bf16[8,6,64,112]{3,2,1,0:T(8,128)(2,1)}), bf16[8,6,64,112]{3,2,1,0:T(8,128)(2,1)S(1)}, u32[]{:S(2)}, u32[]{:S(2)}) async-start(bf16[8,6,64,112]{3,2,1,0:T(8,128)(2,1)} %copy.116), calls=%async_computation.2 | async-start | bytes 1572864 | tf_op jit(solution)/shard_map/all_to_all | solution.py:20
  86.0 16.4 %all-to-all-start.4 = ((bf16[8,28,256]{2,1,0:T(8,128)(2,1)}), bf16[8,28,256]{2,1,0:T(8,128)(2,1)S(1)}, u32[]{:S(2)}, u32[]{:S(2)}) async-start(bf16[8,28,256]{2,1,0:T(8,128)(2,1)} %broadcast_in_dim.38), calls=%async_computation.4 | async-start | bytes 262144 | tf_op jit(solution)/shard_map/all_to_all | solution.py:20
  104.0 27.4 %all-to-all-start.5 = ((bf16[64,2,8,256]{3,2,1,0:T(8,128)(2,1)}), bf16[64,2,8,256]{3,2,1,0:T(8,128)(2,1)S(1)}, u32[]{:S(2)}, u32[]{:S(2)}) async-start(bf16[64,2,8,256]{3,2,1,0:T(8,128)(2,1)} %maximum_bitcast_fusion), calls=%async_computation.5 | async-start | bytes 1048576 | tf_op jit(solution)/shard_map/all_to_all | solution.py:20
  153.0 19.0 %all-to-all-start.7 = ((bf16[8,2,14,256]{3,1,2,0:T(2,128)(2,1)}), bf16[8,2,14,256]{3,1,2,0:T(2,128)(2,1)S(1)}, u32[]{:S(2)}, u32[]{:S(2)}) async-start(bf16[8,2,14,256]{3,1,2,0:T(2,128)(2,1)} %copy.124), calls=%async_computation.7 | async-start | bytes 229376 | tf_op jit(solution)/shard_map/all_to_all | solution.py:20
  156.5 15.7 %copy-start.1 = (bf16[256,256]{1,0:T(8,128)(2,1)}, bf16[256,256]{1,0:T(8,128)(2,1)S(1)}, u32[]{:S(2)}) copy-start(bf16[256,256]{1,0:T(8,128)(2,1)S(1)} %reshape.160) | copy-start | bytes 393220
  187.2 0.6 copy-start.4
  206.8 14.4 %all-to-all-start.10 = ((bf16[64,8,256]{2,1,0:T(8,128)(2,1)}), bf16[64,8,256]{2,1,0:T(8,128)(2,1)S(1)}, u32[]{:S(2)}, u32[]{:S(2)}) async-start(bf16[64,8,256]{2,1,0:T(8,128)(2,1)} %broadcast_in_dim.44), calls=%async_computation.10 | async-start | bytes 524288 | tf_op jit(solution)/shard_map/all_to_all | solution.py:20
  221.6 4.0 %copy-start.3 = (f32[512,112]{0,1:T(8,128)S(1)}, f32[512,112]{0,1:T(8,128)}, u32[]{:S(2)}) copy-start(f32[512,112]{0,1:T(8,128)} %fusion.14) | copy-start | bytes 688132
  222.3 15.2 %all-to-all-start.11 = ((bf16[8,14,256]{2,1,0:T(8,128)(2,1)}), bf16[8,14,256]{2,1,0:T(8,128)(2,1)S(1)}, u32[]{:S(2)}, u32[]{:S(2)}) async-start(bf16[8,14,256]{2,1,0:T(8,128)(2,1)} %reshape.165), calls=%async_computation.11 | async-start | bytes 131072 | tf_op jit(solution)/shard_map/all_to_all | solution.py:20
  226.0 11.6 %copy-start.2 = (bf16[256,256]{1,0:T(8,128)(2,1)S(1)}, bf16[256,256]{1,0:T(8,128)(2,1)}, u32[]{:S(2)}) copy-start(bf16[256,256]{1,0:T(8,128)(2,1)} %copy-done.1) | copy-start | bytes 393220
  238.8 16.8 %all-to-all-start.12 = ((bf16[8,32,256]{2,1,0:T(8,128)(2,1)}), bf16[8,32,256]{2,1,0:T(8,128)(2,1)S(1)}, u32[]{:S(2)}, u32[]{:S(2)}) async-start(bf16[8,32,256]{2,1,0:T(8,128)(2,1)} %broadcast_in_dim.49), calls=%async_computation.12 | async-start | bytes 262144 | tf_op jit(solution)/shard_map/all_to_all | solution.py:20
  256.4 16.2 %all-to-all-start.14 = ((f32[64,2,256]{2,1,0:T(2,128)}), f32[64,2,256]{2,1,0:T(2,128)S(1)}, u32[]{:S(2)}, u32[]{:S(2)}) async-start(f32[64,2,256]{2,1,0:T(2,128)} %broadcast_in_dim.100), calls=%async_computation.14 | async-start | bytes 262144 | tf_op jit(solution)/shard_map/all_to_all | solution.py:20
  272.7 10.8 %all-to-all-start.13 = ((bf16[8,3,64,112]{3,2,1,0:T(8,128)(2,1)}), bf16[8,3,64,112]{3,2,1,0:T(8,128)(2,1)S(1)}, u32[]{:S(2)}, u32[]{:S(2)}) async-start(bf16[8,3,64,112]{3,2,1,0:T(8,128)(2,1)} %copy.130), calls=%async_computation.13 | async-start | bytes 786432 | tf_op jit(solution)/shard_map/all_to_all | solution.py:20

commit v3 on v2

--- a/solution.py
+++ b/solution.py
@@ -8,6 +8,7 @@
 SIZES = (8, 2, 4, 4, 2)
 NEAR = ("zl", "x")
 REST = ("zl", "x", "y", "core")
+LANES = 128
 BF = jnp.bfloat16
 F32 = jnp.float32
 
@@ -61,10 +62,11 @@
         count = 3.0 * (dz * nz) * (ff_dev * nt)
 
         chosen = pool.at[picks].get(mode="promise_in_bounds")
-        wide = gather(chosen, ("y", "core"), nt)
-        wide = wide.transpose(1, 0, 2).reshape(tok_dev, nz, dz).transpose(1, 0, 2)
-        wide = jnp.broadcast_to(wide[:, None], (nz, nx, tok_dev, dz))
-        inputs = exchange(wide.reshape(nz * nx, tok_dev, dz), ("zh", *NEAR)).reshape(tokens, dz)
+        swap = [(i * nt + j, j * nz + i) for i in range(nz) for j in range(nt)]
+        chosen = lax.ppermute(chosen, ("zh", "y", "core"), swap)
+        inputs = gather(chosen, REST, nr).reshape(tokens, dz)
+        targets = targets.reshape(nz, nx, tok_dev, d_dev).transpose(1, 0, 2, 3)
+        targets = targets.reshape(tokens, d_dev)
 
         mats = jnp.stack(
             [
@@ -182,19 +184,27 @@
         delta_gate = both[:, :sub].reshape(ff, tokens)
         delta_up = both[:, sub : 2 * sub].reshape(ff, tokens)
         sums = both[:, 2 * sub :].reshape(nz, 2, 2, tokens).astype(F32)
-        sums = jnp.sum(gather(jnp.sum(sums, axis=(0, 2)), REST, nr), axis=0)
-        scale = 1.0 / jnp.sqrt(total(sums[1:]) / count + 1e-6)
-
-        hv = jnp.stack(
-            [
+        sums = jnp.sum(sums, axis=(0, 2))
+        if tokens > LANES:
+            sums = sums[:, :LANES] + sums[:, LANES:]
+        sums = jnp.pad(sums, ((0, 0), (0, LANES - sums.shape[1])))
+        sums = terms(sums)
+
+        hv = [
+            jnp.pad(v.reshape(nx, d_dev, ff), ((0, 0), (0, 0), (0, LANES - ff)))
+            for v in (
                 dot(inputs, delta_gate, 0, 1).astype(BF),
                 dot(inputs, delta_up, 0, 1).astype(BF),
                 hv_down2.astype(BF),
-            ]
-        )
-        hv = hv.reshape(3, nx, d_dev, ff).transpose(1, 0, 2, 3)
-        hv = exchange(hv, NEAR).transpose(1, 2, 0, 3).reshape(3, d_dev, ff_dev)
-        hv = hv.astype(F32) * scale
+            )
+        ]
+        hv.append(jnp.broadcast_to(sums[None], (nx,) + sums.shape))
+        got = exchange(jnp.concatenate(hv, axis=1), NEAR)
+        sums = jnp.sum(got[:, 3 * d_dev :].astype(F32), axis=0)
+        sums = jnp.sum(gather(sums[:2] + sums[2:], ("y", "core"), nt), axis=0)
+        scale = 1.0 / jnp.sqrt(total(sums[1:]) / count + 1e-6)
+        hv = got[:, : 3 * d_dev, :ff].reshape(nx, 3, d_dev, ff)
+        hv = hv.transpose(1, 2, 0, 3).reshape(3, d_dev, ff_dev).astype(F32) * scale
         return hv[0], hv[1], hv[2].T, jnp.sum(sums[0]) / count
 
     return body

time: 289 us -> 281 us (0.972)
  waiting for transfers between devices: 106 us -> 89.9 us
  blocking collectives: 86.2 us -> 100 us
  starting transfers between devices: 63.5 us -> 59.2 us
    all_to_all x10 -> x8, waiting for transfers between devices: 106 us -> 88.6 us  [exchange(): return lax.all_to_all(v, axes, split_axis=0, concat_axis=0, tiled=True)]
    all_to_all x5 -> x6, blocking collectives: 86.2 us -> 100 us  [exchange(): return lax.all_to_all(v, axes, split_axis=0, concat_axis=0, tiled=True)]
    all_to_all x10 -> x8, starting transfers between devices: 63.5 us -> 52.9 us  [exchange(): return lax.all_to_all(v, axes, split_axis=0, concat_axis=0, tiled=True)]
    ppermute x0 -> x1, starting transfers between devices: none -> 6.29 us  [body(): chosen = lax.ppermute(chosen, ('zh', 'y', 'core'), swap)]
  transfers between devices with their start and end apart: 10 -> 9, of which waited for: 10 -> 9; matrix products, arithmetic and copies ran while one was open for 3% -> 2% of each run, Pallas kernels for 0% -> 0%
where the time goes in v3:
time: 281 us; the launch traced here: 279 us
  blocking collectives  100 us (36%)
  waiting for transfers between devices  89.9 us (32%)
  starting transfers between devices  59.2 us (21%)
  local copies, waits for them, and re-layouts  14.7 us (5%)
  matrix products  7.54 us (3%)
  between operations  4.61 us (2%)
  other arithmetic  3.42 us (1%)
    all_to_all x6, blocking collectives, exchange(): return lax.all_to_all(v, axes, split_axis=0, concat_axis=0, tiled=True)  100 us
    all_to_all x8, waiting for transfers between devices, exchange(): return lax.all_to_all(v, axes, split_axis=0, concat_axis=0, tiled=True)  88.6 us
    all_to_all x8, starting transfers between devices, exchange(): return lax.all_to_all(v, axes, split_axis=0, concat_axis=0, tiled=True)  52.9 us
    ppermute x1, starting transfers between devices, body(): chosen = lax.ppermute(chosen, ('zh', 'y', 'core'), swap)  6.29 us
    dot_general x21, matrix products, dot(): lax.dot_general(a, b, (((ca,), (cb,)), ((), ())), preferred_element_type=...  5.86 us
  transfers between devices with their start and end apart: 9, of which 9 were waited for; matrix products, arithmetic and copies ran while one was open for 2% of the time, Pallas kernels for 0%

profile of v3, /device:TPU:1, one launch (start us, length us, event | category | flops | bytes accessed | tf_op | source)
XLA Modules:
  0.0 279.4 jit_solution(1267198875987868247)
XLA Ops:
  2.4 6.3 %collective-permute-start = (bf16[4,512]{1,0:T(4,128)(2,1)S(1)}, bf16[4,512]{1,0:T(4,128)(2,1)S(1)}, u32[]{:S(2)}, u32[]{:S(2)}) collective-permute-start(bf16[4,512]{1,0:T(4,128)(2,1)S(1)} %gather_fusion), channel_id=1, source_target_pairs={{0,0},{1,64},{2,128},{3,192},{4,256},{5,320},{6,384},{7,448},{64,1... | collective-permute-start | bytes 12296 | tf_op jit(solution)/shard_map/ppermute | solution.py:66
  8.7 1.3 collective-permute-done
  10.0 0.8 broadcast_in_dim.39
  10.8 19.5 %all-to-all-start = ((bf16[64,4,512]{2,1,0:T(4,128)(2,1)}), bf16[64,4,512]{2,1,0:T(4,128)(2,1)S(1)}, u32[]{:S(2)}, u32[]{:S(2)}) async-start(bf16[64,4,512]{2,1,0:T(4,128)(2,1)} %broadcast_in_dim.39), calls=%async_computation | async-start | bytes 524288 | tf_op jit(solution)/shard_map/all_to_all | solution.py:21
  33.7 1.1 copy.138
  34.8 5.3 %all-to-all-done = bf16[64,4,512]{2,1,0:T(4,128)(2,1)S(1)} async-done(((bf16[64,4,512]{2,1,0:T(4,128)(2,1)}), bf16[64,4,512]{2,1,0:T(4,128)(2,1)S(1)}, u32[]{:S(2)}, u32[]{:S(2)}) %all-to-all-start) | async-done | bytes 262176 | tf_op jit(solution)/shard_map/all_to_all | solution.py:21
  40.1 3.5 %all-to-all-start.1 = ((bf16[8,6,64,112]{3,2,1,0:T(8,128)(2,1)}), bf16[8,6,64,112]{3,2,1,0:T(8,128)(2,1)S(1)}, u32[]{:S(2)}, u32[]{:S(2)}) async-start(bf16[8,6,64,112]{3,2,1,0:T(8,128)(2,1)} %copy.138), calls=%async_computation.1 | async-start | bytes 1572864 | tf_op jit(solution)/shard_map/all_to_all | solution.py:21
  44.0 11.7 %all-to-all-done.1 = bf16[8,6,64,112]{3,2,1,0:T(8,128)(2,1)S(1)} async-done(((bf16[8,6,64,112]{3,2,1,0:T(8,128)(2,1)}), bf16[8,6,64,112]{3,2,1,0:T(8,128)(2,1)S(1)}, u32[]{:S(2)}, u32[]{:S(2)}) %all-to-all-start.1) | async-done | bytes 688160 | tf_op jit(solution)/shard_map/all_to_all | solution.py:21
  56.3 27.6 %all_to_all.70 = bf16[8,64,256]{2,1,0:T(8,128)(2,1)S(1)} all-to-all(bf16[8,64,256]{2,1,0:T(8,128)(2,1)S(1)} %copy.143), channel_id=1, replica_groups=mesh['zh'=8,'zl'=2,'x'=4,'y'=4,'core'=2] {'zh'}, dimensions={0} | all-to-all | bytes 524288 | tf_op jit(solution)/shard_map/all_to_all | solution.py:21
  84.7 6.8 %all-to-all-start.3 = ((bf16[8,28,256]{2,1,0:T(8,128)(2,1)}), bf16[8,28,256]{2,1,0:T(8,128)(2,1)S(1)}, u32[]{:S(2)}, u32[]{:S(2)}) async-start(bf16[8,28,256]{2,1,0:T(8,128)(2,1)} %broadcast_in_dim.41), calls=%async_computation.3 | async-start | bytes 262144 | tf_op jit(solution)/shard_map/all_to_all | solution.py:21
  91.5 13.5 %all-to-all-done.3 = bf16[8,28,256]{2,1,0:T(8,128)(2,1)S(1)} async-done(((bf16[8,28,256]{2,1,0:T(8,128)(2,1)}), bf16[8,28,256]{2,1,0:T(8,128)(2,1)S(1)}, u32[]{:S(2)}, u32[]{:S(2)}) %all-to-all-start.3) | async-done | bytes 114720 | tf_op jit(solution)/shard_map/all_to_all | solution.py:21
  105.8 0.8 maximum_bitcast_fusion
  106.6 8.3 %all-to-all-start.4 = ((bf16[64,2,8,256]{3,2,1,0:T(8,128)(2,1)}), bf16[64,2,8,256]{3,2,1,0:T(8,128)(2,1)S(1)}, u32[]{:S(2)}, u32[]{:S(2)}) async-start(bf16[64,2,8,256]{3,2,1,0:T(8,128)(2,1)} %maximum_bitcast_fusion), calls=%async_computation.4 | async-start | bytes 1048576 | tf_op jit(solution)/shard_map/all_to_all | solution.py:21
  115.2 11.9 %all-to-all-done.4 = bf16[64,2,8,256]{3,2,1,0:T(8,128)(2,1)S(1)} async-done(((bf16[64,2,8,256]{3,2,1,0:T(8,128)(2,1)}), bf16[64,2,8,256]{3,2,1,0:T(8,128)(2,1)S(1)}, u32[]{:S(2)}, u32[]{:S(2)}) %all-to-all-start.4) | async-done | bytes 524320 | tf_op jit(solution)/shard_map/all_to_all | solution.py:21
  127.3 19.1 %all_to_all.71 = bf16[64,24,256]{2,1,0:T(8,128)(2,1)S(1)} all-to-all(bf16[64,24,256]{2,1,0:T(8,128)(2,1)S(1)} %broadcast_in_dim.42), channel_id=1, replica_groups=mesh['zh'=8,'zl'=2,'x'=4,'y'=4,'core'=2] {'zl','x','y','core'}, dimensions={0} | all-to-all | bytes 1572864 | tf_op jit(solution)/shard_map/all_to_all | solution.py:21
  147.2 0.8 copy.150
  147.9 3.4 %all-to-all-start.6 = ((bf16[8,2,14,256]{3,1,2,0:T(2,128)(2,1)}), bf16[8,2,14,256]{3,1,2,0:T(2,128)(2,1)S(1)}, u32[]{:S(2)}, u32[]{:S(2)}) async-start(bf16[8,2,14,256]{3,1,2,0:T(2,128)(2,1)} %copy.150), calls=%async_computation.6 | async-start | bytes 229376 | tf_op jit(solution)/shard_map/all_to_all | solution.py:21
  152.0 14.9 %all-to-all-done.6 = bf16[8,2,14,256]{3,1,2,0:T(2,128)(2,1)S(1)} async-done(((bf16[8,2,14,256]{3,1,2,0:T(2,128)(2,1)}), bf16[8,2,14,256]{3,1,2,0:T(2,128)(2,1)S(1)}, u32[]{:S(2)}, u32[]{:S(2)}) %all-to-all-start.6) | async-done | bytes 114720 | tf_op jit(solution)/shard_map/all_to_all | solution.py:21
  167.6 14.6 %all_to_all.72 = bf16[8,16,256]{2,1,0:T(8,128)(2,1)S(1)} all-to-all(bf16[8,16,256]{2,1,0:T(8,128)(2,1)S(1)} %broadcast_in_dim.45), channel_id=1, replica_groups=mesh['zh'=8,'zl'=2,'x'=4,'y'=4,'core'=2] {'zh'}, dimensions={0} | all-to-all | bytes 131072 | tf_op jit(solution)/shard_map/all_to_all | solution.py:21
  183.3 17.7 %all_to_all.73 = bf16[64,10,256]{2,1,0:T(8,128)(2,1)S(1)} all-to-all(bf16[64,10,256]{2,1,0:T(8,128)(2,1)S(1)} %pad_maximum_fusion), channel_id=1, replica_groups=mesh['zh'=8,'zl'=2,'x'=4,'y'=4,'core'=2] {'zl','x','y','core'}, dimensions={0} | all-to-all | bytes 655360 | tf_op jit(solution)/shard_map/all_to_all | solution.py:21
  201.8 4.6 %all-to-all-start.9 = ((bf16[64,8,256]{2,1,0:T(8,128)(2,1)}), bf16[64,8,256]{2,1,0:T(8,128)(2,1)S(1)}, u32[]{:S(2)}, u32[]{:S(2)}) async-start(bf16[64,8,256]{2,1,0:T(8,128)(2,1)} %broadcast_in_dim.47), calls=%async_computation.9 | async-start | bytes 524288 | tf_op jit(solution)/shard_map/all_to_all | solution.py:21
  206.5 1.7 fusion.22
  209.7 6.5 %all-to-all-done.9 = bf16[64,8,256]{2,1,0:T(8,128)(2,1)S(1)} async-done(((bf16[64,8,256]{2,1,0:T(8,128)(2,1)}), bf16[64,8,256]{2,1,0:T(8,128)(2,1)S(1)}, u32[]{:S(2)}, u32[]{:S(2)}) %all-to-all-start.9) | async-done | bytes 262176 | tf_op jit(solution)/shard_map/all_to_all | solution.py:21
  217.3 3.4 %all-to-all-start.10 = ((bf16[8,14,256]{2,1,0:T(8,128)(2,1)}), bf16[8,14,256]{2,1,0:T(8,128)(2,1)S(1)}, u32[]{:S(2)}, u32[]{:S(2)}) async-start(bf16[8,14,256]{2,1,0:T(8,128)(2,1)} %reshape.175), calls=%async_computation.10 | async-start | bytes 131072 | tf_op jit(solution)/shard_map/all_to_all | solution.py:21
  221.0 11.5 %all-to-all-done.10 = bf16[8,14,256]{2,1,0:T(8,128)(2,1)S(1)} async-done(((bf16[8,14,256]{2,1,0:T(8,128)(2,1)}), bf16[8,14,256]{2,1,0:T(8,128)(2,1)S(1)}, u32[]{:S(2)}, u32[]{:S(2)}) %all-to-all-start.10) | async-done | bytes 57376 | tf_op jit(solution)/shard_map/all_to_all | solution.py:21
  233.8 3.4 %all-to-all-start.11 = ((bf16[8,32,256]{2,1,0:T(8,128)(2,1)}), bf16[8,32,256]{2,1,0:T(8,128)(2,1)S(1)}, u32[]{:S(2)}, u32[]{:S(2)}) async-start(bf16[8,32,256]{2,1,0:T(8,128)(2,1)} %broadcast_in_dim.105), calls=%async_computation.11 | async-start | bytes 262144 | tf_op jit(solution)/shard_map/all_to_all | solution.py:21
  237.3 13.3 %all-to-all-done.11 = bf16[8,32,256]{2,1,0:T(8,128)(2,1)S(1)} async-done(((bf16[8,32,256]{2,1,0:T(8,128)(2,1)}), bf16[8,32,256]{2,1,0:T(8,128)(2,1)S(1)}, u32[]{:S(2)}, u32[]{:S(2)}) %all-to-all-start.11) | async-done | bytes 131104 | tf_op jit(solution)/shard_map/all_to_all | solution.py:21
  251.5 9.3 %all_to_all.74 = bf16[8,196,128]{2,1,0:T(8,128)(2,1)S(1)} all-to-all(bf16[8,196,128]{2,1,0:T(8,128)(2,1)S(1)} %fusion.16), channel_id=1, replica_groups=mesh['zh'=8,'zl'=2,'x'=4,'y'=4,'core'=2] {'zl','x'}, dimensions={0} | all-to-all | bytes 802816 | tf_op jit(solution)/shard_map/all_to_all | solution.py:21
  260.9 11.7 %all_to_all.75 = f32[8,2,128]{2,1,0:T(2,128)S(1)} all-to-all(f32[8,2,128]{2,1,0:T(2,128)S(1)} %broadcast_in_dim.107), channel_id=1, replica_groups=mesh['zh'=8,'zl'=2,'x'=4,'y'=4,'core'=2] {'y','core'}, dimensions={0} | all-to-all | bytes 16384 | tf_op jit(solution)/shard_map/all_to_all | solution.py:21
  274.9 0.8 squeeze.33
  275.8 0.8 squeeze.31
  276.8 0.8 squeeze.32
  (147 shorter events, 18.1 us)
Async XLA Ops:
  0.6 1.2 copy-start
  2.4 7.6 %collective-permute-start = (bf16[4,512]{1,0:T(4,128)(2,1)S(1)}, bf16[4,512]{1,0:T(4,128)(2,1)S(1)}, u32[]{:S(2)}, u32[]{:S(2)}) collective-permute-start(bf16[4,512]{1,0:T(4,128)(2,1)S(1)} %gather_fusion), channel_id=1, source_target_pairs={{0,0},{1,64},{2,128},{3,192},{4,256},{5,320},{6,384},{7,448},{64,1... | collective-permute-start | bytes 12296 | tf_op jit(solution)/shard_map/ppermute | solution.py:66
  10.8 19.5 %copy-start.8 = (bf16[64,896]{1,0:T(8,128)(2,1)S(1)}, bf16[64,896]{1,0:T(8,128)(2,1)}, u32[]{:S(2)}) copy-start(bf16[64,896]{1,0:T(8,128)(2,1)} %param.12) | copy-start | bytes 344068
  10.8 19.7 %copy-start.9 = (bf16[64,896]{1,0:T(8,128)(2,1)S(1)}, bf16[64,896]{1,0:T(8,128)(2,1)}, u32[]{:S(2)}) copy-start(bf16[64,896]{1,0:T(8,128)(2,1)} %param.13) | copy-start | bytes 344068
  10.8 29.3 %all-to-all-start = ((bf16[64,4,512]{2,1,0:T(4,128)(2,1)}), bf16[64,4,512]{2,1,0:T(4,128)(2,1)S(1)}, u32[]{:S(2)}, u32[]{:S(2)}) async-start(bf16[64,4,512]{2,1,0:T(4,128)(2,1)} %broadcast_in_dim.39), calls=%async_computation | async-start | bytes 524288 | tf_op jit(solution)/shard_map/all_to_all | solution.py:21
  30.3 0.9 copy-start.5
  31.3 0.9 copy-start.6
  32.2 0.9 copy-start.10
  32.2 1.1 copy-start.7
  40.1 15.6 %all-to-all-start.1 = ((bf16[8,6,64,112]{3,2,1,0:T(8,128)(2,1)}), bf16[8,6,64,112]{3,2,1,0:T(8,128)(2,1)S(1)}, u32[]{:S(2)}, u32[]{:S(2)}) async-start(bf16[8,6,64,112]{3,2,1,0:T(8,128)(2,1)} %copy.138), calls=%async_computation.1 | async-start | bytes 1572864 | tf_op jit(solution)/shard_map/all_to_all | solution.py:21
  84.7 20.4 %all-to-all-start.3 = ((bf16[8,28,256]{2,1,0:T(8,128)(2,1)}), bf16[8,28,256]{2,1,0:T(8,128)(2,1)S(1)}, u32[]{:S(2)}, u32[]{:S(2)}) async-start(bf16[8,28,256]{2,1,0:T(8,128)(2,1)} %broadcast_in_dim.41), calls=%async_computation.3 | async-start | bytes 262144 | tf_op jit(solution)/shard_map/all_to_all | solution.py:21
  106.6 8.3 %copy-start.11 = (bf16[256,64]{0,1:T(8,128)(2,1)S(1)}, bf16[256,64]{0,1:T(8,128)(2,1)}, u32[]{:S(2)}) copy-start(bf16[256,64]{0,1:T(8,128)(2,1)} %param.11) | copy-start | bytes 98308
  106.6 20.5 %all-to-all-start.4 = ((bf16[64,2,8,256]{3,2,1,0:T(8,128)(2,1)}), bf16[64,2,8,256]{3,2,1,0:T(8,128)(2,1)S(1)}, u32[]{:S(2)}, u32[]{:S(2)}) async-start(bf16[64,2,8,256]{3,2,1,0:T(8,128)(2,1)} %maximum_bitcast_fusion), calls=%async_computation.4 | async-start | bytes 1048576 | tf_op jit(solution)/shard_map/all_to_all | solution.py:21
  147.9 19.0 %all-to-all-start.6 = ((bf16[8,2,14,256]{3,1,2,0:T(2,128)(2,1)}), bf16[8,2,14,256]{3,1,2,0:T(2,128)(2,1)S(1)}, u32[]{:S(2)}, u32[]{:S(2)}) async-start(bf16[8,2,14,256]{3,1,2,0:T(2,128)(2,1)} %copy.150), calls=%async_computation.6 | async-start | bytes 229376 | tf_op jit(solution)/shard_map/all_to_all | solution.py:21
  151.5 15.7 %copy-start.1 = (bf16[256,256]{1,0:T(8,128)(2,1)}, bf16[256,256]{1,0:T(8,128)(2,1)S(1)}, u32[]{:S(2)}) copy-start(bf16[256,256]{1,0:T(8,128)(2,1)S(1)} %reshape.170) | copy-start | bytes 393220
  182.2 0.6 copy-start.4
  201.8 14.4 %all-to-all-start.9 = ((bf16[64,8,256]{2,1,0:T(8,128)(2,1)}), bf16[64,8,256]{2,1,0:T(8,128)(2,1)S(1)}, u32[]{:S(2)}, u32[]{:S(2)}) async-start(bf16[64,8,256]{2,1,0:T(8,128)(2,1)} %broadcast_in_dim.47), calls=%async_computation.9 | async-start | bytes 524288 | tf_op jit(solution)/shard_map/all_to_all | solution.py:21
  216.6 4.0 %copy-start.3 = (f32[512,112]{0,1:T(8,128)S(1)}, f32[512,112]{0,1:T(8,128)}, u32[]{:S(2)}) copy-start(f32[512,112]{0,1:T(8,128)} %fusion.22) | copy-start | bytes 688132
  217.3 15.2 %all-to-all-start.10 = ((bf16[8,14,256]{2,1,0:T(8,128)(2,1)}), bf16[8,14,256]{2,1,0:T(8,128)(2,1)S(1)}, u32[]{:S(2)}, u32[]{:S(2)}) async-start(bf16[8,14,256]{2,1,0:T(8,128)(2,1)} %reshape.175), calls=%async_computation.10 | async-start | bytes 131072 | tf_op jit(solution)/shard_map/all_to_all | solution.py:21
  221.0 11.6 %copy-start.2 = (bf16[256,256]{1,0:T(8,128)(2,1)S(1)}, bf16[256,256]{1,0:T(8,128)(2,1)}, u32[]{:S(2)}) copy-start(bf16[256,256]{1,0:T(8,128)(2,1)} %copy-done.1) | copy-start | bytes 393220
  233.8 16.8 %all-to-all-start.11 = ((bf16[8,32,256]{2,1,0:T(8,128)(2,1)}), bf16[8,32,256]{2,1,0:T(8,128)(2,1)S(1)}, u32[]{:S(2)}, u32[]{:S(2)}) async-start(bf16[8,32,256]{2,1,0:T(8,128)(2,1)} %broadcast_in_dim.105), calls=%async_computation.11 | async-start | bytes 262144 | tf_op jit(solution)/shard_map/all_to_all | solution.py:21

commit v4 on v3

--- a/solution.py
+++ b/solution.py
@@ -64,7 +64,6 @@
         chosen = pool.at[picks].get(mode="promise_in_bounds")
         swap = [(i * nt + j, j * nz + i) for i in range(nz) for j in range(nt)]
         chosen = lax.ppermute(chosen, ("zh", "y", "core"), swap)
-        inputs = gather(chosen, REST, nr).reshape(tokens, dz)
         targets = targets.reshape(nz, nx, tok_dev, d_dev).transpose(1, 0, 2, 3)
         targets = targets.reshape(tokens, d_dev)
 
@@ -79,7 +78,10 @@
             ]
         )
         mats = mats.reshape(6, d_dev, nx, ff).transpose(2, 0, 1, 3)
-        mats = exchange(mats, NEAR).transpose(1, 0, 2, 3).reshape(6, dz, ff)
+        mats = exchange(mats, NEAR)
+        chosen, mats = lax.optimization_barrier((chosen, mats))
+        mats = mats.transpose(1, 0, 2, 3).reshape(6, dz, ff)
+        inputs = gather(chosen, REST, nr).reshape(tokens, dz)
         down, pdown = mats[4], mats[5]
 
         first = lax.dot_general(
@@ -161,11 +163,13 @@
 
         hv_down_b = hv_down.astype(BF)
         tan_out = dot(down, tan_hidden, 1, 0) + dot(hv_down_b, hidden, 1, 0)
-        packed = tan_out.astype(BF).reshape(nr, rows, tokens)
-        scal = jnp.broadcast_to(terms(square)[None], (nr, 2, tokens))
+        packed = tan_out.astype(BF).reshape(nr, rows, 2, tokens // 2)
+        scal = terms(square[:, : tokens // 2] + square[:, tokens // 2 :])
+        scal = jnp.broadcast_to(scal[None, None], (nr, 1, 2, tokens // 2))
         got = exchange(jnp.concatenate([packed, scal], axis=1), REST)
-        square = jnp.sum(got[:, rows:].astype(F32), axis=(0, 1))[None]
-        got = jnp.sum(got[:, :rows].astype(F32), axis=0)
+        got, square = got[:, :rows].astype(F32), got[:, rows:].astype(F32)
+        square = jnp.sum(square, axis=(0, 1, 2))[None]
+        got = jnp.sum(got, axis=0).reshape(rows, tokens)
         scale = 1.0 / jnp.sqrt(total(square) / count + 1e-6)
         tan_resid = (got / tokens).astype(BF)
         tan_resid = gather(tan_resid, REST, nr).reshape(dz, tokens)

time: 281 us -> 273 us (0.972)
  waiting for transfers between devices: 89.9 us -> 84.5 us
  blocking collectives: 100 us -> 95.1 us
  starting transfers between devices: 59.2 us -> 62.7 us
    all_to_all x8, waiting for transfers between devices: 88.6 us -> 83.2 us  [exchange(): return lax.all_to_all(v, axes, split_axis=0, concat_axis=0, tiled=True)]
    all_to_all x6, blocking collectives: 100 us -> 95.1 us  [exchange(): return lax.all_to_all(v, axes, split_axis=0, concat_axis=0, tiled=True)]
    all_to_all x8, starting transfers between devices: 52.9 us -> 57 us  [exchange(): return lax.all_to_all(v, axes, split_axis=0, concat_axis=0, tiled=True)]
  transfers between devices with their start and end apart: 9 -> 9, of which waited for: 9 -> 9; matrix products, arithmetic and copies ran while one was open for 2% -> 1% of each run, Pallas kernels for 0% -> 0%
where the time goes in v4:
time: 273 us; the launch traced here: 272 us
  blocking collectives  95.1 us (35%)
  waiting for transfers between devices  84.5 us (31%)
  starting transfers between devices  62.7 us (23%)
  local copies, waits for them, and re-layouts  15.4 us (6%)
  matrix products  6.73 us (2%)
  between operations  4.6 us (2%)
  other arithmetic  3 us (1%)
    all_to_all x6, blocking collectives, exchange(): return lax.all_to_all(v, axes, split_axis=0, concat_axis=0, tiled=True)  95.1 us
    all_to_all x8, waiting for transfers between devices, exchange(): return lax.all_to_all(v, axes, split_axis=0, concat_axis=0, tiled=True)  83.2 us
    all_to_all x8, starting transfers between devices, exchange(): return lax.all_to_all(v, axes, split_axis=0, concat_axis=0, tiled=True)  57 us
    ppermute x1, starting transfers between devices, body(): chosen = lax.ppermute(chosen, ('zh', 'y', 'core'), swap)  5.74 us
  transfers between devices with their start and end apart: 9, of which 9 were waited for; matrix products, arithmetic and copies ran while one was open for 1% of the time, Pallas kernels for 0%

profile of v4, /device:TPU:1, one launch (start us, length us, event | category | flops | bytes accessed | tf_op | source)
XLA Modules:
  0.0 272.1 jit_solution(14211639446706533519)
XLA Ops:
  0.7 1.2 stack.39
  5.2 1.1 copy.168
  6.2 6.3 %all-to-all-start = ((bf16[8,6,64,112]{3,2,1,0:T(8,128)(2,1)}), bf16[8,6,64,112]{3,2,1,0:T(8,128)(2,1)S(1)}, u32[]{:S(2)}, u32[]{:S(2)}) async-start(bf16[8,6,64,112]{3,2,1,0:T(8,128)(2,1)} %copy.168), calls=%async_computation | async-start | bytes 1572864 | tf_op jit(solution)/shard_map/all_to_all | solution.py:21
  13.2 5.7 %collective-permute-start = (bf16[4,512]{1,0:T(4,128)(2,1)S(1)}, bf16[4,512]{1,0:T(4,128)(2,1)S(1)}, u32[]{:S(2)}, u32[]{:S(2)}) collective-permute-start(bf16[4,512]{1,0:T(4,128)(2,1)S(1)} %gather_fusion), channel_id=1, source_target_pairs={{0,0},{1,64},{2,128},{3,192},{4,256},{5,320},{6,384},{7,448},{64,1... | collective-permute-start | bytes 12296 | tf_op jit(solution)/shard_map/ppermute | solution.py:66
  18.9 1.4 collective-permute-done
  20.9 0.8 broadcast_in_dim.37
  21.7 23.1 %all-to-all-start.1 = ((bf16[64,4,512]{2,1,0:T(4,128)(2,1)}), bf16[64,4,512]{2,1,0:T(4,128)(2,1)S(1)}, u32[]{:S(2)}, u32[]{:S(2)}) async-start(bf16[64,4,512]{2,1,0:T(4,128)(2,1)} %broadcast_in_dim.37), calls=%async_computation.1 | async-start | bytes 524288 | tf_op jit(solution)/shard_map/all_to_all | solution.py:21
  44.9 9.6 %all-to-all-done.1 = bf16[64,4,512]{2,1,0:T(4,128)(2,1)S(1)} async-done(((bf16[64,4,512]{2,1,0:T(4,128)(2,1)}), bf16[64,4,512]{2,1,0:T(4,128)(2,1)S(1)}, u32[]{:S(2)}, u32[]{:S(2)}) %all-to-all-start.1) | async-done | bytes 262176 | tf_op jit(solution)/shard_map/all_to_all | solution.py:21
  55.5 24.5 %all_to_all.70 = bf16[8,64,256]{2,1,0:T(8,128)(2,1)S(1)} all-to-all(bf16[8,64,256]{2,1,0:T(8,128)(2,1)S(1)} %copy.173), channel_id=1, replica_groups=mesh['zh'=8,'zl'=2,'x'=4,'y'=4,'core'=2] {'zh'}, dimensions={0} | all-to-all | bytes 524288 | tf_op jit(solution)/shard_map/all_to_all | solution.py:21
  80.8 6.2 %all-to-all-start.3 = ((bf16[8,28,256]{2,1,0:T(8,128)(2,1)}), bf16[8,28,256]{2,1,0:T(8,128)(2,1)S(1)}, u32[]{:S(2)}, u32[]{:S(2)}) async-start(bf16[8,28,256]{2,1,0:T(8,128)(2,1)} %broadcast_in_dim.39), calls=%async_computation.3 | async-start | bytes 262144 | tf_op jit(solution)/shard_map/all_to_all | solution.py:21
  87.0 14.0 %all-to-all-done.3 = bf16[8,28,256]{2,1,0:T(8,128)(2,1)S(1)} async-done(((bf16[8,28,256]{2,1,0:T(8,128)(2,1)}), bf16[8,28,256]{2,1,0:T(8,128)(2,1)S(1)}, u32[]{:S(2)}, u32[]{:S(2)}) %all-to-all-start.3) | async-done | bytes 114720 | tf_op jit(solution)/shard_map/all_to_all | solution.py:21
  101.7 0.8 maximum_bitcast_fusion
  102.6 6.6 %all-to-all-start.4 = ((bf16[64,2,8,256]{3,2,1,0:T(8,128)(2,1)}), bf16[64,2,8,256]{3,2,1,0:T(8,128)(2,1)S(1)}, u32[]{:S(2)}, u32[]{:S(2)}) async-start(bf16[64,2,8,256]{3,2,1,0:T(8,128)(2,1)} %maximum_bitcast_fusion), calls=%async_computation.4 | async-start | bytes 1048576 | tf_op jit(solution)/shard_map/all_to_all | solution.py:21
  109.5 12.0 %all-to-all-done.4 = bf16[64,2,8,256]{3,2,1,0:T(8,128)(2,1)S(1)} async-done(((bf16[64,2,8,256]{3,2,1,0:T(8,128)(2,1)}), bf16[64,2,8,256]{3,2,1,0:T(8,128)(2,1)S(1)}, u32[]{:S(2)}, u32[]{:S(2)}) %all-to-all-start.4) | async-done | bytes 524320 | tf_op jit(solution)/shard_map/all_to_all | solution.py:21
  121.6 19.0 %all_to_all.71 = bf16[64,24,256]{2,1,0:T(8,128)(2,1)S(1)} all-to-all(bf16[64,24,256]{2,1,0:T(8,128)(2,1)S(1)} %broadcast_in_dim.40), channel_id=1, replica_groups=mesh['zh'=8,'zl'=2,'x'=4,'y'=4,'core'=2] {'zl','x','y','core'}, dimensions={0} | all-to-all | bytes 1572864 | tf_op jit(solution)/shard_map/all_to_all | solution.py:21
  141.4 0.8 copy.180
  142.1 3.4 %all-to-all-start.6 = ((bf16[8,2,14,256]{3,1,2,0:T(2,128)(2,1)}), bf16[8,2,14,256]{3,1,2,0:T(2,128)(2,1)S(1)}, u32[]{:S(2)}, u32[]{:S(2)}) async-start(bf16[8,2,14,256]{3,1,2,0:T(2,128)(2,1)} %copy.180), calls=%async_computation.6 | async-start | bytes 229376 | tf_op jit(solution)/shard_map/all_to_all | solution.py:21
  146.2 14.9 %all-to-all-done.6 = bf16[8,2,14,256]{3,1,2,0:T(2,128)(2,1)S(1)} async-done(((bf16[8,2,14,256]{3,1,2,0:T(2,128)(2,1)}), bf16[8,2,14,256]{3,1,2,0:T(2,128)(2,1)S(1)}, u32[]{:S(2)}, u32[]{:S(2)}) %all-to-all-start.6) | async-done | bytes 114720 | tf_op jit(solution)/shard_map/all_to_all | solution.py:21
  161.7 14.6 %all_to_all.72 = bf16[8,16,256]{2,1,0:T(8,128)(2,1)S(1)} all-to-all(bf16[8,16,256]{2,1,0:T(8,128)(2,1)S(1)} %broadcast_in_dim.43), channel_id=1, replica_groups=mesh['zh'=8,'zl'=2,'x'=4,'y'=4,'core'=2] {'zh'}, dimensions={0} | all-to-all | bytes 131072 | tf_op jit(solution)/shard_map/all_to_all | solution.py:21
  177.6 15.6 %all_to_all.73 = bf16[64,9,2,128]{3,2,1,0:T(2,128)(2,1)S(1)} all-to-all(bf16[64,9,2,128]{3,2,1,0:T(2,128)(2,1)S(1)} %pad_maximum_fusion), channel_id=1, replica_groups=mesh['zh'=8,'zl'=2,'x'=4,'y'=4,'core'=2] {'zl','x','y','core'}, dimensions={0} | all-to-all | bytes 589824 | tf_op jit(solution)/shard_map/all_to_all | solution.py:21
  194.2 4.4 %all-to-all-start.9 = ((bf16[64,8,256]{2,1,0:T(8,128)(2,1)}), bf16[64,8,256]{2,1,0:T(8,128)(2,1)S(1)}, u32[]{:S(2)}, u32[]{:S(2)}) async-start(bf16[64,8,256]{2,1,0:T(8,128)(2,1)} %broadcast_in_dim.46), calls=%async_computation.9 | async-start | bytes 524288 | tf_op jit(solution)/shard_map/all_to_all | solution.py:21
  198.6 0.9 fusion.22
  201.0 7.5 %all-to-all-done.9 = bf16[64,8,256]{2,1,0:T(8,128)(2,1)S(1)} async-done(((bf16[64,8,256]{2,1,0:T(8,128)(2,1)}), bf16[64,8,256]{2,1,0:T(8,128)(2,1)S(1)}, u32[]{:S(2)}, u32[]{:S(2)}) %all-to-all-start.9) | async-done | bytes 262176 | tf_op jit(solution)/shard_map/all_to_all | solution.py:21
  209.5 3.5 %all-to-all-start.10 = ((bf16[8,14,256]{2,1,0:T(8,128)(2,1)}), bf16[8,14,256]{2,1,0:T(8,128)(2,1)S(1)}, u32[]{:S(2)}, u32[]{:S(2)}) async-start(bf16[8,14,256]{2,1,0:T(8,128)(2,1)} %reshape.159), calls=%async_computation.10 | async-start | bytes 131072 | tf_op jit(solution)/shard_map/all_to_all | solution.py:21
  213.4 11.5 %all-to-all-done.10 = bf16[8,14,256]{2,1,0:T(8,128)(2,1)S(1)} async-done(((bf16[8,14,256]{2,1,0:T(8,128)(2,1)}), bf16[8,14,256]{2,1,0:T(8,128)(2,1)S(1)}, u32[]{:S(2)}, u32[]{:S(2)}) %all-to-all-start.10) | async-done | bytes 57376 | tf_op jit(solution)/shard_map/all_to_all | solution.py:21
  226.2 3.4 %all-to-all-start.11 = ((bf16[8,32,256]{2,1,0:T(8,128)(2,1)}), bf16[8,32,256]{2,1,0:T(8,128)(2,1)S(1)}, u32[]{:S(2)}, u32[]{:S(2)}) async-start(bf16[8,32,256]{2,1,0:T(8,128)(2,1)} %broadcast_in_dim.101), calls=%async_computation.11 | async-start | bytes 262144 | tf_op jit(solution)/shard_map/all_to_all | solution.py:21
  229.7 13.1 %all-to-all-done.11 = bf16[8,32,256]{2,1,0:T(8,128)(2,1)S(1)} async-done(((bf16[8,32,256]{2,1,0:T(8,128)(2,1)}), bf16[8,32,256]{2,1,0:T(8,128)(2,1)S(1)}, u32[]{:S(2)}, u32[]{:S(2)}) %all-to-all-start.11) | async-done | bytes 131104 | tf_op jit(solution)/shard_map/all_to_all | solution.py:21
  243.7 9.4 %all_to_all.74 = bf16[8,196,128]{2,1,0:T(8,128)(2,1)S(1)} all-to-all(bf16[8,196,128]{2,1,0:T(8,128)(2,1)S(1)} %fusion.16), channel_id=1, replica_groups=mesh['zh'=8,'zl'=2,'x'=4,'y'=4,'core'=2] {'zl','x'}, dimensions={0} | all-to-all | bytes 802816 | tf_op jit(solution)/shard_map/all_to_all | solution.py:21
  253.1 12.0 %all_to_all.75 = f32[8,2,128]{2,1,0:T(2,128)S(1)} all-to-all(f32[8,2,128]{2,1,0:T(2,128)S(1)} %broadcast_in_dim.103), channel_id=1, replica_groups=mesh['zh'=8,'zl'=2,'x'=4,'y'=4,'core'=2] {'y','core'}, dimensions={0} | all-to-all | bytes 16384 | tf_op jit(solution)/shard_map/all_to_all | solution.py:21
  267.5 0.8 squeeze.31
  268.5 0.8 squeeze.32
  269.4 0.8 squeeze.33
  (143 shorter events, 17.7 us)
Async XLA Ops:
  0.6 12.0 %copy-start = (bf16[1024,512]{1,0:T(8,128)(2,1)S(1)}, bf16[1024,512]{1,0:T(8,128)(2,1)}, u32[]{:S(2)}) copy-start(bf16[1024,512]{1,0:T(8,128)(2,1)} %param.9) | copy-start | bytes 3145732
  0.6 1.2 copy-start.5
  1.8 0.9 copy-start.2
  2.8 0.9 copy-start.3
  3.7 0.9 copy-start.6
  3.7 1.1 copy-start.4
  6.2 6.3 %copy-start.8 = (s32[4]{0:T(128)S(1)}, s32[4]{0:T(128)}, u32[]{:S(2)}) copy-start(s32[4]{0:T(128)} %param.10) | copy-start | bytes 52
  6.2 14.7 %all-to-all-start = ((bf16[8,6,64,112]{3,2,1,0:T(8,128)(2,1)}), bf16[8,6,64,112]{3,2,1,0:T(8,128)(2,1)S(1)}, u32[]{:S(2)}, u32[]{:S(2)}) async-start(bf16[8,6,64,112]{3,2,1,0:T(8,128)(2,1)} %copy.168), calls=%async_computation | async-start | bytes 1572864 | tf_op jit(solution)/shard_map/all_to_all | solution.py:21
  13.2 7.1 %collective-permute-start = (bf16[4,512]{1,0:T(4,128)(2,1)S(1)}, bf16[4,512]{1,0:T(4,128)(2,1)S(1)}, u32[]{:S(2)}, u32[]{:S(2)}) collective-permute-start(bf16[4,512]{1,0:T(4,128)(2,1)S(1)} %gather_fusion), channel_id=1, source_target_pairs={{0,0},{1,64},{2,128},{3,192},{4,256},{5,320},{6,384},{7,448},{64,1... | collective-permute-start | bytes 12296 | tf_op jit(solution)/shard_map/ppermute | solution.py:66
  21.7 32.9 %all-to-all-start.1 = ((bf16[64,4,512]{2,1,0:T(4,128)(2,1)}), bf16[64,4,512]{2,1,0:T(4,128)(2,1)S(1)}, u32[]{:S(2)}, u32[]{:S(2)}) async-start(bf16[64,4,512]{2,1,0:T(4,128)(2,1)} %broadcast_in_dim.37), calls=%async_computation.1 | async-start | bytes 524288 | tf_op jit(solution)/shard_map/all_to_all | solution.py:21
  80.8 20.2 %all-to-all-start.3 = ((bf16[8,28,256]{2,1,0:T(8,128)(2,1)}), bf16[8,28,256]{2,1,0:T(8,128)(2,1)S(1)}, u32[]{:S(2)}, u32[]{:S(2)}) async-start(bf16[8,28,256]{2,1,0:T(8,128)(2,1)} %broadcast_in_dim.39), calls=%async_computation.3 | async-start | bytes 262144 | tf_op jit(solution)/shard_map/all_to_all | solution.py:21
  102.6 6.6 %copy-start.7 = (bf16[256,64]{0,1:T(8,128)(2,1)S(1)}, bf16[256,64]{0,1:T(8,128)(2,1)}, u32[]{:S(2)}) copy-start(bf16[256,64]{0,1:T(8,128)(2,1)} %param.11) | copy-start | bytes 98308
  102.6 18.9 %all-to-all-start.4 = ((bf16[64,2,8,256]{3,2,1,0:T(8,128)(2,1)}), bf16[64,2,8,256]{3,2,1,0:T(8,128)(2,1)S(1)}, u32[]{:S(2)}, u32[]{:S(2)}) async-start(bf16[64,2,8,256]{3,2,1,0:T(8,128)(2,1)} %maximum_bitcast_fusion), calls=%async_computation.4 | async-start | bytes 1048576 | tf_op jit(solution)/shard_map/all_to_all | solution.py:21
  142.1 19.0 %all-to-all-start.6 = ((bf16[8,2,14,256]{3,1,2,0:T(2,128)(2,1)}), bf16[8,2,14,256]{3,1,2,0:T(2,128)(2,1)S(1)}, u32[]{:S(2)}, u32[]{:S(2)}) async-start(bf16[8,2,14,256]{3,1,2,0:T(2,128)(2,1)} %copy.180), calls=%async_computation.6 | async-start | bytes 229376 | tf_op jit(solution)/shard_map/all_to_all | solution.py:21
  194.2 14.3 %all-to-all-start.9 = ((bf16[64,8,256]{2,1,0:T(8,128)(2,1)}), bf16[64,8,256]{2,1,0:T(8,128)(2,1)S(1)}, u32[]{:S(2)}, u32[]{:S(2)}) async-start(bf16[64,8,256]{2,1,0:T(8,128)(2,1)} %broadcast_in_dim.46), calls=%async_computation.9 | async-start | bytes 524288 | tf_op jit(solution)/shard_map/all_to_all | solution.py:21
  208.9 4.2 %copy-start.1 = (f32[512,112]{0,1:T(8,128)S(1)}, f32[512,112]{0,1:T(8,128)}, u32[]{:S(2)}) copy-start(f32[512,112]{0,1:T(8,128)} %fusion.22) | copy-start | bytes 688132
  209.5 15.3 %all-to-all-start.10 = ((bf16[8,14,256]{2,1,0:T(8,128)(2,1)}), bf16[8,14,256]{2,1,0:T(8,128)(2,1)S(1)}, u32[]{:S(2)}, u32[]{:S(2)}) async-start(bf16[8,14,256]{2,1,0:T(8,128)(2,1)} %reshape.159), calls=%async_computation.10 | async-start | bytes 131072 | tf_op jit(solution)/shard_map/all_to_all | solution.py:21
  226.2 16.6 %all-to-all-start.11 = ((bf16[8,32,256]{2,1,0:T(8,128)(2,1)}), bf16[8,32,256]{2,1,0:T(8,128)(2,1)S(1)}, u32[]{:S(2)}, u32[]{:S(2)}) async-start(bf16[8,32,256]{2,1,0:T(8,128)(2,1)} %broadcast_in_dim.101), calls=%async_computation.11 | async-start | bytes 262144 | tf_op jit(solution)/shard_map/all_to_all | solution.py:21

commit v5 on v4

--- a/solution.py
+++ b/solution.py
@@ -1,6 +1,10 @@
+import functools
+
 import jax
 import jax.numpy as jnp
 from jax import lax
+from jax.experimental import pallas as pl
+from jax.experimental.pallas import tpu as pltpu
 from jax.sharding import Mesh
 from jax.sharding import PartitionSpec as P
 
@@ -44,6 +48,28 @@
         v, ones, (((1,), (0,)), ((), ())), precision=lax.Precision.HIGHEST, preferred_element_type=F32
     )
     return both[:, :1]
+
+
+def pack_kernel(ff, *refs):
+    out = refs[-1]
+    for m, ref in enumerate(refs[:-1]):
+        v = ref[...].astype(F32)
+        for e in range(out.shape[0]):
+            out[e, m] = v[:, e * ff : (e + 1) * ff].astype(BF)
+
+
+def pack(mats, parts):
+    rows, columns = mats[0].shape
+    ff = columns // parts
+    shape = (parts, len(mats), rows, ff)
+    return pl.pallas_call(
+        functools.partial(pack_kernel, ff),
+        out_shape=jax.ShapeDtypeStruct(shape, BF),
+        in_specs=[pl.BlockSpec(memory_space=pltpu.VMEM)] * len(mats),
+        out_specs=pl.BlockSpec(memory_space=pltpu.VMEM),
+        compiler_params=pltpu.CompilerParams(vmem_limit_bytes=16 << 20),
+        cost_estimate=pl.CostEstimate(flops=0, bytes_accessed=2 << 20, transcendentals=0),
+    )(*mats)
 
 
 def make_body(nz, nl, nx, ny, nc):
@@ -61,23 +87,15 @@
         rows = dz // nr
         count = 3.0 * (dz * nz) * (ff_dev * nt)
 
-        chosen = pool.at[picks].get(mode="promise_in_bounds")
+        picked = pool.at[picks].get(mode="promise_in_bounds")
         swap = [(i * nt + j, j * nz + i) for i in range(nz) for j in range(nt)]
-        chosen = lax.ppermute(chosen, ("zh", "y", "core"), swap)
+        chosen = lax.ppermute(picked, ("zh", "y", "core"), swap)
         targets = targets.reshape(nz, nx, tok_dev, d_dev).transpose(1, 0, 2, 3)
         targets = targets.reshape(tokens, d_dev)
 
-        mats = jnp.stack(
-            [
-                gate_w,
-                up_w,
-                probe_g.astype(BF),
-                probe_u.astype(BF),
-                down_w.T,
-                probe_d.T.astype(BF),
-            ]
-        )
-        mats = mats.reshape(6, d_dev, nx, ff).transpose(2, 0, 1, 3)
+        mats = (gate_w, up_w, probe_g, probe_u, down_w.T, probe_d.T)
+        picked, mats = lax.optimization_barrier((picked, mats))
+        mats = pack(mats, nx)
         mats = exchange(mats, NEAR)
         chosen, mats = lax.optimization_barrier((chosen, mats))
         mats = mats.transpose(1, 0, 2, 3).reshape(6, dz, ff)
@@ -205,11 +223,14 @@
         hv.append(jnp.broadcast_to(sums[None], (nx,) + sums.shape))
         got = exchange(jnp.concatenate(hv, axis=1), NEAR)
         sums = jnp.sum(got[:, 3 * d_dev :].astype(F32), axis=0)
+        hv = got[:, : 3 * d_dev, :ff].reshape(nx, 3, d_dev, ff)
+        hv = hv.transpose(1, 2, 0, 3).reshape(3, d_dev, ff_dev)
         sums = jnp.sum(gather(sums[:2] + sums[2:], ("y", "core"), nt), axis=0)
-        scale = 1.0 / jnp.sqrt(total(sums[1:]) / count + 1e-6)
-        hv = got[:, : 3 * d_dev, :ff].reshape(nx, 3, d_dev, ff)
-        hv = hv.transpose(1, 2, 0, 3).reshape(3, d_dev, ff_dev).astype(F32) * scale
-        return hv[0], hv[1], hv[2].T, jnp.sum(sums[0]) / count
+        hv, sums = lax.optimization_barrier((hv, sums))
+        sums = total(sums)
+        scale = 1.0 / jnp.sqrt(sums[1:] / count + 1e-6)
+        gate, up, down = (v.astype(F32) * scale for v in hv)
+        return gate, up, down.T, sums[0, 0] / count
 
     return body
 

time: 273 us -> 274 us (level)
  blocking collectives: 95.1 us -> 82.4 us
  starting transfers between devices: 62.7 us -> 70.3 us
  waiting for transfers between devices: 84.5 us -> 89.4 us
    all_to_all x6 -> x5, blocking collectives: 95.1 us -> 82.4 us  [exchange(): return lax.all_to_all(v, axes, split_axis=0, concat_axis=0, tiled=True)]
    all_to_all x8 -> x9, starting transfers between devices: 57 us -> 64.6 us  [exchange(): return lax.all_to_all(v, axes, split_axis=0, concat_axis=0, tiled=True)]
    all_to_all x8 -> x9, waiting for transfers between devices: 83.2 us -> 88.2 us  [exchange(): return lax.all_to_all(v, axes, split_axis=0, concat_axis=0, tiled=True)]
    unnamed x25 -> x20, local copies, waits for them, and re-layouts: 2.43 us -> 6.17 us
  transfers between devices with their start and end apart: 9 -> 10, of which waited for: 9 -> 10; matrix products, arithmetic and copies ran while one was open for 1% -> 1% of each run, Pallas kernels for 0% -> 0%
where the time goes in v5:
time: 274 us; the launch traced here: 273 us
  waiting for transfers between devices  89.4 us (33%)
  blocking collectives  82.4 us (30%)
  starting transfers between devices  70.3 us (26%)
  local copies, waits for them, and re-layouts  14.7 us (5%)
  matrix products  6.2 us (2%)
  between operations  4.39 us (2%)
  other arithmetic  3.82 us (1%)
    all_to_all x9, waiting for transfers between devices, exchange(): return lax.all_to_all(v, axes, split_axis=0, concat_axis=0, tiled=True)  88.2 us
    all_to_all x5, blocking collectives, exchange(): return lax.all_to_all(v, axes, split_axis=0, concat_axis=0, tiled=True)  82.4 us
    all_to_all x9, starting transfers between devices, exchange(): return lax.all_to_all(v, axes, split_axis=0, concat_axis=0, tiled=True)  64.6 us
    unnamed x20, local copies, waits for them, and re-layouts  6.17 us
    ppermute x1, starting transfers between devices, body(): chosen = lax.ppermute(picked, ('zh', 'y', 'core'), swap)  5.73 us
  transfers between devices with their start and end apart: 10, of which 10 were waited for; matrix products, arithmetic and copies ran while one was open for 1% of the time, Pallas kernels for 0%

profile of v5, /device:TPU:1, one launch (start us, length us, event | category | flops | bytes accessed | tf_op | source)
XLA Modules:
  0.0 272.6 jit_solution(5159297865600362199)
XLA Ops:
  2.5 0.9 copy-done.1
  3.4 0.9 copy-done.2
  4.3 0.9 copy-done.3
  5.3 0.9 copy-done.4
  6.2 0.9 copy-done.5
  8.0 1.3 shard_map.120
  9.3 6.2 %all-to-all-start = ((bf16[8,6,64,112]{3,2,1,0:T(8,128)(2,1)}), bf16[8,6,64,112]{3,2,1,0:T(8,128)(2,1)S(1)}, u32[]{:S(2)}, u32[]{:S(2)}) async-start(bf16[8,6,64,112]{3,2,1,0:T(8,128)(2,1)} %shard_map.120), calls=%async_computation | async-start | bytes 1572864 | tf_op jit(solution)/shard_map/all_to_all | solution.py:25
  15.5 5.7 %collective-permute-start = (bf16[4,512]{1,0:T(4,128)(2,1)S(1)}, bf16[4,512]{1,0:T(4,128)(2,1)S(1)}, u32[]{:S(2)}, u32[]{:S(2)}) collective-permute-start(bf16[4,512]{1,0:T(4,128)(2,1)S(1)} %gather_fusion), channel_id=1, source_target_pairs={{0,0},{1,64},{2,128},{3,192},{4,256},{5,320},{6,384},{7,448},{64,1... | collective-permute-start | bytes 12296 | tf_op jit(solution)/shard_map/ppermute | solution.py:92
  21.2 1.3 collective-permute-done
  22.5 1.3 all-to-all-done
  24.6 23.1 %all-to-all-start.1 = ((bf16[64,4,512]{2,1,0:T(4,128)(2,1)}), bf16[64,4,512]{2,1,0:T(4,128)(2,1)S(1)}, u32[]{:S(2)}, u32[]{:S(2)}) async-start(bf16[64,4,512]{2,1,0:T(4,128)(2,1)} %broadcast_in_dim.37), calls=%async_computation.1 | async-start | bytes 524288 | tf_op jit(solution)/shard_map/all_to_all | solution.py:25
  47.8 9.6 %all-to-all-done.1 = bf16[64,4,512]{2,1,0:T(4,128)(2,1)S(1)} async-done(((bf16[64,4,512]{2,1,0:T(4,128)(2,1)}), bf16[64,4,512]{2,1,0:T(4,128)(2,1)S(1)}, u32[]{:S(2)}, u32[]{:S(2)}) %all-to-all-start.1) | async-done | bytes 262176 | tf_op jit(solution)/shard_map/all_to_all | solution.py:25
  58.4 23.9 %all_to_all.70 = bf16[8,64,256]{2,1,0:T(8,128)(2,1)S(1)} all-to-all(bf16[8,64,256]{2,1,0:T(8,128)(2,1)S(1)} %copy.122), channel_id=1, replica_groups=mesh['zh'=8,'zl'=2,'x'=4,'y'=4,'core'=2] {'zh'}, dimensions={0} | all-to-all | bytes 524288 | tf_op jit(solution)/shard_map/all_to_all | solution.py:25
  83.1 6.2 %all-to-all-start.3 = ((bf16[8,28,256]{2,1,0:T(8,128)(2,1)}), bf16[8,28,256]{2,1,0:T(8,128)(2,1)S(1)}, u32[]{:S(2)}, u32[]{:S(2)}) async-start(bf16[8,28,256]{2,1,0:T(8,128)(2,1)} %broadcast_in_dim.39), calls=%async_computation.3 | async-start | bytes 262144 | tf_op jit(solution)/shard_map/all_to_all | solution.py:25
  89.3 14.0 %all-to-all-done.3 = bf16[8,28,256]{2,1,0:T(8,128)(2,1)S(1)} async-done(((bf16[8,28,256]{2,1,0:T(8,128)(2,1)}), bf16[8,28,256]{2,1,0:T(8,128)(2,1)S(1)}, u32[]{:S(2)}, u32[]{:S(2)}) %all-to-all-start.3) | async-done | bytes 114720 | tf_op jit(solution)/shard_map/all_to_all | solution.py:25
  104.8 6.6 %all-to-all-start.4 = ((bf16[64,2,8,256]{3,2,1,0:T(8,128)(2,1)}), bf16[64,2,8,256]{3,2,1,0:T(8,128)(2,1)S(1)}, u32[]{:S(2)}, u32[]{:S(2)}) async-start(bf16[64,2,8,256]{3,2,1,0:T(8,128)(2,1)} %maximum_bitcast_fusion), calls=%async_computation.4 | async-start | bytes 1048576 | tf_op jit(solution)/shard_map/all_to_all | solution.py:25
  111.7 12.0 %all-to-all-done.4 = bf16[64,2,8,256]{3,2,1,0:T(8,128)(2,1)S(1)} async-done(((bf16[64,2,8,256]{3,2,1,0:T(8,128)(2,1)}), bf16[64,2,8,256]{3,2,1,0:T(8,128)(2,1)S(1)}, u32[]{:S(2)}, u32[]{:S(2)}) %all-to-all-start.4) | async-done | bytes 524320 | tf_op jit(solution)/shard_map/all_to_all | solution.py:25
  123.9 19.0 %all_to_all.71 = bf16[64,24,256]{2,1,0:T(8,128)(2,1)S(1)} all-to-all(bf16[64,24,256]{2,1,0:T(8,128)(2,1)S(1)} %broadcast_in_dim.40), channel_id=1, replica_groups=mesh['zh'=8,'zl'=2,'x'=4,'y'=4,'core'=2] {'zl','x','y','core'}, dimensions={0} | all-to-all | bytes 1572864 | tf_op jit(solution)/shard_map/all_to_all | solution.py:25
  144.4 3.4 %all-to-all-start.6 = ((bf16[8,2,14,256]{3,1,2,0:T(2,128)(2,1)}), bf16[8,2,14,256]{3,1,2,0:T(2,128)(2,1)S(1)}, u32[]{:S(2)}, u32[]{:S(2)}) async-start(bf16[8,2,14,256]{3,1,2,0:T(2,128)(2,1)} %copy.129), calls=%async_computation.6 | async-start | bytes 229376 | tf_op jit(solution)/shard_map/all_to_all | solution.py:25
  148.5 14.9 %all-to-all-done.6 = bf16[8,2,14,256]{3,1,2,0:T(2,128)(2,1)S(1)} async-done(((bf16[8,2,14,256]{3,1,2,0:T(2,128)(2,1)}), bf16[8,2,14,256]{3,1,2,0:T(2,128)(2,1)S(1)}, u32[]{:S(2)}, u32[]{:S(2)}) %all-to-all-start.6) | async-done | bytes 114720 | tf_op jit(solution)/shard_map/all_to_all | solution.py:25
  164.0 14.6 %all_to_all.72 = bf16[8,16,256]{2,1,0:T(8,128)(2,1)S(1)} all-to-all(bf16[8,16,256]{2,1,0:T(8,128)(2,1)S(1)} %broadcast_in_dim.43), channel_id=1, replica_groups=mesh['zh'=8,'zl'=2,'x'=4,'y'=4,'core'=2] {'zh'}, dimensions={0} | all-to-all | bytes 131072 | tf_op jit(solution)/shard_map/all_to_all | solution.py:25
  179.8 15.6 %all_to_all.73 = bf16[64,9,2,128]{3,2,1,0:T(2,128)(2,1)S(1)} all-to-all(bf16[64,9,2,128]{3,2,1,0:T(2,128)(2,1)S(1)} %pad_maximum_fusion), channel_id=1, replica_groups=mesh['zh'=8,'zl'=2,'x'=4,'y'=4,'core'=2] {'zl','x','y','core'}, dimensions={0} | all-to-all | bytes 589824 | tf_op jit(solution)/shard_map/all_to_all | solution.py:25
  196.4 4.4 %all-to-all-start.9 = ((bf16[64,8,256]{2,1,0:T(8,128)(2,1)}), bf16[64,8,256]{2,1,0:T(8,128)(2,1)S(1)}, u32[]{:S(2)}, u32[]{:S(2)}) async-start(bf16[64,8,256]{2,1,0:T(8,128)(2,1)} %broadcast_in_dim.46), calls=%async_computation.9 | async-start | bytes 524288 | tf_op jit(solution)/shard_map/all_to_all | solution.py:25
  200.9 0.9 fusion.22
  203.2 7.5 %all-to-all-done.9 = bf16[64,8,256]{2,1,0:T(8,128)(2,1)S(1)} async-done(((bf16[64,8,256]{2,1,0:T(8,128)(2,1)}), bf16[64,8,256]{2,1,0:T(8,128)(2,1)S(1)}, u32[]{:S(2)}, u32[]{:S(2)}) %all-to-all-start.9) | async-done | bytes 262176 | tf_op jit(solution)/shard_map/all_to_all | solution.py:25
  211.8 3.4 %all-to-all-start.10 = ((bf16[8,14,256]{2,1,0:T(8,128)(2,1)}), bf16[8,14,256]{2,1,0:T(8,128)(2,1)S(1)}, u32[]{:S(2)}, u32[]{:S(2)}) async-start(bf16[8,14,256]{2,1,0:T(8,128)(2,1)} %reshape.144), calls=%async_computation.10 | async-start | bytes 131072 | tf_op jit(solution)/shard_map/all_to_all | solution.py:25
  215.5 11.5 %all-to-all-done.10 = bf16[8,14,256]{2,1,0:T(8,128)(2,1)S(1)} async-done(((bf16[8,14,256]{2,1,0:T(8,128)(2,1)}), bf16[8,14,256]{2,1,0:T(8,128)(2,1)S(1)}, u32[]{:S(2)}, u32[]{:S(2)}) %all-to-all-start.10) | async-done | bytes 57376 | tf_op jit(solution)/shard_map/all_to_all | solution.py:25
  228.3 3.4 %all-to-all-start.11 = ((bf16[8,32,256]{2,1,0:T(8,128)(2,1)}), bf16[8,32,256]{2,1,0:T(8,128)(2,1)S(1)}, u32[]{:S(2)}, u32[]{:S(2)}) async-start(bf16[8,32,256]{2,1,0:T(8,128)(2,1)} %broadcast_in_dim.100), calls=%async_computation.11 | async-start | bytes 262144 | tf_op jit(solution)/shard_map/all_to_all | solution.py:25
  231.8 13.3 %all-to-all-done.11 = bf16[8,32,256]{2,1,0:T(8,128)(2,1)S(1)} async-done(((bf16[8,32,256]{2,1,0:T(8,128)(2,1)}), bf16[8,32,256]{2,1,0:T(8,128)(2,1)S(1)}, u32[]{:S(2)}, u32[]{:S(2)}) %all-to-all-start.11) | async-done | bytes 131104 | tf_op jit(solution)/shard_map/all_to_all | solution.py:25
  246.0 9.3 %all_to_all.74 = bf16[8,196,128]{2,1,0:T(8,128)(2,1)S(1)} all-to-all(bf16[8,196,128]{2,1,0:T(8,128)(2,1)S(1)} %fusion.16), channel_id=1, replica_groups=mesh['zh'=8,'zl'=2,'x'=4,'y'=4,'core'=2] {'zl','x'}, dimensions={0} | all-to-all | bytes 802816 | tf_op jit(solution)/shard_map/all_to_all | solution.py:25
  256.0 8.0 %all-to-all-start.13 = ((f32[8,2,128]{2,1,0:T(2,128)}), f32[8,2,128]{2,1,0:T(2,128)S(1)}, u32[]{:S(2)}, u32[]{:S(2)}) async-start(f32[8,2,128]{2,1,0:T(2,128)} %broadcast_in_dim.102), calls=%async_computation.13 | async-start | bytes 16384 | tf_op jit(solution)/shard_map/all_to_all | solution.py:25
  264.6 4.0 %all-to-all-done.13 = f32[8,2,128]{2,1,0:T(2,128)S(1)} async-done(((f32[8,2,128]{2,1,0:T(2,128)}), f32[8,2,128]{2,1,0:T(2,128)S(1)}, u32[]{:S(2)}, u32[]{:S(2)}) %all-to-all-start.13) | async-done | bytes 8224 | tf_op jit(solution)/shard_map/all_to_all | solution.py:25
  (125 shorter events, 19.2 us)
Async XLA Ops:
  0.6 1.2 copy-start
  2.4 0.9 copy-start.1
  3.4 0.9 copy-start.2
  4.3 0.9 copy-start.3
  5.3 0.9 copy-start.4
  6.2 0.9 copy-start.5
  7.1 0.9 copy-start.6
  9.3 14.5 %all-to-all-start = ((bf16[8,6,64,112]{3,2,1,0:T(8,128)(2,1)}), bf16[8,6,64,112]{3,2,1,0:T(8,128)(2,1)S(1)}, u32[]{:S(2)}, u32[]{:S(2)}) async-start(bf16[8,6,64,112]{3,2,1,0:T(8,128)(2,1)} %shard_map.120), calls=%async_computation | async-start | bytes 1572864 | tf_op jit(solution)/shard_map/all_to_all | solution.py:25
  15.5 7.0 %collective-permute-start = (bf16[4,512]{1,0:T(4,128)(2,1)S(1)}, bf16[4,512]{1,0:T(4,128)(2,1)S(1)}, u32[]{:S(2)}, u32[]{:S(2)}) collective-permute-start(bf16[4,512]{1,0:T(4,128)(2,1)S(1)} %gather_fusion), channel_id=1, source_target_pairs={{0,0},{1,64},{2,128},{3,192},{4,256},{5,320},{6,384},{7,448},{64,1... | collective-permute-start | bytes 12296 | tf_op jit(solution)/shard_map/ppermute | solution.py:92
  24.6 32.9 %all-to-all-start.1 = ((bf16[64,4,512]{2,1,0:T(4,128)(2,1)}), bf16[64,4,512]{2,1,0:T(4,128)(2,1)S(1)}, u32[]{:S(2)}, u32[]{:S(2)}) async-start(bf16[64,4,512]{2,1,0:T(4,128)(2,1)} %broadcast_in_dim.37), calls=%async_computation.1 | async-start | bytes 524288 | tf_op jit(solution)/shard_map/all_to_all | solution.py:25
  83.1 20.2 %all-to-all-start.3 = ((bf16[8,28,256]{2,1,0:T(8,128)(2,1)}), bf16[8,28,256]{2,1,0:T(8,128)(2,1)S(1)}, u32[]{:S(2)}, u32[]{:S(2)}) async-start(bf16[8,28,256]{2,1,0:T(8,128)(2,1)} %broadcast_in_dim.39), calls=%async_computation.3 | async-start | bytes 262144 | tf_op jit(solution)/shard_map/all_to_all | solution.py:25
  104.8 6.6 %copy-start.8 = (bf16[256,64]{0,1:T(8,128)(2,1)S(1)}, bf16[256,64]{0,1:T(8,128)(2,1)}, u32[]{:S(2)}) copy-start(bf16[256,64]{0,1:T(8,128)(2,1)} %param.11) | copy-start | bytes 98308
  104.8 18.9 %all-to-all-start.4 = ((bf16[64,2,8,256]{3,2,1,0:T(8,128)(2,1)}), bf16[64,2,8,256]{3,2,1,0:T(8,128)(2,1)S(1)}, u32[]{:S(2)}, u32[]{:S(2)}) async-start(bf16[64,2,8,256]{3,2,1,0:T(8,128)(2,1)} %maximum_bitcast_fusion), calls=%async_computation.4 | async-start | bytes 1048576 | tf_op jit(solution)/shard_map/all_to_all | solution.py:25
  144.4 19.0 %all-to-all-start.6 = ((bf16[8,2,14,256]{3,1,2,0:T(2,128)(2,1)}), bf16[8,2,14,256]{3,1,2,0:T(2,128)(2,1)S(1)}, u32[]{:S(2)}, u32[]{:S(2)}) async-start(bf16[8,2,14,256]{3,1,2,0:T(2,128)(2,1)} %copy.129), calls=%async_computation.6 | async-start | bytes 229376 | tf_op jit(solution)/shard_map/all_to_all | solution.py:25
  196.4 14.3 %all-to-all-start.9 = ((bf16[64,8,256]{2,1,0:T(8,128)(2,1)}), bf16[64,8,256]{2,1,0:T(8,128)(2,1)S(1)}, u32[]{:S(2)}, u32[]{:S(2)}) async-start(bf16[64,8,256]{2,1,0:T(8,128)(2,1)} %broadcast_in_dim.46), calls=%async_computation.9 | async-start | bytes 524288 | tf_op jit(solution)/shard_map/all_to_all | solution.py:25
  211.2 4.0 %copy-start.7 = (f32[512,112]{0,1:T(8,128)S(1)}, f32[512,112]{0,1:T(8,128)}, u32[]{:S(2)}) copy-start(f32[512,112]{0,1:T(8,128)} %fusion.22) | copy-start | bytes 688132
  211.8 15.2 %all-to-all-start.10 = ((bf16[8,14,256]{2,1,0:T(8,128)(2,1)}), bf16[8,14,256]{2,1,0:T(8,128)(2,1)S(1)}, u32[]{:S(2)}, u32[]{:S(2)}) async-start(bf16[8,14,256]{2,1,0:T(8,128)(2,1)} %reshape.144), calls=%async_computation.10 | async-start | bytes 131072 | tf_op jit(solution)/shard_map/all_to_all | solution.py:25
  228.3 16.8 %all-to-all-start.11 = ((bf16[8,32,256]{2,1,0:T(8,128)(2,1)}), bf16[8,32,256]{2,1,0:T(8,128)(2,1)S(1)}, u32[]{:S(2)}, u32[]{:S(2)}) async-start(bf16[8,32,256]{2,1,0:T(8,128)(2,1)} %broadcast_in_dim.100), calls=%async_computation.11 | async-start | bytes 262144 | tf_op jit(solution)/shard_map/all_to_all | solution.py:25
  256.0 12.6 %all-to-all-start.13 = ((f32[8,2,128]{2,1,0:T(2,128)}), f32[8,2,128]{2,1,0:T(2,128)S(1)}, u32[]{:S(2)}, u32[]{:S(2)}) async-start(f32[8,2,128]{2,1,0:T(2,128)} %broadcast_in_dim.102), calls=%async_computation.13 | async-start | bytes 16384 | tf_op jit(solution)/shard_map/all_to_all | solution.py:25

commit v6 on v5

--- a/solution.py
+++ b/solution.py
@@ -43,17 +43,26 @@
 
 
 def total(v):
-    ones = jnp.ones((v.shape[1], 128), F32)
-    both = lax.dot_general(
+    ones = jnp.ones((v.shape[1], LANES), F32)
+    return lax.dot_general(
         v, ones, (((1,), (0,)), ((), ())), precision=lax.Precision.HIGHEST, preferred_element_type=F32
     )
-    return both[:, :1]
-
-
-def pack_kernel(ff, *refs):
-    out = refs[-1]
-    for m, ref in enumerate(refs[:-1]):
-        v = ref[...].astype(F32)
+
+
+def across(row, columns):
+    return jnp.concatenate([row] * pl.cdiv(columns, LANES), axis=1)[:, :columns]
+
+
+def pack_kernel(ff, count, *refs):
+    mats, out, held, sem = refs[:count], refs[count], refs[count + 1 : -1], refs[-1]
+    copies = [
+        pltpu.make_async_copy(mats[m], held[m], sem.at[m]) for m in range(count)
+    ]
+    for copy in copies:
+        copy.start()
+    for m, copy in enumerate(copies):
+        copy.wait()
+        v = held[m][...].astype(F32)
         for e in range(out.shape[0]):
             out[e, m] = v[:, e * ff : (e + 1) * ff].astype(BF)
 
@@ -63,11 +72,13 @@
     ff = columns // parts
     shape = (parts, len(mats), rows, ff)
     return pl.pallas_call(
-        functools.partial(pack_kernel, ff),
+        functools.partial(pack_kernel, ff, len(mats)),
         out_shape=jax.ShapeDtypeStruct(shape, BF),
-        in_specs=[pl.BlockSpec(memory_space=pltpu.VMEM)] * len(mats),
+        in_specs=[pl.BlockSpec(memory_space=pl.ANY)] * len(mats),
         out_specs=pl.BlockSpec(memory_space=pltpu.VMEM),
-        compiler_params=pltpu.CompilerParams(vmem_limit_bytes=16 << 20),
+        scratch_shapes=[pltpu.VMEM(m.shape, m.dtype) for m in mats]
+        + [pltpu.SemaphoreType.DMA((len(mats),))],
+        compiler_params=pltpu.CompilerParams(vmem_limit_bytes=56 << 20),
         cost_estimate=pl.CostEstimate(flops=0, bytes_accessed=2 << 20, transcendentals=0),
     )(*mats)
 
@@ -102,6 +113,19 @@
         inputs = gather(chosen, REST, nr).reshape(tokens, dz)
         down, pdown = mats[4], mats[5]
 
+        def to_out(first, second):
+            pair = jnp.concatenate([first, second], axis=1)
+            return lambda h: dot(pair, h, 1, 0).astype(BF)
+
+        def to_back(first, second):
+            pair = jnp.concatenate([first, second], axis=0)
+            return lambda r: dot(pair, r, 0, 0).astype(BF)
+
+        def with_tangent(v, tan):
+            upper = jnp.concatenate([v, tan], axis=1)
+            lower = jnp.concatenate([jnp.zeros_like(v), v], axis=1)
+            return jnp.concatenate([upper, lower], axis=0)
+
         first = lax.dot_general(
             mats[:4], inputs, (((1,), (1,)), ((), ())), preferred_element_type=F32
         )
@@ -127,16 +151,15 @@
         hidden = both[:, :sub].reshape(ff, tokens)
         tan_hidden = both[:, sub:].reshape(ff, tokens)
 
-        out = dot(down, hidden, 1, 0)
-        tan_out = dot(down, tan_hidden, 1, 0) + dot(pdown, hidden, 1, 0)
-        packed = jnp.stack([out.astype(BF), tan_out.astype(BF)])
-        packed = packed.reshape(2, nr, rows, tokens).transpose(1, 0, 2, 3)
+        packed = to_out(down, pdown)(with_tangent(hidden, tan_hidden))
+        packed = packed.reshape(nr, rows, 2 * tokens)
         got = jnp.sum(exchange(packed, REST).astype(F32), axis=0)
+        out, tan_out = got[:, :tokens], got[:, tokens:]
         wanted = lax.dynamic_slice_in_dim(
             targets.T, lax.axis_index(("y", "core")) * rows, rows, 0
         )
-        resid = ((got[0] - wanted.astype(F32)) / tokens).astype(BF)
-        tan_resid = (got[1] / tokens).astype(BF)
+        resid = ((out - wanted.astype(F32)) / tokens).astype(BF)
+        tan_resid = (tan_out / tokens).astype(BF)
         packed = jnp.concatenate([resid, tan_resid, *two_terms(gram)])
         both = gather(packed, REST, nr)
         resid = both[:, :rows].reshape(dz, tokens)
@@ -147,12 +170,10 @@
         def by_gram(v):
             return dot(v, gram_hi, 1, 0) + dot(v, gram_lo, 1, 0)
 
-        back = dot(down, resid, 0, 0)
-        tan_back = dot(down, tan_resid, 0, 0) + dot(pdown, resid, 0, 0)
-        packed = jnp.stack([back.astype(BF), tan_back.astype(BF)])
-        packed = packed.reshape(2, nz, sub, tokens).transpose(1, 0, 2, 3)
+        packed = to_back(down, pdown)(with_tangent(resid, tan_resid))
+        packed = packed.reshape(nz, sub, 2 * tokens)
         got = jnp.sum(exchange(packed, "zh").astype(F32), axis=0)
-        back, tan_back = got[0], got[1]
+        back, tan_back = got[:, :tokens], got[:, tokens:]
         hv_down = dot(resid, tan_hidden, 1, 1) + dot(tan_resid, hidden, 1, 1)
 
         def deltas(tan_back, tan_gate, tan_upper):
@@ -180,8 +201,8 @@
         square = jnp.sum(both[:, sub:].astype(F32), axis=(0, 1))[None]
 
         hv_down_b = hv_down.astype(BF)
-        tan_out = dot(down, tan_hidden, 1, 0) + dot(hv_down_b, hidden, 1, 0)
-        packed = tan_out.astype(BF).reshape(nr, rows, 2, tokens // 2)
+        packed = to_out(down, hv_down_b)(jnp.concatenate([tan_hidden, hidden]))
+        packed = packed.reshape(nr, rows, 2, tokens // 2)
         scal = terms(square[:, : tokens // 2] + square[:, tokens // 2 :])
         scal = jnp.broadcast_to(scal[None, None], (nr, 1, 2, tokens // 2))
         got = exchange(jnp.concatenate([packed, scal], axis=1), REST)
@@ -192,15 +213,17 @@
         tan_resid = (got / tokens).astype(BF)
         tan_resid = gather(tan_resid, REST, nr).reshape(dz, tokens)
 
-        tan_back = dot(down, tan_resid, 0, 0) + dot(hv_down_b, resid, 0, 0)
-        packed = tan_back.astype(BF).reshape(nz, sub, tokens)
+        packed = to_back(down, hv_down_b)(jnp.concatenate([tan_resid, resid]))
+        packed = packed.reshape(nz, sub, tokens)
         tan_back = jnp.sum(exchange(packed, "zh").astype(F32), axis=0)
-        hv_down2 = (dot(resid, tan_hidden, 1, 1) + dot(tan_resid, hidden, 1, 1)) * scale
-
-        tangents = tangents * scale
-        delta = deltas(tan_back * scale, tangents[:sub], tangents[sub:])
+        hv_down2 = (dot(resid, tan_hidden, 1, 1) + dot(tan_resid, hidden, 1, 1))
+        hv_down2 = hv_down2 * across(scale, ff)
+        wide_scale = across(scale, tokens)
+
+        tangents = tangents * wide_scale
+        delta = deltas(tan_back * wide_scale, tangents[:sub], tangents[sub:])
         wide = delta.astype(F32)
-        inner = lanes(tangents * wide) + lanes((hv_down * scale) * hv_down2)
+        inner = lanes(tangents * wide) + lanes((hv_down * across(scale, ff)) * hv_down2)
         square = lanes(by_gram(delta) * wide) + lanes(hv_down2 * hv_down2)
         both = gather(jnp.concatenate([delta, terms(inner, square)]), "zh", nz)
         delta_gate = both[:, :sub].reshape(ff, tokens)
@@ -228,7 +251,7 @@
         sums = jnp.sum(gather(sums[:2] + sums[2:], ("y", "core"), nt), axis=0)
         hv, sums = lax.optimization_barrier((hv, sums))
         sums = total(sums)
-        scale = 1.0 / jnp.sqrt(sums[1:] / count + 1e-6)
+        scale = across(1.0 / jnp.sqrt(sums[1:] / count + 1e-6), ff_dev)
         gate, up, down = (v.astype(F32) * scale for v in hv)
         return gate, up, down.T, sums[0, 0] / count
 

time: 274 us -> 271 us (0.989)
  blocking collectives: 82.4 us -> 68.2 us
  waiting for transfers between devices: 89.4 us -> 103 us
  local copies, waits for them, and re-layouts: 14.7 us -> 9.68 us
  starting transfers between devices: 70.3 us -> 73.6 us
    all_to_all x5 -> x4, blocking collectives: 82.4 us -> 68.2 us  [exchange(): return lax.all_to_all(v, axes, split_axis=0, concat_axis=0, tiled=True)]
    all_to_all x9 -> x10, waiting for transfers between devices: 88.2 us -> 102 us  [exchange(): return lax.all_to_all(v, axes, split_axis=0, concat_axis=0, tiled=True)]
    unnamed x20 -> x19, local copies, waits for them, and re-layouts: 6.17 us -> 0.7 us
    all_to_all x9 -> x10, starting transfers between devices: 64.6 us -> 67.8 us  [exchange(): return lax.all_to_all(v, axes, split_axis=0, concat_axis=0, tiled=True)]
    dot_general x21 -> x15, matrix products: 5.06 us -> 6.06 us  [dot(): lax.dot_general(a, b, (((ca,), (cb,)), ((), ())), preferred_element_type=...]
  transfers between devices with their start and end apart: 10 -> 11, of which waited for: 10 -> 11; matrix products, arithmetic and copies ran while one was open for 1% -> 1% of each run, Pallas kernels for 0% -> 0%
where the time goes in v6:
time: 271 us; the launch traced here: 270 us
  waiting for transfers between devices  103 us (38%)
  starting transfers between devices  73.6 us (27%)
  blocking collectives  68.2 us (25%)
  local copies, waits for them, and re-layouts  9.68 us (4%)
  matrix products  6.66 us (2%)
  other arithmetic  3.18 us (1%)
  between operations  3.05 us (1%)
    all_to_all x10, waiting for transfers between devices, exchange(): return lax.all_to_all(v, axes, split_axis=0, concat_axis=0, tiled=True)  102 us
    all_to_all x4, blocking collectives, exchange(): return lax.all_to_all(v, axes, split_axis=0, concat_axis=0, tiled=True)  68.2 us
    all_to_all x10, starting transfers between devices, exchange(): return lax.all_to_all(v, axes, split_axis=0, concat_axis=0, tiled=True)  67.8 us
    dot_general x15, matrix products, dot(): lax.dot_general(a, b, (((ca,), (cb,)), ((), ())), preferred_element_type=...  6.06 us
    ppermute x1, starting transfers between devices, body(): chosen = lax.ppermute(picked, ('zh', 'y', 'core'), swap)  5.73 us
  transfers between devices with their start and end apart: 11, of which 11 were waited for; matrix products, arithmetic and copies ran while one was open for 1% of the time, Pallas kernels for 0%

profile of v6, /device:TPU:1, one launch (start us, length us, event | category | flops | bytes accessed | tf_op | source)
XLA Modules:
  0.0 269.9 jit_solution(11710723732420272431)
XLA Ops:
  2.4 2.6 shard_map.120
  5.0 6.2 %all-to-all-start = ((bf16[8,6,64,112]{3,2,1,0:T(8,128)(2,1)}), bf16[8,6,64,112]{3,2,1,0:T(8,128)(2,1)S(1)}, u32[]{:S(2)}, u32[]{:S(2)}) async-start(bf16[8,6,64,112]{3,2,1,0:T(8,128)(2,1)} %shard_map.120), calls=%async_computation | async-start | bytes 1572864 | tf_op jit(solution)/shard_map/all_to_all | solution.py:25
  11.3 5.7 %collective-permute-start = (bf16[4,512]{1,0:T(4,128)(2,1)S(1)}, bf16[4,512]{1,0:T(4,128)(2,1)S(1)}, u32[]{:S(2)}, u32[]{:S(2)}) collective-permute-start(bf16[4,512]{1,0:T(4,128)(2,1)S(1)} %gather_fusion), channel_id=1, source_target_pairs={{0,0},{1,64},{2,128},{3,192},{4,256},{5,320},{6,384},{7,448},{64,1... | collective-permute-start | bytes 12296 | tf_op jit(solution)/shard_map/ppermute | solution.py:103
  17.0 1.3 collective-permute-done
  18.3 1.3 all-to-all-done
  19.6 0.8 broadcast_in_dim.37
  20.4 23.1 %all-to-all-start.1 = ((bf16[64,4,512]{2,1,0:T(4,128)(2,1)}), bf16[64,4,512]{2,1,0:T(4,128)(2,1)S(1)}, u32[]{:S(2)}, u32[]{:S(2)}) async-start(bf16[64,4,512]{2,1,0:T(4,128)(2,1)} %broadcast_in_dim.37), calls=%async_computation.1 | async-start | bytes 524288 | tf_op jit(solution)/shard_map/all_to_all | solution.py:25
  43.6 9.6 %all-to-all-done.1 = bf16[64,4,512]{2,1,0:T(4,128)(2,1)S(1)} async-done(((bf16[64,4,512]{2,1,0:T(4,128)(2,1)}), bf16[64,4,512]{2,1,0:T(4,128)(2,1)S(1)}, u32[]{:S(2)}, u32[]{:S(2)}) %all-to-all-start.1) | async-done | bytes 262176 | tf_op jit(solution)/shard_map/all_to_all | solution.py:25
  54.2 23.9 %all_to_all.70 = bf16[8,64,256]{2,1,0:T(8,128)(2,1)S(1)} all-to-all(bf16[8,64,256]{2,1,0:T(8,128)(2,1)S(1)} %copy.94), channel_id=1, replica_groups=mesh['zh'=8,'zl'=2,'x'=4,'y'=4,'core'=2] {'zh'}, dimensions={0} | all-to-all | bytes 524288 | tf_op jit(solution)/shard_map/all_to_all | solution.py:25
  78.9 6.2 %all-to-all-start.3 = ((bf16[8,28,256]{2,1,0:T(8,128)(2,1)}), bf16[8,28,256]{2,1,0:T(8,128)(2,1)S(1)}, u32[]{:S(2)}, u32[]{:S(2)}) async-start(bf16[8,28,256]{2,1,0:T(8,128)(2,1)} %broadcast_in_dim.39), calls=%async_computation.3 | async-start | bytes 262144 | tf_op jit(solution)/shard_map/all_to_all | solution.py:25
  85.1 14.0 %all-to-all-done.3 = bf16[8,28,256]{2,1,0:T(8,128)(2,1)S(1)} async-done(((bf16[8,28,256]{2,1,0:T(8,128)(2,1)}), bf16[8,28,256]{2,1,0:T(8,128)(2,1)S(1)}, u32[]{:S(2)}, u32[]{:S(2)}) %all-to-all-start.3) | async-done | bytes 114720 | tf_op jit(solution)/shard_map/all_to_all | solution.py:25
  99.2 1.1 fusion.1
  100.3 6.4 %all-to-all-start.4 = ((bf16[64,8,512]{2,1,0:T(8,128)(2,1)}), bf16[64,8,512]{2,1,0:T(8,128)(2,1)S(1)}, u32[]{:S(2)}, u32[]{:S(2)}) async-start(bf16[64,8,512]{2,1,0:T(8,128)(2,1)} %fusion.1), calls=%async_computation.4 | async-start | bytes 1048576 | tf_op jit(solution)/shard_map/all_to_all | solution.py:25
  107.1 12.0 %all-to-all-done.4 = bf16[64,8,512]{2,1,0:T(8,128)(2,1)S(1)} async-done(((bf16[64,8,512]{2,1,0:T(8,128)(2,1)}), bf16[64,8,512]{2,1,0:T(8,128)(2,1)S(1)}, u32[]{:S(2)}, u32[]{:S(2)}) %all-to-all-start.4) | async-done | bytes 524320 | tf_op jit(solution)/shard_map/all_to_all | solution.py:25
  119.2 19.0 %all_to_all.71 = bf16[64,24,256]{2,1,0:T(8,128)(2,1)S(1)} all-to-all(bf16[64,24,256]{2,1,0:T(8,128)(2,1)S(1)} %broadcast_in_dim.40), channel_id=1, replica_groups=mesh['zh'=8,'zl'=2,'x'=4,'y'=4,'core'=2] {'zl','x','y','core'}, dimensions={0} | all-to-all | bytes 1572864 | tf_op jit(solution)/shard_map/all_to_all | solution.py:25
  139.5 3.4 %all-to-all-start.6 = ((bf16[8,14,512]{2,1,0:T(8,128)(2,1)}), bf16[8,14,512]{2,1,0:T(8,128)(2,1)S(1)}, u32[]{:S(2)}, u32[]{:S(2)}) async-start(bf16[8,14,512]{2,1,0:T(8,128)(2,1)} %reshape.133), calls=%async_computation.6 | async-start | bytes 262144 | tf_op jit(solution)/shard_map/all_to_all | solution.py:25
  143.4 15.5 %all-to-all-done.6 = bf16[8,14,512]{2,1,0:T(8,128)(2,1)S(1)} async-done(((bf16[8,14,512]{2,1,0:T(8,128)(2,1)}), bf16[8,14,512]{2,1,0:T(8,128)(2,1)S(1)}, u32[]{:S(2)}, u32[]{:S(2)}) %all-to-all-start.6) | async-done | bytes 114720 | tf_op jit(solution)/shard_map/all_to_all | solution.py:25
  160.0 3.4 %all-to-all-start.7 = ((bf16[8,16,256]{2,1,0:T(8,128)(2,1)}), bf16[8,16,256]{2,1,0:T(8,128)(2,1)S(1)}, u32[]{:S(2)}, u32[]{:S(2)}) async-start(bf16[8,16,256]{2,1,0:T(8,128)(2,1)} %broadcast_in_dim.43), calls=%async_computation.7 | async-start | bytes 131072 | tf_op jit(solution)/shard_map/all_to_all | solution.py:25
  163.4 11.9 %all-to-all-done.7 = bf16[8,16,256]{2,1,0:T(8,128)(2,1)S(1)} async-done(((bf16[8,16,256]{2,1,0:T(8,128)(2,1)}), bf16[8,16,256]{2,1,0:T(8,128)(2,1)S(1)}, u32[]{:S(2)}, u32[]{:S(2)}) %all-to-all-start.7) | async-done | bytes 65568 | tf_op jit(solution)/shard_map/all_to_all | solution.py:25
  176.4 16.0 %all_to_all.72 = bf16[64,9,2,128]{3,2,1,0:T(2,128)(2,1)S(1)} all-to-all(bf16[64,9,2,128]{3,2,1,0:T(2,128)(2,1)S(1)} %pad_maximum_fusion), channel_id=1, replica_groups=mesh['zh'=8,'zl'=2,'x'=4,'y'=4,'core'=2] {'zl','x','y','core'}, dimensions={0} | all-to-all | bytes 589824 | tf_op jit(solution)/shard_map/all_to_all | solution.py:25
  193.4 4.4 %all-to-all-start.9 = ((bf16[64,8,256]{2,1,0:T(8,128)(2,1)}), bf16[64,8,256]{2,1,0:T(8,128)(2,1)S(1)}, u32[]{:S(2)}, u32[]{:S(2)}) async-start(bf16[64,8,256]{2,1,0:T(8,128)(2,1)} %broadcast_in_dim.46), calls=%async_computation.9 | async-start | bytes 524288 | tf_op jit(solution)/shard_map/all_to_all | solution.py:25
  197.8 1.0 fusion.102
  199.1 8.5 %all-to-all-done.9 = bf16[64,8,256]{2,1,0:T(8,128)(2,1)S(1)} async-done(((bf16[64,8,256]{2,1,0:T(8,128)(2,1)}), bf16[64,8,256]{2,1,0:T(8,128)(2,1)S(1)}, u32[]{:S(2)}, u32[]{:S(2)}) %all-to-all-start.9) | async-done | bytes 262176 | tf_op jit(solution)/shard_map/all_to_all | solution.py:25
  207.7 1.3 convolution_convert_fusion.6
  209.6 3.4 %all-to-all-start.10 = ((bf16[8,14,256]{2,1,0:T(8,128)(2,1)}), bf16[8,14,256]{2,1,0:T(8,128)(2,1)S(1)}, u32[]{:S(2)}, u32[]{:S(2)}) async-start(bf16[8,14,256]{2,1,0:T(8,128)(2,1)} %reshape.139), calls=%async_computation.10 | async-start | bytes 131072 | tf_op jit(solution)/shard_map/all_to_all | solution.py:25
  213.3 11.5 %all-to-all-done.10 = bf16[8,14,256]{2,1,0:T(8,128)(2,1)S(1)} async-done(((bf16[8,14,256]{2,1,0:T(8,128)(2,1)}), bf16[8,14,256]{2,1,0:T(8,128)(2,1)S(1)}, u32[]{:S(2)}, u32[]{:S(2)}) %all-to-all-start.10) | async-done | bytes 57376 | tf_op jit(solution)/shard_map/all_to_all | solution.py:25
  226.1 3.4 %all-to-all-start.11 = ((bf16[8,32,256]{2,1,0:T(8,128)(2,1)}), bf16[8,32,256]{2,1,0:T(8,128)(2,1)S(1)}, u32[]{:S(2)}, u32[]{:S(2)}) async-start(bf16[8,32,256]{2,1,0:T(8,128)(2,1)} %broadcast_in_dim.102), calls=%async_computation.11 | async-start | bytes 262144 | tf_op jit(solution)/shard_map/all_to_all | solution.py:25
  229.6 13.3 %all-to-all-done.11 = bf16[8,32,256]{2,1,0:T(8,128)(2,1)S(1)} async-done(((bf16[8,32,256]{2,1,0:T(8,128)(2,1)}), bf16[8,32,256]{2,1,0:T(8,128)(2,1)S(1)}, u32[]{:S(2)}, u32[]{:S(2)}) %all-to-all-start.11) | async-done | bytes 131104 | tf_op jit(solution)/shard_map/all_to_all | solution.py:25
  243.8 9.3 %all_to_all.73 = bf16[8,196,128]{2,1,0:T(8,128)(2,1)S(1)} all-to-all(bf16[8,196,128]{2,1,0:T(8,128)(2,1)S(1)} %fusion.28), channel_id=1, replica_groups=mesh['zh'=8,'zl'=2,'x'=4,'y'=4,'core'=2] {'zl','x'}, dimensions={0} | all-to-all | bytes 802816 | tf_op jit(solution)/shard_map/all_to_all | solution.py:25
  253.8 8.0 %all-to-all-start.13 = ((f32[8,2,128]{2,1,0:T(2,128)}), f32[8,2,128]{2,1,0:T(2,128)S(1)}, u32[]{:S(2)}, u32[]{:S(2)}) async-start(f32[8,2,128]{2,1,0:T(2,128)} %broadcast_in_dim.104), calls=%async_computation.13 | async-start | bytes 16384 | tf_op jit(solution)/shard_map/all_to_all | solution.py:25
  262.4 4.0 %all-to-all-done.13 = f32[8,2,128]{2,1,0:T(2,128)S(1)} async-done(((f32[8,2,128]{2,1,0:T(2,128)}), f32[8,2,128]{2,1,0:T(2,128)S(1)}, u32[]{:S(2)}, u32[]{:S(2)}) %all-to-all-start.13) | async-done | bytes 8224 | tf_op jit(solution)/shard_map/all_to_all | solution.py:25
  267.9 0.9 fusion.49
  (124 shorter events, 14.4 us)
Async XLA Ops:
  0.6 1.2 copy-start
  5.0 14.5 %all-to-all-start = ((bf16[8,6,64,112]{3,2,1,0:T(8,128)(2,1)}), bf16[8,6,64,112]{3,2,1,0:T(8,128)(2,1)S(1)}, u32[]{:S(2)}, u32[]{:S(2)}) async-start(bf16[8,6,64,112]{3,2,1,0:T(8,128)(2,1)} %shard_map.120), calls=%async_computation | async-start | bytes 1572864 | tf_op jit(solution)/shard_map/all_to_all | solution.py:25
  11.3 7.0 %collective-permute-start = (bf16[4,512]{1,0:T(4,128)(2,1)S(1)}, bf16[4,512]{1,0:T(4,128)(2,1)S(1)}, u32[]{:S(2)}, u32[]{:S(2)}) collective-permute-start(bf16[4,512]{1,0:T(4,128)(2,1)S(1)} %gather_fusion), channel_id=1, source_target_pairs={{0,0},{1,64},{2,128},{3,192},{4,256},{5,320},{6,384},{7,448},{64,1... | collective-permute-start | bytes 12296 | tf_op jit(solution)/shard_map/ppermute | solution.py:103
  20.4 32.9 %all-to-all-start.1 = ((bf16[64,4,512]{2,1,0:T(4,128)(2,1)}), bf16[64,4,512]{2,1,0:T(4,128)(2,1)S(1)}, u32[]{:S(2)}, u32[]{:S(2)}) async-start(bf16[64,4,512]{2,1,0:T(4,128)(2,1)} %broadcast_in_dim.37), calls=%async_computation.1 | async-start | bytes 524288 | tf_op jit(solution)/shard_map/all_to_all | solution.py:25
  78.9 20.2 %all-to-all-start.3 = ((bf16[8,28,256]{2,1,0:T(8,128)(2,1)}), bf16[8,28,256]{2,1,0:T(8,128)(2,1)S(1)}, u32[]{:S(2)}, u32[]{:S(2)}) async-start(bf16[8,28,256]{2,1,0:T(8,128)(2,1)} %broadcast_in_dim.39), calls=%async_computation.3 | async-start | bytes 262144 | tf_op jit(solution)/shard_map/all_to_all | solution.py:25
  99.2 7.6 %copy-start.7 = (bf16[256,64]{0,1:T(8,128)(2,1)S(1)}, bf16[256,64]{0,1:T(8,128)(2,1)}, u32[]{:S(2)}) copy-start(bf16[256,64]{0,1:T(8,128)(2,1)} %param.11) | copy-start | bytes 98308
  100.3 18.7 %all-to-all-start.4 = ((bf16[64,8,512]{2,1,0:T(8,128)(2,1)}), bf16[64,8,512]{2,1,0:T(8,128)(2,1)S(1)}, u32[]{:S(2)}, u32[]{:S(2)}) async-start(bf16[64,8,512]{2,1,0:T(8,128)(2,1)} %fusion.1), calls=%async_computation.4 | async-start | bytes 1048576 | tf_op jit(solution)/shard_map/all_to_all | solution.py:25
  138.4 1.0 copy-start.1
  139.5 19.4 %all-to-all-start.6 = ((bf16[8,14,512]{2,1,0:T(8,128)(2,1)}), bf16[8,14,512]{2,1,0:T(8,128)(2,1)S(1)}, u32[]{:S(2)}, u32[]{:S(2)}) async-start(bf16[8,14,512]{2,1,0:T(8,128)(2,1)} %reshape.133), calls=%async_computation.6 | async-start | bytes 262144 | tf_op jit(solution)/shard_map/all_to_all | solution.py:25
  143.4 50.0 %copy-start.5 = (bf16[512,112]{0,1:T(8,128)(2,1)}, bf16[512,112]{0,1:T(8,128)(2,1)S(1)}, u32[]{:S(2)}) copy-start(bf16[512,112]{0,1:T(8,128)(2,1)S(1)} %get-tuple-element.36) | copy-start | bytes 344068
  158.9 16.5 %copy-start.3 = (f32[14,512]{1,0:T(8,128)}, f32[14,512]{1,0:T(8,128)S(1)}, u32[]{:S(2)}) copy-start(f32[14,512]{1,0:T(8,128)S(1)} %convert_reduce_fusion.3) | copy-start | bytes 86020
  160.0 15.4 %all-to-all-start.7 = ((bf16[8,16,256]{2,1,0:T(8,128)(2,1)}), bf16[8,16,256]{2,1,0:T(8,128)(2,1)S(1)}, u32[]{:S(2)}, u32[]{:S(2)}) async-start(bf16[8,16,256]{2,1,0:T(8,128)(2,1)} %broadcast_in_dim.43), calls=%async_computation.7 | async-start | bytes 131072 | tf_op jit(solution)/shard_map/all_to_all | solution.py:25
  163.4 12.0 %copy-start.6 = (bf16[512,112]{0,1:T(8,128)(2,1)}, bf16[512,112]{0,1:T(8,128)(2,1)S(1)}, u32[]{:S(2)}) copy-start(bf16[512,112]{0,1:T(8,128)(2,1)S(1)} %copy.98) | copy-start | bytes 344068
  175.4 17.9 %copy-start.2 = (bf16[112,256]{1,0:T(8,128)(2,1)}, bf16[112,256]{1,0:T(8,128)(2,1)S(1)}, u32[]{:S(2)}) copy-start(bf16[112,256]{1,0:T(8,128)(2,1)S(1)} %reshape.136) | copy-start | bytes 172036
  193.4 14.3 %all-to-all-start.9 = ((bf16[64,8,256]{2,1,0:T(8,128)(2,1)}), bf16[64,8,256]{2,1,0:T(8,128)(2,1)S(1)}, u32[]{:S(2)}, u32[]{:S(2)}) async-start(bf16[64,8,256]{2,1,0:T(8,128)(2,1)} %broadcast_in_dim.46), calls=%async_computation.9 | async-start | bytes 524288 | tf_op jit(solution)/shard_map/all_to_all | solution.py:25
  207.7 17.2 %copy-start.4 = (f32[14,512]{1,0:T(8,128)S(1)}, f32[14,512]{1,0:T(8,128)}, u32[]{:S(2)}) copy-start(f32[14,512]{1,0:T(8,128)} %copy-done.3) | copy-start | bytes 86020
  209.6 15.2 %all-to-all-start.10 = ((bf16[8,14,256]{2,1,0:T(8,128)(2,1)}), bf16[8,14,256]{2,1,0:T(8,128)(2,1)S(1)}, u32[]{:S(2)}, u32[]{:S(2)}) async-start(bf16[8,14,256]{2,1,0:T(8,128)(2,1)} %reshape.139), calls=%async_computation.10 | async-start | bytes 131072 | tf_op jit(solution)/shard_map/all_to_all | solution.py:25
  226.1 16.8 %all-to-all-start.11 = ((bf16[8,32,256]{2,1,0:T(8,128)(2,1)}), bf16[8,32,256]{2,1,0:T(8,128)(2,1)S(1)}, u32[]{:S(2)}, u32[]{:S(2)}) async-start(bf16[8,32,256]{2,1,0:T(8,128)(2,1)} %broadcast_in_dim.102), calls=%async_computation.11 | async-start | bytes 262144 | tf_op jit(solution)/shard_map/all_to_all | solution.py:25
  253.8 12.6 %all-to-all-start.13 = ((f32[8,2,128]{2,1,0:T(2,128)}), f32[8,2,128]{2,1,0:T(2,128)S(1)}, u32[]{:S(2)}, u32[]{:S(2)}) async-start(f32[8,2,128]{2,1,0:T(2,128)} %broadcast_in_dim.104), calls=%async_computation.13 | async-start | bytes 16384 | tf_op jit(solution)/shard_map/all_to_all | solution.py:25

commit v7 on v6

v7 whole, which is shorter than its diff:
```python
import functools

import jax
import jax.numpy as jnp
from jax import lax
from jax.experimental import pallas as pl
from jax.experimental.pallas import tpu as pltpu
from jax.sharding import Mesh
from jax.sharding import PartitionSpec as P

AXES = ("zh", "zl", "x", "y", "core")
SIZES = (8, 2, 4, 4, 2)
NEAR = ("zl", "x")
REST = ("zl", "x", "y", "core")
LANES = 128
BF = jnp.bfloat16
F32 = jnp.float32


def dot(a, b, ca, cb):
    return lax.dot_general(a, b, (((ca,), (cb,)), ((), ())), preferred_element_type=F32)


def exchange(v, axes):
    return lax.all_to_all(v, axes, split_axis=0, concat_axis=0, tiled=True)


def alone(v, axes, live):
    v, live = lax.optimization_barrier((v, live))
    return lax.optimization_barrier((exchange(v, axes), live))


def gather(v, axes, n, live):
    return alone(jnp.broadcast_to(v[None], (n,) + v.shape), axes, live)


def two_terms(v):
    high = lax.reduce_precision(v, 8, 7)
    return high.astype(BF), (v - high).astype(BF)


def silu_parts(values):
    s = jax.nn.sigmoid(values)
    activated = values * s
    slope_one = s * (1.0 + values * (1.0 - s))
    slope_two = s * (1.0 - s) * (2.0 + values * (1.0 - 2.0 * s))
    return activated, slope_one, slope_two


def total(v):
    ones = jnp.ones((v.shape[1], LANES), F32)
    return lax.dot_general(
        v, ones, (((1,), (0,)), ((), ())), precision=lax.Precision.HIGHEST, preferred_element_type=F32
    )


def across(row, columns):
    return jnp.concatenate([row] * pl.cdiv(columns, LANES), axis=1)[:, :columns]


def pack_kernel(ff, count, *refs):
    mats, out, held, sem = refs[:count], refs[count], refs[count + 1 : -1], refs[-1]
    copies = [
        pltpu.make_async_copy(mats[m], held[m], sem.at[m]) for m in range(count)
    ]
    for copy in copies:
        copy.start()
    for m, copy in enumerate(copies):
        copy.wait()
        v = held[m][...].astype(F32)
        for e in range(out.shape[0]):
            out[e, m] = v[:, e * ff : (e + 1) * ff].astype(BF)


def pack(mats, parts):
    rows, columns = mats[0].shape
    ff = columns // parts
    shape = (parts, len(mats), rows, ff)
    return pl.pallas_call(
        functools.partial(pack_kernel, ff, len(mats)),
        out_shape=jax.ShapeDtypeStruct(shape, BF),
        in_specs=[pl.BlockSpec(memory_space=pl.ANY)] * len(mats),
        out_specs=pl.BlockSpec(memory_space=pltpu.VMEM),
        scratch_shapes=[pltpu.VMEM(m.shape, m.dtype) for m in mats]
        + [pltpu.SemaphoreType.DMA((len(mats),))],
        compiler_params=pltpu.CompilerParams(vmem_limit_bytes=56 << 20),
        cost_estimate=pl.CostEstimate(flops=0, bytes_accessed=2 << 20, transcendentals=0),
    )(*mats)


def make_body(nz, nl, nx, ny, nc):
    nt = ny * nc
    nx = nl * nx
    nr = nx * nt

    def body(pool, picks, targets, gate_w, up_w, down_w, probe_g, probe_u, probe_d):
        tok_dev = picks.shape[0]
        tokens = targets.shape[0]
        d_dev, ff_dev = gate_w.shape
        ff = ff_dev // nx
        dz = d_dev * nx
        sub = ff // nz
        rows = dz // nr
        count = 3.0 * (dz * nz) * (ff_dev * nt)

        picked = pool.at[picks].get(mode="promise_in_bounds")
        mats = (gate_w, up_w, probe_g, probe_u, down_w.T, probe_d.T)
        picked, mats = lax.optimization_barrier((picked, mats))
        swap = [(i * nt + j, j * nz + i) for i in range(nz) for j in range(nt)]
        chosen = lax.ppermute(picked, ("zh", "y", "core"), swap)
        mats = exchange(pack(mats, nx), NEAR)

        wanted = targets.reshape(nz, nx, tok_dev, d_dev).transpose(1, 0, 2, 3)
        wanted = wanted.reshape(tokens, d_dev).T
        wanted = lax.dynamic_slice_in_dim(
            wanted, lax.axis_index(("y", "core")) * rows, rows, 0
        )
        mats = mats.transpose(1, 0, 2, 3).reshape(6, dz, ff)
        live = {
            "own": lax.axis_index(REST),
            "wanted": wanted,
            "mats": mats[:4],
            "down": mats[4],
            "wide": jnp.concatenate([mats[4], mats[5]], axis=1),
            "tall": jnp.concatenate([mats[4], mats[5]], axis=0),
        }
        inputs, live = gather(chosen, REST, nr, live)
        inputs = live["inputs"] = inputs.reshape(tokens, dz)

        first = lax.dot_general(
            live.pop("mats"), inputs, (((1,), (1,)), ((), ())), preferred_element_type=F32
        )
        gram_rows = tokens // nr
        mine = lax.dynamic_slice_in_dim(inputs, live.pop("own") * gram_rows, gram_rows, 0)
        gram = jnp.concatenate(two_terms(dot(mine, inputs, 1, 1)))
        packed = first.astype(BF).reshape(4, nz, sub, tokens).transpose(1, 0, 2, 3)
        packed = packed.reshape(nz, 4 * sub, tokens)
        packed = jnp.concatenate(
            [packed, jnp.broadcast_to(gram[None], (nz,) + gram.shape)], axis=1
        )
        got, live = alone(packed, "zh", live)
        got = jnp.sum(got.astype(F32), axis=0)
        gate_val, upper, tan_gate, tan_upper = (
            got[i * sub : (i + 1) * sub] for i in range(4)
        )
        live["sums"] = (gate_val, upper, tan_gate, tan_upper)
        gram = got[4 * sub : 4 * sub + gram_rows] + got[4 * sub + gram_rows :]
        live["gram"] = jnp.concatenate(two_terms(gram))
        activated, slope_one, _ = silu_parts(gate_val)
        hidden = (activated * upper).astype(BF)
        tan_hidden = (slope_one * tan_gate * upper + activated * tan_upper).astype(BF)
        both, live = gather(jnp.concatenate([hidden, tan_hidden]), "zh", nz, live)
        hidden = live["hidden"] = both[:, :sub].reshape(ff, tokens)
        tan_hidden = live["tan_hidden"] = both[:, sub:].reshape(ff, tokens)

        def with_tangent(v, tan):
            upper = jnp.concatenate([v, tan], axis=1)
            lower = jnp.concatenate([jnp.zeros_like(v), v], axis=1)
            return jnp.concatenate([upper, lower], axis=0)

        out = dot(live.pop("wide"), with_tangent(hidden, tan_hidden), 1, 0).astype(BF)
        got, live = alone(out.reshape(nr, rows, 2 * tokens), REST, live)
        got = jnp.sum(got.astype(F32), axis=0)
        out, tan_out = got[:, :tokens], got[:, tokens:]
        resid = ((out - live.pop("wanted").astype(F32)) / tokens).astype(BF)
        tan_resid = (tan_out / tokens).astype(BF)
        packed = jnp.concatenate([resid, tan_resid, live.pop("gram")])
        both, live = gather(packed, REST, nr, live)
        resid = live["resid"] = both[:, :rows].reshape(dz, tokens)
        tan_resid = both[:, rows : 2 * rows].reshape(dz, tokens)
        gram_hi = both[:, 2 * rows : 2 * rows + gram_rows].reshape(tokens, tokens)
        gram_lo = both[:, 2 * rows + gram_rows :].reshape(tokens, tokens)
        live["gram"] = (gram_hi, gram_lo)

        back = dot(live.pop("tall"), with_tangent(resid, tan_resid), 0, 0).astype(BF)
        hv_down = dot(resid, live.pop("tan_hidden"), 1, 1)
        hv_down = live["hv_down"] = hv_down + dot(tan_resid, live["hidden"], 1, 1)
        down, hv_down_b = live.pop("down"), hv_down.astype(BF)
        live["wide"] = jnp.concatenate([down, hv_down_b], axis=1)
        live["tall"] = jnp.concatenate([down, hv_down_b], axis=0)

        def lanes(v):
            v = jnp.sum(v, axis=0, keepdims=True)
            return jnp.pad(v, ((0, 0), (0, tokens - v.shape[1])))

        def terms(*values):
            return jnp.concatenate([t for v in values for t in two_terms(v)])

        live["square"] = lanes(hv_down * hv_down)
        got, live = alone(back.reshape(nz, sub, 2 * tokens), "zh", live)
        got = jnp.sum(got.astype(F32), axis=0)
        live["back"] = got[:, :tokens]

        def by_gram(v):
            high, low = live["gram"]
            return dot(v, high, 1, 0) + dot(v, low, 1, 0)

        def deltas(tan_back, tan_gate, tan_upper):
            gate_val, upper, _, _ = live["sums"]
            activated, slope_one, slope_two = silu_parts(gate_val)
            back = live["back"]
            up = tan_back * activated + back * (slope_one * tan_gate)
            gate = (tan_back * upper + back * tan_upper) * slope_one + (
                back * upper
            ) * slope_two * tan_gate
            return jnp.concatenate([gate.astype(BF), up.astype(BF)])

        delta = deltas(got[:, tokens:], *live["sums"][2:])

        tangents = live["tangents"] = by_gram(delta)
        square = lanes(delta.astype(F32) * tangents) + live.pop("square")
        gate_val, upper, _, _ = live["sums"]
        activated, slope_one, _ = silu_parts(gate_val)
        tan_hidden = (
            (slope_one * tangents[:sub]) * upper + activated * tangents[sub:]
        ).astype(BF)
        both, live = gather(jnp.concatenate([tan_hidden, terms(square)]), "zh", nz, live)
        tan_hidden = live["tan_hidden"] = both[:, :sub].reshape(ff, tokens)
        square = jnp.sum(both[:, sub:].astype(F32), axis=(0, 1))[None]

        half = tokens // 2
        out = jnp.concatenate([tan_hidden, live["hidden"]])
        out = dot(live.pop("wide"), out, 1, 0).astype(BF).reshape(nr, rows, 2, half)
        scal = terms(square[:, :half] + square[:, half:])
        scal = jnp.broadcast_to(scal[None, None], (nr, 1, 2, half))
        got, live = alone(jnp.concatenate([out, scal], axis=1), REST, live)
        got, square = got[:, :rows].astype(F32), got[:, rows:].astype(F32)
        square = jnp.sum(square, axis=(0, 1, 2))[None]
        live["scale"] = 1.0 / jnp.sqrt(total(square) / count + 1e-6)
        got = jnp.sum(got, axis=0).reshape(rows, tokens)
        tan_resid = (got / tokens).astype(BF)
        tan_resid, live = gather(tan_resid, REST, nr, live)
        tan_resid = tan_resid.reshape(dz, tokens)

        resid = live.pop("resid")
        back = dot(live.pop("tall"), jnp.concatenate([tan_resid, resid]), 0, 0).astype(BF)
        scale = live.pop("scale")
        hv_down2 = dot(resid, live.pop("tan_hidden"), 1, 1)
        hv_down2 = hv_down2 + dot(tan_resid, live.pop("hidden"), 1, 1)
        hv_down2 = hv_down2 * across(scale, ff)
        live["inner"] = lanes((live.pop("hv_down") * across(scale, ff)) * hv_down2)
        live["square"] = lanes(hv_down2 * hv_down2)
        live["hv_down"] = hv_down2.astype(BF)
        live["scale"] = across(scale, tokens)
        got, live = alone(back.reshape(nz, sub, tokens), "zh", live)
        got = jnp.sum(got.astype(F32), axis=0)

        scale = live.pop("scale")
        tangents = live.pop("tangents") * scale
        delta = deltas(got * scale, tangents[:sub], tangents[sub:])
        wide = delta.astype(F32)
        inner = lanes(tangents * wide) + live.pop("inner")
        square = lanes(by_gram(delta) * wide) + live.pop("square")
        del live["gram"], live["sums"], live["back"]
        both, live = gather(jnp.concatenate([delta, terms(inner, square)]), "zh", nz, live)
        delta_gate = both[:, :sub].reshape(ff, tokens)
        delta_up = both[:, sub : 2 * sub].reshape(ff, tokens)
        sums = both[:, 2 * sub :].reshape(nz, 2, 2, tokens).astype(F32)
        sums = jnp.sum(sums, axis=(0, 2))
        if tokens > LANES:
            sums = sums[:, :LANES] + sums[:, LANES:]
        sums = jnp.pad(sums, ((0, 0), (0, LANES - sums.shape[1])))
        sums = terms(sums)

        hv = [
            jnp.pad(v.reshape(nx, d_dev, ff), ((0, 0), (0, 0), (0, LANES - ff)))
            for v in (
                dot(live["inputs"], delta_gate, 0, 1).astype(BF),
                dot(live["inputs"], delta_up, 0, 1).astype(BF),
                live["hv_down"],
            )
        ]
        hv.append(jnp.broadcast_to(sums[None], (nx,) + sums.shape))
        got, _ = alone(jnp.concatenate(hv, axis=1), NEAR, ())
        sums = jnp.sum(got[:, 3 * d_dev :].astype(F32), axis=0)
        hv = got[:, : 3 * d_dev, :ff].reshape(nx, 3, d_dev, ff)
        hv = hv.transpose(1, 2, 0, 3).reshape(3, d_dev, ff_dev)
        sums, hv = gather(sums[:2] + sums[2:], ("y", "core"), nt, hv)
        sums = total(jnp.sum(sums, axis=0))
        scale = across(1.0 / jnp.sqrt(sums[1:] / count + 1e-6), ff_dev)
        gate, up, down = (v.astype(F32) * scale for v in hv)
        return gate, up, down.T, sums[0, 0] / count

    return body


def build(devices, sizes):
    wide = Mesh(devices.reshape(sizes), AXES)
    dp, tensor = ("zh", *NEAR), ("y", "core")
    placed = (
        P(dp, tensor),
        P(dp),
        P(None, dp),
        P(dp, tensor),
        P(dp, tensor),
        P(tensor, dp),
        P(dp, tensor),
        P(dp, tensor),
        P(tensor, dp),
    )
    return jax.shard_map(
        make_body(*sizes),
        mesh=wide,
        in_specs=placed,
        out_specs=(P(dp, tensor), P(dp, tensor), P(tensor, dp), P()),
        check_vma=False,
    )


def solution(mesh):
    return build(mesh.devices, SIZES)
```

time: 271 us -> 262 us (0.967)
  blocking collectives: 68.2 us -> 228 us
  waiting for transfers between devices: 103 us -> 2.27 us
  starting transfers between devices: 73.6 us -> 11.9 us
  local copies, waits for them, and re-layouts: 9.68 us -> 5.18 us
  matrix products: 6.66 us -> 3.92 us
    all_to_all x4 -> x13, blocking collectives: 68.2 us -> 228 us  [exchange(): return lax.all_to_all(v, axes, split_axis=0, concat_axis=0, tiled=True)]
    all_to_all x10 -> x1, waiting for transfers between devices: 102 us -> 2.27 us  [exchange(): return lax.all_to_all(v, axes, split_axis=0, concat_axis=0, tiled=True)]
    all_to_all x10 -> x1, starting transfers between devices: 67.8 us -> 6.22 us  [exchange(): return lax.all_to_all(v, axes, split_axis=0, concat_axis=0, tiled=True)]
    broadcast_in_dim x8, local copies, waits for them, and re-layouts: 4.12 us -> 0.22 us  [the longest x7 0.2 us: gather(): return alone(jnp.broadcast_to(v[None], (n,) + v.shape), axes, live)]
    dot_general x15, matrix products: 6.06 us -> 3.32 us  [dot(): lax.dot_general(a, b, (((ca,), (cb,)), ((), ())), preferred_element_type=...]
  transfers between devices with their start and end apart: 11 -> 2, of which waited for: 11 -> 1; matrix products, arithmetic and copies ran while one was open for 1% -> 0% of each run, Pallas kernels for 0% -> 0%
where the time goes in v7:
time: 262 us; the launch traced here: 261 us
  blocking collectives  228 us (87%)
  starting transfers between devices  11.9 us (5%)
  local copies, waits for them, and re-layouts  5.18 us (2%)
  other arithmetic  4.8 us (2%)
  matrix products  3.92 us (1%)
  between operations  3.04 us (1%)
    all_to_all x13, blocking collectives, exchange(): return lax.all_to_all(v, axes, split_axis=0, concat_axis=0, tiled=True)  228 us
    all_to_all x1, starting transfers between devices, exchange(): return lax.all_to_all(v, axes, split_axis=0, concat_axis=0, tiled=True)  6.22 us
    ppermute x1, starting transfers between devices, body(): chosen = lax.ppermute(picked, ('zh', 'y', 'core'), swap)  5.73 us
  transfers between devices with their start and end apart: 2, of which 1 were waited for; matrix products, arithmetic and copies ran while one was open for 0% of the time, Pallas kernels for 0%

profile of v7, /device:TPU:1, one launch (start us, length us, event | category | flops | bytes accessed | tf_op | source)
XLA Modules:
  0.0 261.4 jit_solution(4248332159236333492)
XLA Ops:
  0.6 0.7 compare_select_fusion
  1.4 0.5 copy-done
  1.9 0.6 gather_fusion
  2.4 2.6 shard_map.120
  5.1 6.2 %all-to-all-start = ((bf16[8,6,64,112]{3,2,1,0:T(8,128)(2,1)}), bf16[8,6,64,112]{3,2,1,0:T(8,128)(2,1)S(1)}, u32[]{:S(2)}, u32[]{:S(2)}) async-start(bf16[8,6,64,112]{3,2,1,0:T(8,128)(2,1)} %shard_map.120), calls=%async_computation | async-start | bytes 1572864 | tf_op jit(solution)/shard_map/all_to_all | solution.py:25
  11.3 5.7 %collective-permute-start = (bf16[4,512]{1,0:T(4,128)(2,1)S(1)}, bf16[4,512]{1,0:T(4,128)(2,1)S(1)}, u32[]{:S(2)}, u32[]{:S(2)}) collective-permute-start(bf16[4,512]{1,0:T(4,128)(2,1)S(1)} %gather_fusion), channel_id=1, source_target_pairs={{0,0},{1,64},{2,128},{3,192},{4,256},{5,320},{6,384},{7,448},{64,1... | collective-permute-start | bytes 12296 | tf_op jit(solution)/shard_map/ppermute | solution.py:110
  17.3 2.3 all-to-all-done
  19.6 0.7 pad_maximum_fusion.1
  20.7 31.6 %all_to_all.70 = bf16[64,4,512]{2,1,0:T(4,128)(2,1)S(1)} all-to-all(bf16[64,4,512]{2,1,0:T(4,128)(2,1)S(1)} %broadcast_in_dim.37), channel_id=1, replica_groups=mesh['zh'=8,'zl'=2,'x'=4,'y'=4,'core'=2] {'zl','x','y','core'}, dimensions={0} | all-to-all | bytes 524288 | tf_op jit(solution)/shard_map/all_to_all | solution.py:25
  52.5 0.3 convolution_convert_fusion.2
  53.3 23.9 %all_to_all.71 = bf16[8,64,256]{2,1,0:T(8,128)(2,1)S(1)} all-to-all(bf16[8,64,256]{2,1,0:T(8,128)(2,1)S(1)} %copy.79), channel_id=1, replica_groups=mesh['zh'=8,'zl'=2,'x'=4,'y'=4,'core'=2] {'zh'}, dimensions={0} | all-to-all | bytes 524288 | tf_op jit(solution)/shard_map/all_to_all | solution.py:25
  77.4 19.8 %all_to_all.72 = bf16[8,28,256]{2,1,0:T(8,128)(2,1)S(1)} all-to-all(bf16[8,28,256]{2,1,0:T(8,128)(2,1)S(1)} %broadcast_in_dim.39), channel_id=1, replica_groups=mesh['zh'=8,'zl'=2,'x'=4,'y'=4,'core'=2] {'zh'}, dimensions={0} | all-to-all | bytes 229376 | tf_op jit(solution)/shard_map/all_to_all | solution.py:25
  97.2 0.3 fusion.1
  97.5 18.6 %all_to_all.73 = bf16[64,8,512]{2,1,0:T(8,128)(2,1)S(1)} all-to-all(bf16[64,8,512]{2,1,0:T(8,128)(2,1)S(1)} %fusion.1), channel_id=1, replica_groups=mesh['zh'=8,'zl'=2,'x'=4,'y'=4,'core'=2] {'zl','x','y','core'}, dimensions={0} | all-to-all | bytes 1048576 | tf_op jit(solution)/shard_map/all_to_all | solution.py:25
  116.3 19.1 %all_to_all.74 = bf16[64,24,256]{2,1,0:T(8,128)(2,1)S(1)} all-to-all(bf16[64,24,256]{2,1,0:T(8,128)(2,1)S(1)} %broadcast_in_dim.40), channel_id=1, replica_groups=mesh['zh'=8,'zl'=2,'x'=4,'y'=4,'core'=2] {'zl','x','y','core'}, dimensions={0} | all-to-all | bytes 1572864 | tf_op jit(solution)/shard_map/all_to_all | solution.py:25
  135.4 0.7 slice_bitcast_fusion
  136.6 0.3 fusion.102
  136.9 0.7 pad_maximum_fusion.4
  137.7 0.3 convolution_convert_fusion.3
  138.1 17.1 %all_to_all.75 = bf16[8,14,512]{2,1,0:T(8,128)(2,1)S(1)} all-to-all(bf16[8,14,512]{2,1,0:T(8,128)(2,1)S(1)} %reshape.134), channel_id=1, replica_groups=mesh['zh'=8,'zl'=2,'x'=4,'y'=4,'core'=2] {'zh'}, dimensions={0} | all-to-all | bytes 229376 | tf_op jit(solution)/shard_map/all_to_all | solution.py:25
  155.6 15.2 %all_to_all.76 = bf16[8,16,256]{2,1,0:T(8,128)(2,1)S(1)} all-to-all(bf16[8,16,256]{2,1,0:T(8,128)(2,1)S(1)} %broadcast_in_dim.43), channel_id=1, replica_groups=mesh['zh'=8,'zl'=2,'x'=4,'y'=4,'core'=2] {'zh'}, dimensions={0} | all-to-all | bytes 131072 | tf_op jit(solution)/shard_map/all_to_all | solution.py:25
  171.5 0.4 pad_maximum_fusion
  171.9 17.2 %all_to_all.77 = bf16[64,9,2,128]{3,2,1,0:T(2,128)(2,1)S(1)} all-to-all(bf16[64,9,2,128]{3,2,1,0:T(2,128)(2,1)S(1)} %pad_maximum_fusion), channel_id=1, replica_groups=mesh['zh'=8,'zl'=2,'x'=4,'y'=4,'core'=2] {'zl','x','y','core'}, dimensions={0} | all-to-all | bytes 589824 | tf_op jit(solution)/shard_map/all_to_all | solution.py:25
  189.6 13.8 %all_to_all.78 = bf16[64,8,256]{2,1,0:T(8,128)(2,1)S(1)} all-to-all(bf16[64,8,256]{2,1,0:T(8,128)(2,1)S(1)} %broadcast_in_dim.46), channel_id=1, replica_groups=mesh['zh'=8,'zl'=2,'x'=4,'y'=4,'core'=2] {'zl','x','y','core'}, dimensions={0} | all-to-all | bytes 524288 | tf_op jit(solution)/shard_map/all_to_all | solution.py:25
  203.9 0.3 multiply_reduce_fusion
  204.2 14.3 %all_to_all.79 = bf16[8,14,256]{2,1,0:T(8,128)(2,1)S(1)} all-to-all(bf16[8,14,256]{2,1,0:T(8,128)(2,1)S(1)} %reshape.140), channel_id=1, replica_groups=mesh['zh'=8,'zl'=2,'x'=4,'y'=4,'core'=2] {'zh'}, dimensions={0} | all-to-all | bytes 114688 | tf_op jit(solution)/shard_map/all_to_all | solution.py:25
  219.2 16.2 %all_to_all.80 = bf16[8,32,256]{2,1,0:T(8,128)(2,1)S(1)} all-to-all(bf16[8,32,256]{2,1,0:T(8,128)(2,1)S(1)} %broadcast_in_dim.102), channel_id=1, replica_groups=mesh['zh'=8,'zl'=2,'x'=4,'y'=4,'core'=2] {'zh'}, dimensions={0} | all-to-all | bytes 262144 | tf_op jit(solution)/shard_map/all_to_all | solution.py:25
  236.5 9.3 %all_to_all.81 = bf16[8,196,128]{2,1,0:T(8,128)(2,1)S(1)} all-to-all(bf16[8,196,128]{2,1,0:T(8,128)(2,1)S(1)} %fusion.28), channel_id=1, replica_groups=mesh['zh'=8,'zl'=2,'x'=4,'y'=4,'core'=2] {'zl','x'}, dimensions={0} | all-to-all | bytes 802816 | tf_op jit(solution)/shard_map/all_to_all | solution.py:25
  246.1 0.3 reshape.147
  246.4 11.5 %all_to_all.82 = f32[8,2,128]{2,1,0:T(2,128)S(1)} all-to-all(f32[8,2,128]{2,1,0:T(2,128)S(1)} %broadcast_in_dim.104), channel_id=1, replica_groups=mesh['zh'=8,'zl'=2,'x'=4,'y'=4,'core'=2] {'y','core'}, dimensions={0} | all-to-all | bytes 16384 | tf_op jit(solution)/shard_map/all_to_all | solution.py:25
  258.1 0.5 slice.173
  258.8 0.9 fusion.37
  (117 shorter events, 6.2 us)
Async XLA Ops:
  0.6 1.2 copy-start
  5.0 12.0 %copy-start.4 = (bf16[256,64]{0,1:T(8,128)(2,1)S(1)}, bf16[256,64]{0,1:T(8,128)(2,1)}, u32[]{:S(2)}) copy-start(bf16[256,64]{0,1:T(8,128)(2,1)} %param.11) | copy-start | bytes 98308
  5.1 14.5 %all-to-all-start = ((bf16[8,6,64,112]{3,2,1,0:T(8,128)(2,1)}), bf16[8,6,64,112]{3,2,1,0:T(8,128)(2,1)S(1)}, u32[]{:S(2)}, u32[]{:S(2)}) async-start(bf16[8,6,64,112]{3,2,1,0:T(8,128)(2,1)} %shard_map.120), calls=%async_computation | async-start | bytes 1572864 | tf_op jit(solution)/shard_map/all_to_all | solution.py:25
  11.3 9.3 %collective-permute-start = (bf16[4,512]{1,0:T(4,128)(2,1)S(1)}, bf16[4,512]{1,0:T(4,128)(2,1)S(1)}, u32[]{:S(2)}, u32[]{:S(2)}) collective-permute-start(bf16[4,512]{1,0:T(4,128)(2,1)S(1)} %gather_fusion), channel_id=1, source_target_pairs={{0,0},{1,64},{2,128},{3,192},{4,256},{5,320},{6,384},{7,448},{64,1... | collective-permute-start | bytes 12296 | tf_op jit(solution)/shard_map/ppermute | solution.py:110
  136.6 1.1 copy-start.1
  136.6 1.1 copy-start.2
  171.4 31.9 %copy-start.3 = (bf16[1024,112]{0,1:T(8,128)(2,1)S(1)}, bf16[1024,112]{0,1:T(8,128)(2,1)}, u32[]{:S(2)}) copy-start(bf16[1024,112]{0,1:T(8,128)(2,1)} %pad_maximum_fusion.4) | copy-start | bytes 688132

commit v8 on v7

--- a/solution.py
+++ b/solution.py
@@ -12,6 +12,7 @@
 SIZES = (8, 2, 4, 4, 2)
 NEAR = ("zl", "x")
 REST = ("zl", "x", "y", "core")
+QUAD = ("zl", "x", "y")
 LANES = 128
 BF = jnp.bfloat16
 F32 = jnp.float32
@@ -37,6 +38,10 @@
 def two_terms(v):
     high = lax.reduce_precision(v, 8, 7)
     return high.astype(BF), (v - high).astype(BF)
+
+
+def sibling(v):
+    return lax.ppermute(v, "core", [(0, 1), (1, 0)])
 
 
 def silu_parts(values):
@@ -101,6 +106,9 @@
         dz = d_dev * nx
         sub = ff // nz
         rows = dz // nr
+        nq = nr // nc
+        part = dz // nc
+        core = lax.axis_index("core")
         count = 3.0 * (dz * nz) * (ff_dev * nt)
 
         picked = pool.at[picks].get(mode="promise_in_bounds")
@@ -115,14 +123,23 @@
         wanted = lax.dynamic_slice_in_dim(
             wanted, lax.axis_index(("y", "core")) * rows, rows, 0
         )
-        mats = mats.transpose(1, 0, 2, 3).reshape(6, dz, ff)
+        mats = mats.transpose(1, 0, 2, 3)
+
+        def halves(v):
+            mine = lax.dynamic_index_in_dim(v, core, 0, keepdims=False)
+            return mine, lax.dynamic_index_in_dim(v, 1 - core, 0, keepdims=False)
+
+        pair = mats[4:].reshape(2, nx, ny, nc, rows, ff).transpose(3, 0, 1, 2, 4, 5)
+        mine, other = halves(pair.reshape(nc, 2, part, ff))
         live = {
-            "own": lax.axis_index(REST),
+            "own": core * nq + lax.axis_index(QUAD),
+            "first": core == 0,
             "wanted": wanted,
-            "mats": mats[:4],
-            "down": mats[4],
-            "wide": jnp.concatenate([mats[4], mats[5]], axis=1),
-            "tall": jnp.concatenate([mats[4], mats[5]], axis=0),
+            "mats": mats[:4].reshape(4, dz, ff),
+            "down": jnp.concatenate([mine[0], other[0]], axis=0),
+            "wide": jnp.concatenate([mine[0], mine[1]], axis=1),
+            "away": jnp.concatenate([other[0], other[1]], axis=1),
+            "tall": jnp.concatenate([mine[0], other[0], mine[1], other[1]], axis=0),
         }
         inputs, live = gather(chosen, REST, nr, live)
         inputs = live["inputs"] = inputs.reshape(tokens, dz)
@@ -158,26 +175,39 @@
             lower = jnp.concatenate([jnp.zeros_like(v), v], axis=1)
             return jnp.concatenate([upper, lower], axis=0)
 
-        out = dot(live.pop("wide"), with_tangent(hidden, tan_hidden), 1, 0).astype(BF)
-        got, live = alone(out.reshape(nr, rows, 2 * tokens), REST, live)
+        both = with_tangent(hidden, tan_hidden)
+        got = sibling(dot(live.pop("away"), both, 1, 0).astype(BF))
+        out = (dot(live.pop("wide"), both, 1, 0) + got.astype(F32)).astype(BF)
+        got, live = alone(out.reshape(nq, rows, 2 * tokens), QUAD, live)
         got = jnp.sum(got.astype(F32), axis=0)
         out, tan_out = got[:, :tokens], got[:, tokens:]
         resid = ((out - live.pop("wanted").astype(F32)) / tokens).astype(BF)
         tan_resid = (tan_out / tokens).astype(BF)
         packed = jnp.concatenate([resid, tan_resid, live.pop("gram")])
-        both, live = gather(packed, REST, nr, live)
-        resid = live["resid"] = both[:, :rows].reshape(dz, tokens)
-        tan_resid = both[:, rows : 2 * rows].reshape(dz, tokens)
-        gram_hi = both[:, 2 * rows : 2 * rows + gram_rows].reshape(tokens, tokens)
-        gram_lo = both[:, 2 * rows + gram_rows :].reshape(tokens, tokens)
-        live["gram"] = (gram_hi, gram_lo)
+        mine, live = gather(packed, QUAD, nq, live)
+        other = sibling(mine)
+
+        def joined(start, stop):
+            each = (v[:, start:stop].reshape(nq * (stop - start), tokens) for v in (mine, other))
+            return jnp.concatenate(list(each), axis=0)
+
+        def in_order(v):
+            swapped = jnp.concatenate([v[tokens // 2 :], v[: tokens // 2]], axis=0)
+            return jnp.where(live["first"], v, swapped)
+
+        resid = live["resid"] = joined(0, rows)
+        tan_resid = joined(rows, 2 * rows)
+        live["gram"] = (
+            in_order(joined(2 * rows, 2 * rows + gram_rows)),
+            in_order(joined(2 * rows + gram_rows, 2 * rows + 2 * gram_rows)),
+        )
+
+        del live["first"]
 
         back = dot(live.pop("tall"), with_tangent(resid, tan_resid), 0, 0).astype(BF)
         hv_down = dot(resid, live.pop("tan_hidden"), 1, 1)
         hv_down = live["hv_down"] = hv_down + dot(tan_resid, live["hidden"], 1, 1)
-        down, hv_down_b = live.pop("down"), hv_down.astype(BF)
-        live["wide"] = jnp.concatenate([down, hv_down_b], axis=1)
-        live["tall"] = jnp.concatenate([down, hv_down_b], axis=0)
+        live["hv_down_b"] = hv_down.astype(BF)
 
         def lanes(v):
             v = jnp.sum(v, axis=0, keepdims=True)
@@ -218,29 +248,39 @@
         tan_hidden = live["tan_hidden"] = both[:, :sub].reshape(ff, tokens)
         square = jnp.sum(both[:, sub:].astype(F32), axis=(0, 1))[None]
 
+        def out_rows(start, stop):
+            v = dot(live["down"][start:stop], tan_hidden, 1, 0)
+            return v + dot(live["hv_down_b"][start:stop], live["hidden"], 1, 0)
+
         half = tokens // 2
-        out = jnp.concatenate([tan_hidden, live["hidden"]])
-        out = dot(live.pop("wide"), out, 1, 0).astype(BF).reshape(nr, rows, 2, half)
+        got = jnp.concatenate([out_rows(part, dz).astype(BF), terms(square)])
+        got = sibling(got).astype(F32)
+        out = (out_rows(0, part) + got[:part]).astype(BF).reshape(nq, rows, 2, half)
+        square = square + got[part : part + 1] + got[part + 1 :]
         scal = terms(square[:, :half] + square[:, half:])
-        scal = jnp.broadcast_to(scal[None, None], (nr, 1, 2, half))
-        got, live = alone(jnp.concatenate([out, scal], axis=1), REST, live)
+        scal = jnp.broadcast_to(scal[None, None], (nq, 1, 2, half))
+        got, live = alone(jnp.concatenate([out, scal], axis=1), QUAD, live)
         got, square = got[:, :rows].astype(F32), got[:, rows:].astype(F32)
         square = jnp.sum(square, axis=(0, 1, 2))[None]
         live["scale"] = 1.0 / jnp.sqrt(total(square) / count + 1e-6)
         got = jnp.sum(got, axis=0).reshape(rows, tokens)
         tan_resid = (got / tokens).astype(BF)
-        tan_resid, live = gather(tan_resid, REST, nr, live)
-        tan_resid = tan_resid.reshape(dz, tokens)
+        tan_resid, live = gather(tan_resid, QUAD, nq, live)
+        tan_resid = tan_resid.reshape(part, tokens)
+        tan_resid = jnp.concatenate([tan_resid, sibling(tan_resid)], axis=0)
 
         resid = live.pop("resid")
-        back = dot(live.pop("tall"), jnp.concatenate([tan_resid, resid]), 0, 0).astype(BF)
+        back = dot(live.pop("down"), tan_resid, 0, 0)
+        back = (back + dot(live.pop("hv_down_b"), resid, 0, 0)).astype(BF)
         scale = live.pop("scale")
         hv_down2 = dot(resid, live.pop("tan_hidden"), 1, 1)
         hv_down2 = hv_down2 + dot(tan_resid, live.pop("hidden"), 1, 1)
         hv_down2 = hv_down2 * across(scale, ff)
         live["inner"] = lanes((live.pop("hv_down") * across(scale, ff)) * hv_down2)
         live["square"] = lanes(hv_down2 * hv_down2)
-        live["hv_down"] = hv_down2.astype(BF)
+        hv_down2 = jnp.stack(halves(hv_down2.astype(BF).reshape(nc, part, ff)))
+        hv_down2 = hv_down2.reshape(nc, nx, ny, rows, ff).transpose(1, 2, 0, 3, 4)
+        live["hv_down"] = hv_down2.reshape(dz, ff)
         live["scale"] = across(scale, tokens)
         got, live = alone(back.reshape(nz, sub, tokens), "zh", live)
         got = jnp.sum(got.astype(F32), axis=0)

time: 262 us -> 262 us (level)
  blocking collectives: 228 us -> 206 us
  starting transfers between devices: 11.9 us -> 30.8 us
  waiting for transfers between devices: 2.27 us -> 6.34 us
    all_to_all x13, blocking collectives: 228 us -> 206 us  [exchange(): return lax.all_to_all(v, axes, split_axis=0, concat_axis=0, tiled=True)]
    ppermute x0 -> x4, starting transfers between devices: none -> 18.9 us  [sibling(): return lax.ppermute(v, 'core', [(0, 1), (1, 0)])]
    ppermute x0 -> x4, waiting for transfers between devices: none -> 4.07 us  [sibling(): return lax.ppermute(v, 'core', [(0, 1), (1, 0)])]
  transfers between devices with their start and end apart: 2 -> 6, of which waited for: 1 -> 5; matrix products, arithmetic and copies ran while one was open for 0% -> 0% of each run, Pallas kernels for 0% -> 0%
where the time goes in v8:
time: 262 us; the launch traced here: 261 us
  blocking collectives  206 us (79%)
  starting transfers between devices  30.8 us (12%)
  waiting for transfers between devices  6.34 us (2%)
  matrix products  4.73 us (2%)
  local copies, waits for them, and re-layouts  4.37 us (2%)
  between operations  3.24 us (1%)
  other arithmetic  3.09 us (1%)
    all_to_all x13, blocking collectives, exchange(): return lax.all_to_all(v, axes, split_axis=0, concat_axis=0, tiled=True)  206 us
    ppermute x4, starting transfers between devices, sibling(): return lax.ppermute(v, 'core', [(0, 1), (1, 0)])  18.9 us
    all_to_all x1, starting transfers between devices, exchange(): return lax.all_to_all(v, axes, split_axis=0, concat_axis=0, tiled=True)  6.22 us
    ppermute x1, starting transfers between devices, body(): chosen = lax.ppermute(picked, ('zh', 'y', 'core'), swap)  5.73 us
  transfers between devices with their start and end apart: 6, of which 5 were waited for; matrix products, arithmetic and copies ran while one was open for 0% of the time, Pallas kernels for 0%

profile of v8, /device:TPU:1, one launch (start us, length us, event | category | flops | bytes accessed | tf_op | source)
XLA Modules:
  0.0 261.1 jit_solution(15464811035054337154)
XLA Ops:
  0.6 0.7 compare_select_fusion
  1.4 0.5 copy-done
  1.9 0.6 gather_fusion
  2.4 2.6 shard_map.120
  5.1 6.2 %all-to-all-start = ((bf16[8,6,64,112]{3,2,1,0:T(8,128)(2,1)}), bf16[8,6,64,112]{3,2,1,0:T(8,128)(2,1)S(1)}, u32[]{:S(2)}, u32[]{:S(2)}) async-start(bf16[8,6,64,112]{3,2,1,0:T(8,128)(2,1)} %shard_map.120), calls=%async_computation | async-start | bytes 1572864 | tf_op jit(solution)/shard_map/all_to_all | solution.py:26
  11.3 5.7 %collective-permute-start = (bf16[4,512]{1,0:T(4,128)(2,1)S(1)}, bf16[4,512]{1,0:T(4,128)(2,1)S(1)}, u32[]{:S(2)}, u32[]{:S(2)}) collective-permute-start(bf16[4,512]{1,0:T(4,128)(2,1)S(1)} %gather_fusion), channel_id=1, source_target_pairs={{0,0},{1,64},{2,128},{3,192},{4,256},{5,320},{6,384},{7,448},{64,1... | collective-permute-start | bytes 12296 | tf_op jit(solution)/shard_map/ppermute | solution.py:118
  17.3 2.3 all-to-all-done
  20.1 32.2 %all_to_all.70 = bf16[64,4,512]{2,1,0:T(4,128)(2,1)S(1)} all-to-all(bf16[64,4,512]{2,1,0:T(4,128)(2,1)S(1)} %broadcast_in_dim.35), channel_id=1, replica_groups=mesh['zh'=8,'zl'=2,'x'=4,'y'=4,'core'=2] {'zl','x','y','core'}, dimensions={0} | all-to-all | bytes 524288 | tf_op jit(solution)/shard_map/all_to_all | solution.py:26
  52.5 0.3 convolution_convert_fusion.1
  53.3 23.9 %all_to_all.71 = bf16[8,64,256]{2,1,0:T(8,128)(2,1)S(1)} all-to-all(bf16[8,64,256]{2,1,0:T(8,128)(2,1)S(1)} %copy.84), channel_id=1, replica_groups=mesh['zh'=8,'zl'=2,'x'=4,'y'=4,'core'=2] {'zh'}, dimensions={0} | all-to-all | bytes 524288 | tf_op jit(solution)/shard_map/all_to_all | solution.py:26
  77.4 19.8 %all_to_all.72 = bf16[8,28,256]{2,1,0:T(8,128)(2,1)S(1)} all-to-all(bf16[8,28,256]{2,1,0:T(8,128)(2,1)S(1)} %broadcast_in_dim.37), channel_id=1, replica_groups=mesh['zh'=8,'zl'=2,'x'=4,'y'=4,'core'=2] {'zh'}, dimensions={0} | all-to-all | bytes 229376 | tf_op jit(solution)/shard_map/all_to_all | solution.py:26
  97.4 4.6 %collective-permute-start.1 = (bf16[256,512]{1,0:T(8,128)(2,1)S(1)}, bf16[256,512]{1,0:T(8,128)(2,1)S(1)}, u32[]{:S(2)}, u32[]{:S(2)}) collective-permute-start(bf16[256,512]{1,0:T(8,128)(2,1)S(1)} %convolution_convert_fusion), channel_id=1, source_target_pairs={{0,1},{1,0},{2,3},{3,2},{4,5},{5,4},{6,7},{7,6},{8,9},{9,8},{10,11... | collective-permute-start | bytes 786440 | tf_op jit(solution)/shard_map/ppermute | solution.py:44
  102.0 1.1 collective-permute-done.1
  103.4 11.3 %all_to_all.73 = bf16[32,8,512]{2,1,0:T(8,128)(2,1)S(1)} all-to-all(bf16[32,8,512]{2,1,0:T(8,128)(2,1)S(1)} %fusion.31), channel_id=1, replica_groups=mesh['zh'=8,'zl'=2,'x'=4,'y'=4,'core'=2] {'zl','x','y'}, dimensions={0} | all-to-all | bytes 524288 | tf_op jit(solution)/shard_map/all_to_all | solution.py:26
  114.8 12.6 %all_to_all.74 = bf16[32,24,256]{2,1,0:T(8,128)(2,1)S(1)} all-to-all(bf16[32,24,256]{2,1,0:T(8,128)(2,1)S(1)} %broadcast_in_dim.38), channel_id=1, replica_groups=mesh['zh'=8,'zl'=2,'x'=4,'y'=4,'core'=2] {'zl','x','y'}, dimensions={0} | all-to-all | bytes 786432 | tf_op jit(solution)/shard_map/all_to_all | solution.py:26
  127.4 4.7 %collective-permute-start.2 = (bf16[32,24,256]{2,1,0:T(8,128)(2,1)S(1)}, bf16[32,24,256]{2,1,0:T(8,128)(2,1)S(1)}, u32[]{:S(2)}, u32[]{:S(2)}) collective-permute-start(bf16[32,24,256]{2,1,0:T(8,128)(2,1)S(1)} %all_to_all.74), channel_id=1, source_target_pairs={{0,1},{1,0},{2,3},{3,2},{4,5},{5,4},{6,7},{7,6},{8,9},{9,8},{10,11... | collective-permute-start | bytes 1179656 | tf_op jit(solution)/shard_map/ppermute | solution.py:44
  132.2 1.2 collective-permute-done.2
  133.7 0.3 convolution_convert_fusion.2
  134.5 15.9 %all_to_all.75 = bf16[8,14,512]{2,1,0:T(8,128)(2,1)S(1)} all-to-all(bf16[8,14,512]{2,1,0:T(8,128)(2,1)S(1)} %reshape.195), channel_id=1, replica_groups=mesh['zh'=8,'zl'=2,'x'=4,'y'=4,'core'=2] {'zh'}, dimensions={0} | all-to-all | bytes 229376 | tf_op jit(solution)/shard_map/all_to_all | solution.py:26
  150.9 16.5 %all_to_all.76 = bf16[8,16,256]{2,1,0:T(8,128)(2,1)S(1)} all-to-all(bf16[8,16,256]{2,1,0:T(8,128)(2,1)S(1)} %broadcast_in_dim.41), channel_id=1, replica_groups=mesh['zh'=8,'zl'=2,'x'=4,'y'=4,'core'=2] {'zh'}, dimensions={0} | all-to-all | bytes 131072 | tf_op jit(solution)/shard_map/all_to_all | solution.py:26
  167.9 4.8 %collective-permute-start.3 = (bf16[258,256]{1,0:T(8,128)(2,1)S(1)}, bf16[258,256]{1,0:T(8,128)(2,1)S(1)}, u32[]{:S(2)}, u32[]{:S(2)}) collective-permute-start(bf16[258,256]{1,0:T(8,128)(2,1)S(1)} %pad_maximum_fusion.7), channel_id=1, source_target_pairs={{0,1},{1,0},{2,3},{3,2},{4,5},{5,4},{6,7},{7,6},{8,9},{9,8},{10,11... | collective-permute-start | bytes 396296 | tf_op jit(solution)/shard_map/ppermute | solution.py:44
  172.8 0.8 collective-permute-done.3
  174.3 11.3 %all_to_all.77 = bf16[32,9,2,128]{3,2,1,0:T(2,128)(2,1)S(1)} all-to-all(bf16[32,9,2,128]{3,2,1,0:T(2,128)(2,1)S(1)} %pad_maximum_fusion.6), channel_id=1, replica_groups=mesh['zh'=8,'zl'=2,'x'=4,'y'=4,'core'=2] {'zl','x','y'}, dimensions={0} | all-to-all | bytes 294912 | tf_op jit(solution)/shard_map/all_to_all | solution.py:26
  185.8 10.7 %all_to_all.78 = bf16[32,8,256]{2,1,0:T(8,128)(2,1)S(1)} all-to-all(bf16[32,8,256]{2,1,0:T(8,128)(2,1)S(1)} %broadcast_in_dim.43), channel_id=1, replica_groups=mesh['zh'=8,'zl'=2,'x'=4,'y'=4,'core'=2] {'zl','x','y'}, dimensions={0} | all-to-all | bytes 262144 | tf_op jit(solution)/shard_map/all_to_all | solution.py:26
  197.0 4.9 %collective-permute-start.4 = (bf16[256,256]{1,0:T(8,128)(2,1)S(1)}, bf16[256,256]{1,0:T(8,128)(2,1)S(1)}, u32[]{:S(2)}, u32[]{:S(2)}) collective-permute-start(bf16[256,256]{1,0:T(8,128)(2,1)S(1)} %bitcast.127), channel_id=1, source_target_pairs={{0,1},{1,0},{2,3},{3,2},{4,5},{5,4},{6,7},{7,6},{8,9},{9,8},{10,11... | collective-permute-start | bytes 393224 | tf_op jit(solution)/shard_map/ppermute | solution.py:44
  201.9 0.9 collective-permute-done.4
  203.7 14.5 %all_to_all.79 = bf16[8,14,256]{2,1,0:T(8,128)(2,1)S(1)} all-to-all(bf16[8,14,256]{2,1,0:T(8,128)(2,1)S(1)} %reshape.203), channel_id=1, replica_groups=mesh['zh'=8,'zl'=2,'x'=4,'y'=4,'core'=2] {'zh'}, dimensions={0} | all-to-all | bytes 114688 | tf_op jit(solution)/shard_map/all_to_all | solution.py:26
  218.8 15.5 %all_to_all.80 = bf16[8,32,256]{2,1,0:T(8,128)(2,1)S(1)} all-to-all(bf16[8,32,256]{2,1,0:T(8,128)(2,1)S(1)} %broadcast_in_dim.48), channel_id=1, replica_groups=mesh['zh'=8,'zl'=2,'x'=4,'y'=4,'core'=2] {'zh'}, dimensions={0} | all-to-all | bytes 262144 | tf_op jit(solution)/shard_map/all_to_all | solution.py:26
  235.2 9.5 %all_to_all.81 = bf16[8,196,128]{2,1,0:T(8,128)(2,1)S(1)} all-to-all(bf16[8,196,128]{2,1,0:T(8,128)(2,1)S(1)} %fusion.29), channel_id=1, replica_groups=mesh['zh'=8,'zl'=2,'x'=4,'y'=4,'core'=2] {'zl','x'}, dimensions={0} | all-to-all | bytes 802816 | tf_op jit(solution)/shard_map/all_to_all | solution.py:26
  245.3 12.3 %all_to_all.82 = f32[8,2,128]{2,1,0:T(2,128)S(1)} all-to-all(f32[8,2,128]{2,1,0:T(2,128)S(1)} %broadcast_in_dim.50), channel_id=1, replica_groups=mesh['zh'=8,'zl'=2,'x'=4,'y'=4,'core'=2] {'y','core'}, dimensions={0} | all-to-all | bytes 16384 | tf_op jit(solution)/shard_map/all_to_all | solution.py:26
  257.7 0.5 slice.230
  259.1 0.9 fusion.38
  (139 shorter events, 8.3 us)
Async XLA Ops:
  0.6 1.2 copy-start
  5.0 12.0 %copy-start.1 = (bf16[256,64]{0,1:T(8,128)(2,1)S(1)}, bf16[256,64]{0,1:T(8,128)(2,1)}, u32[]{:S(2)}) copy-start(bf16[256,64]{0,1:T(8,128)(2,1)} %param.11) | copy-start | bytes 98308
  5.1 14.5 %all-to-all-start = ((bf16[8,6,64,112]{3,2,1,0:T(8,128)(2,1)}), bf16[8,6,64,112]{3,2,1,0:T(8,128)(2,1)S(1)}, u32[]{:S(2)}, u32[]{:S(2)}) async-start(bf16[8,6,64,112]{3,2,1,0:T(8,128)(2,1)} %shard_map.120), calls=%async_computation | async-start | bytes 1572864 | tf_op jit(solution)/shard_map/all_to_all | solution.py:26
  11.3 8.8 %collective-permute-start = (bf16[4,512]{1,0:T(4,128)(2,1)S(1)}, bf16[4,512]{1,0:T(4,128)(2,1)S(1)}, u32[]{:S(2)}, u32[]{:S(2)}) collective-permute-start(bf16[4,512]{1,0:T(4,128)(2,1)S(1)} %gather_fusion), channel_id=1, source_target_pairs={{0,0},{1,64},{2,128},{3,192},{4,256},{5,320},{6,384},{7,448},{64,1... | collective-permute-start | bytes 12296 | tf_op jit(solution)/shard_map/ppermute | solution.py:118
  97.4 5.7 %collective-permute-start.1 = (bf16[256,512]{1,0:T(8,128)(2,1)S(1)}, bf16[256,512]{1,0:T(8,128)(2,1)S(1)}, u32[]{:S(2)}, u32[]{:S(2)}) collective-permute-start(bf16[256,512]{1,0:T(8,128)(2,1)S(1)} %convolution_convert_fusion), channel_id=1, source_target_pairs={{0,1},{1,0},{2,3},{3,2},{4,5},{5,4},{6,7},{7,6},{8,9},{9,8},{10,11... | collective-permute-start | bytes 786440 | tf_op jit(solution)/shard_map/ppermute | solution.py:44
  127.4 6.0 %collective-permute-start.2 = (bf16[32,24,256]{2,1,0:T(8,128)(2,1)S(1)}, bf16[32,24,256]{2,1,0:T(8,128)(2,1)S(1)}, u32[]{:S(2)}, u32[]{:S(2)}) collective-permute-start(bf16[32,24,256]{2,1,0:T(8,128)(2,1)S(1)} %all_to_all.74), channel_id=1, source_target_pairs={{0,1},{1,0},{2,3},{3,2},{4,5},{5,4},{6,7},{7,6},{8,9},{9,8},{10,11... | collective-permute-start | bytes 1179656 | tf_op jit(solution)/shard_map/ppermute | solution.py:44
  167.9 5.8 %collective-permute-start.3 = (bf16[258,256]{1,0:T(8,128)(2,1)S(1)}, bf16[258,256]{1,0:T(8,128)(2,1)S(1)}, u32[]{:S(2)}, u32[]{:S(2)}) collective-permute-start(bf16[258,256]{1,0:T(8,128)(2,1)S(1)} %pad_maximum_fusion.7), channel_id=1, source_target_pairs={{0,1},{1,0},{2,3},{3,2},{4,5},{5,4},{6,7},{7,6},{8,9},{9,8},{10,11... | collective-permute-start | bytes 396296 | tf_op jit(solution)/shard_map/ppermute | solution.py:44
  197.0 5.9 %collective-permute-start.4 = (bf16[256,256]{1,0:T(8,128)(2,1)S(1)}, bf16[256,256]{1,0:T(8,128)(2,1)S(1)}, u32[]{:S(2)}, u32[]{:S(2)}) collective-permute-start(bf16[256,256]{1,0:T(8,128)(2,1)S(1)} %bitcast.127), channel_id=1, source_target_pairs={{0,1},{1,0},{2,3},{3,2},{4,5},{5,4},{6,7},{7,6},{8,9},{9,8},{10,11... | collective-permute-start | bytes 393224 | tf_op jit(solution)/shard_map/ppermute | solution.py:44

commit v9 on v7

--- a/solution.py
+++ b/solution.py
@@ -12,7 +12,9 @@
 SIZES = (8, 2, 4, 4, 2)
 NEAR = ("zl", "x")
 REST = ("zl", "x", "y", "core")
+QUAD = ("zl", "x", "y")
 LANES = 128
+TILE = 16
 BF = jnp.bfloat16
 F32 = jnp.float32
 
@@ -37,6 +39,10 @@
 def two_terms(v):
     high = lax.reduce_precision(v, 8, 7)
     return high.astype(BF), (v - high).astype(BF)
+
+
+def sibling(v):
+    return lax.ppermute(v, "core", [(0, 1), (1, 0)])
 
 
 def silu_parts(values):
@@ -47,45 +53,63 @@
     return activated, slope_one, slope_two
 
 
-def total(v):
-    ones = jnp.ones((v.shape[1], LANES), F32)
+def total(v, columns):
+    ones = jnp.ones((v.shape[1], columns), F32)
     return lax.dot_general(
         v, ones, (((1,), (0,)), ((), ())), precision=lax.Precision.HIGHEST, preferred_element_type=F32
     )
 
 
-def across(row, columns):
-    return jnp.concatenate([row] * pl.cdiv(columns, LANES), axis=1)[:, :columns]
-
-
-def pack_kernel(ff, count, *refs):
-    mats, out, held, sem = refs[:count], refs[count], refs[count + 1 : -1], refs[-1]
-    copies = [
-        pltpu.make_async_copy(mats[m], held[m], sem.at[m]) for m in range(count)
-    ]
+def load_kernel(ff, count, picks, pool, *refs):
+    mats, chosen, out = refs[:count], refs[count], refs[count + 1]
+    held, near, sem = refs[count + 2 : -2], refs[-2], refs[-1]
+    tok_dev = chosen.shape[0]
+    copies = []
+    for k in range(tok_dev):
+        first = pl.multiple_of(picks[k] // TILE * TILE, TILE)
+        copies.append(
+            pltpu.make_async_copy(pool.at[pl.ds(first, TILE)], near.at[k], sem.at[count + k])
+        )
+    for m in range(count):
+        copies.append(pltpu.make_async_copy(mats[m], held[m], sem.at[m]))
     for copy in copies:
         copy.start()
-    for m, copy in enumerate(copies):
-        copy.wait()
+    for m in range(count):
+        copies[tok_dev + m].wait()
         v = held[m][...].astype(F32)
         for e in range(out.shape[0]):
             out[e, m] = v[:, e * ff : (e + 1) * ff].astype(BF)
-
-
-def pack(mats, parts):
+    picked = []
+    for k in range(tok_dev):
+        copies[k].wait()
+        v = near[k].astype(F32)
+        row = lax.broadcasted_iota(jnp.int32, v.shape, 0)
+        v = jnp.where(row == picks[k] % TILE, v, 0.0)
+        picked.append(jnp.sum(v, axis=0, keepdims=True))
+    chosen[...] = jnp.concatenate(picked, axis=0).astype(BF)
+
+
+def load(picks, pool, mats, parts):
     rows, columns = mats[0].shape
     ff = columns // parts
-    shape = (parts, len(mats), rows, ff)
+    tok_dev, width = picks.shape[0], pool.shape[1]
     return pl.pallas_call(
-        functools.partial(pack_kernel, ff, len(mats)),
-        out_shape=jax.ShapeDtypeStruct(shape, BF),
-        in_specs=[pl.BlockSpec(memory_space=pl.ANY)] * len(mats),
-        out_specs=pl.BlockSpec(memory_space=pltpu.VMEM),
+        functools.partial(load_kernel, ff, len(mats)),
+        out_shape=[
+            jax.ShapeDtypeStruct((tok_dev, width), BF),
+            jax.ShapeDtypeStruct((parts, len(mats), rows, ff), BF),
+        ],
+        in_specs=[pl.BlockSpec(memory_space=pltpu.SMEM)]
+        + [pl.BlockSpec(memory_space=pl.ANY)] * (1 + len(mats)),
+        out_specs=[pl.BlockSpec(memory_space=pltpu.VMEM)] * 2,
         scratch_shapes=[pltpu.VMEM(m.shape, m.dtype) for m in mats]
-        + [pltpu.SemaphoreType.DMA((len(mats),))],
+        + [
+            pltpu.VMEM((tok_dev, TILE, width), BF),
+            pltpu.SemaphoreType.DMA((len(mats) + tok_dev,)),
+        ],
         compiler_params=pltpu.CompilerParams(vmem_limit_bytes=56 << 20),
         cost_estimate=pl.CostEstimate(flops=0, bytes_accessed=2 << 20, transcendentals=0),
-    )(*mats)
+    )(picks, pool, *mats)
 
 
 def make_body(nz, nl, nx, ny, nc):
@@ -101,14 +125,14 @@
         dz = d_dev * nx
         sub = ff // nz
         rows = dz // nr
+        nq = nr // nc
         count = 3.0 * (dz * nz) * (ff_dev * nt)
 
-        picked = pool.at[picks].get(mode="promise_in_bounds")
         mats = (gate_w, up_w, probe_g, probe_u, down_w.T, probe_d.T)
-        picked, mats = lax.optimization_barrier((picked, mats))
+        picked, mats = load(picks, pool, mats, nx)
         swap = [(i * nt + j, j * nz + i) for i in range(nz) for j in range(nt)]
         chosen = lax.ppermute(picked, ("zh", "y", "core"), swap)
-        mats = exchange(pack(mats, nx), NEAR)
+        mats = exchange(mats, NEAR)
 
         wanted = targets.reshape(nz, nx, tok_dev, d_dev).transpose(1, 0, 2, 3)
         wanted = wanted.reshape(tokens, d_dev).T
@@ -120,9 +144,10 @@
             "own": lax.axis_index(REST),
             "wanted": wanted,
             "mats": mats[:4],
+            "first": lax.axis_index("core") == 0,
             "down": mats[4],
             "wide": jnp.concatenate([mats[4], mats[5]], axis=1),
-            "tall": jnp.concatenate([mats[4], mats[5]], axis=0),
+            "tall": mats[4:].reshape(2 * dz, ff),
         }
         inputs, live = gather(chosen, REST, nr, live)
         inputs = live["inputs"] = inputs.reshape(tokens, dz)
@@ -165,19 +190,24 @@
         resid = ((out - live.pop("wanted").astype(F32)) / tokens).astype(BF)
         tan_resid = (tan_out / tokens).astype(BF)
         packed = jnp.concatenate([resid, tan_resid, live.pop("gram")])
-        both, live = gather(packed, REST, nr, live)
-        resid = live["resid"] = both[:, :rows].reshape(dz, tokens)
-        tan_resid = both[:, rows : 2 * rows].reshape(dz, tokens)
-        gram_hi = both[:, 2 * rows : 2 * rows + gram_rows].reshape(tokens, tokens)
-        gram_lo = both[:, 2 * rows + gram_rows :].reshape(tokens, tokens)
-        live["gram"] = (gram_hi, gram_lo)
+        mine, live = gather(packed, QUAD, nq, live)
+        other, first = sibling(mine), live.pop("first")
+        both = jnp.stack([jnp.where(first, mine, other), jnp.where(first, other, mine)], axis=1)
+
+        def joined(start, stop):
+            return both[:, :, start:stop].reshape(nr * (stop - start), tokens)
+
+        resid = live["resid"] = joined(0, rows)
+        tan_resid = joined(rows, 2 * rows)
+        live["gram"] = (
+            joined(2 * rows, 2 * rows + gram_rows),
+            joined(2 * rows + gram_rows, 2 * rows + 2 * gram_rows),
+        )
 
         back = dot(live.pop("tall"), with_tangent(resid, tan_resid), 0, 0).astype(BF)
         hv_down = dot(resid, live.pop("tan_hidden"), 1, 1)
         hv_down = live["hv_down"] = hv_down + dot(tan_resid, live["hidden"], 1, 1)
-        down, hv_down_b = live.pop("down"), hv_down.astype(BF)
-        live["wide"] = jnp.concatenate([down, hv_down_b], axis=1)
-        live["tall"] = jnp.concatenate([down, hv_down_b], axis=0)
+        live["hv_down_b"] = hv_down.astype(BF)
 
         def lanes(v):
             v = jnp.sum(v, axis=0, keepdims=True)
@@ -219,29 +249,31 @@
         square = jnp.sum(both[:, sub:].astype(F32), axis=(0, 1))[None]
 
         half = tokens // 2
-        out = jnp.concatenate([tan_hidden, live["hidden"]])
-        out = dot(live.pop("wide"), out, 1, 0).astype(BF).reshape(nr, rows, 2, half)
+        out = dot(live["down"], tan_hidden, 1, 0)
+        out = (out + dot(live["hv_down_b"], live["hidden"], 1, 0)).astype(BF)
+        out = out.reshape(nr, rows, 2, half)
         scal = terms(square[:, :half] + square[:, half:])
         scal = jnp.broadcast_to(scal[None, None], (nr, 1, 2, half))
         got, live = alone(jnp.concatenate([out, scal], axis=1), REST, live)
         got, square = got[:, :rows].astype(F32), got[:, rows:].astype(F32)
         square = jnp.sum(square, axis=(0, 1, 2))[None]
-        live["scale"] = 1.0 / jnp.sqrt(total(square) / count + 1e-6)
+        live["scale"] = 1.0 / jnp.sqrt(total(square, tokens) / count + 1e-6)
         got = jnp.sum(got, axis=0).reshape(rows, tokens)
         tan_resid = (got / tokens).astype(BF)
         tan_resid, live = gather(tan_resid, REST, nr, live)
         tan_resid = tan_resid.reshape(dz, tokens)
 
         resid = live.pop("resid")
-        back = dot(live.pop("tall"), jnp.concatenate([tan_resid, resid]), 0, 0).astype(BF)
+        back = dot(live.pop("down"), tan_resid, 0, 0)
+        back = (back + dot(live.pop("hv_down_b"), resid, 0, 0)).astype(BF)
         scale = live.pop("scale")
         hv_down2 = dot(resid, live.pop("tan_hidden"), 1, 1)
         hv_down2 = hv_down2 + dot(tan_resid, live.pop("hidden"), 1, 1)
-        hv_down2 = hv_down2 * across(scale, ff)
-        live["inner"] = lanes((live.pop("hv_down") * across(scale, ff)) * hv_down2)
+        hv_down2 = hv_down2 * scale[:, :ff]
+        live["inner"] = lanes((live.pop("hv_down") * scale[:, :ff]) * hv_down2)
         live["square"] = lanes(hv_down2 * hv_down2)
         live["hv_down"] = hv_down2.astype(BF)
-        live["scale"] = across(scale, tokens)
+        live["scale"] = scale
         got, live = alone(back.reshape(nz, sub, tokens), "zh", live)
         got = jnp.sum(got.astype(F32), axis=0)
 
@@ -276,10 +308,10 @@
         hv = got[:, : 3 * d_dev, :ff].reshape(nx, 3, d_dev, ff)
         hv = hv.transpose(1, 2, 0, 3).reshape(3, d_dev, ff_dev)
         sums, hv = gather(sums[:2] + sums[2:], ("y", "core"), nt, hv)
-        sums = total(jnp.sum(sums, axis=0))
-        scale = across(1.0 / jnp.sqrt(sums[1:] / count + 1e-6), ff_dev)
+        sums = total(jnp.sum(sums, axis=0), ff_dev) / count
+        scale = 1.0 / jnp.sqrt(sums[1:] + 1e-6)
         gate, up, down = (v.astype(F32) * scale for v in hv)
-        return gate, up, down.T, sums[0, 0] / count
+        return gate, up, down.T, sums[:1, :1].reshape(())
 
     return body
 

time: 262 us -> 257 us (0.981)
  blocking collectives: 228 us -> 221 us
  starting transfers between devices: 11.9 us -> 16.4 us
    all_to_all x13, blocking collectives: 228 us -> 221 us  [exchange(): return lax.all_to_all(v, axes, split_axis=0, concat_axis=0, tiled=True)]
    ppermute x0 -> x1, starting transfers between devices: none -> 4.42 us  [sibling(): return lax.ppermute(v, 'core', [(0, 1), (1, 0)])]
  transfers between devices with their start and end apart: 2 -> 3, of which waited for: 1 -> 2; matrix products, arithmetic and copies ran while one was open for 0% -> 0% of each run, Pallas kernels for 0% -> 0%
where the time goes in v9:
time: 257 us; the launch traced here: 256 us
  blocking collectives  221 us (86%)
  starting transfers between devices  16.4 us (6%)
  matrix products  4.38 us (2%)
  waiting for transfers between devices  3.58 us (1%)
  Pallas kernels  3.41 us (1%)
  local copies, waits for them, and re-layouts  3.24 us (1%)
    all_to_all x13, blocking collectives, exchange(): return lax.all_to_all(v, axes, split_axis=0, concat_axis=0, tiled=True)  221 us
    all_to_all x1, starting transfers between devices, exchange(): return lax.all_to_all(v, axes, split_axis=0, concat_axis=0, tiled=True)  6.22 us
    ppermute x1, starting transfers between devices, body(): chosen = lax.ppermute(picked, ('zh', 'y', 'core'), swap)  5.74 us
  transfers between devices with their start and end apart: 3, of which 2 were waited for; matrix products, arithmetic and copies ran while one was open for 0% of the time, Pallas kernels for 0%

profile of v9, /device:TPU:1, one launch (start us, length us, event | category | flops | bytes accessed | tf_op | source)
XLA Modules:
  0.0 255.9 jit_solution(16014364593620636350)
XLA Ops:
  0.6 3.4 %shard_map.120 = (bf16[4,512]{1,0:T(4,128)(2,1)}, bf16[8,6,64,112]{3,2,1,0:T(8,128)(2,1)}) custom-call(s32[4]{0:T(128)} %picks.1, bf16[1024,512]{1,0:T(8,128)(2,1)} %pool.1, bf16[64,896]{1,0:T(8,128)(2,1)} %refs_0_.1, bf16[64,896]{1,0:T(8,128)(2,1)} %refs_1_.1, f32[64,896]{1,0:T(8,128)} %refs_2_.1, f32[64,896]{1,0:T(8,128)} %refs_3_.1, ...), custom_call_target="tpu_custom_call" | custom-call | bytes 2097152 | tf_op jit(solution)/shard_map/pallas_call | solution.py:96
  4.1 6.2 %all-to-all-start = ((bf16[8,6,64,112]{3,2,1,0:T(8,128)(2,1)}), bf16[8,6,64,112]{3,2,1,0:T(8,128)(2,1)S(1)}, u32[]{:S(2)}, u32[]{:S(2)}) async-start(bf16[8,6,64,112]{3,2,1,0:T(8,128)(2,1)} %get-tuple-element.255), calls=%async_computation | async-start | bytes 1572864 | tf_op jit(solution)/shard_map/all_to_all | solution.py:27
  10.3 5.7 %collective-permute-start = (bf16[4,512]{1,0:T(4,128)(2,1)S(1)}, bf16[4,512]{1,0:T(4,128)(2,1)S(1)}, u32[]{:S(2)}, u32[]{:S(2)}) collective-permute-start(bf16[4,512]{1,0:T(4,128)(2,1)S(1)} %copy-done.1), channel_id=1, source_target_pairs={{0,0},{1,64},{2,128},{3,192},{4,256},{5,320},{6,384},{7,448},{64,1... | collective-permute-start | bytes 12296 | tf_op jit(solution)/shard_map/ppermute | solution.py:134
  16.4 2.2 all-to-all-done
  19.0 32.3 %all_to_all.70 = bf16[64,4,512]{2,1,0:T(4,128)(2,1)S(1)} all-to-all(bf16[64,4,512]{2,1,0:T(4,128)(2,1)S(1)} %broadcast_in_dim.38), channel_id=1, replica_groups=mesh['zh'=8,'zl'=2,'x'=4,'y'=4,'core'=2] {'zl','x','y','core'}, dimensions={0} | all-to-all | bytes 524288 | tf_op jit(solution)/shard_map/all_to_all | solution.py:27
  51.5 0.3 convolution_convert_fusion.1
  52.3 23.9 %all_to_all.71 = bf16[8,64,256]{2,1,0:T(8,128)(2,1)S(1)} all-to-all(bf16[8,64,256]{2,1,0:T(8,128)(2,1)S(1)} %copy.80), channel_id=1, replica_groups=mesh['zh'=8,'zl'=2,'x'=4,'y'=4,'core'=2] {'zh'}, dimensions={0} | all-to-all | bytes 524288 | tf_op jit(solution)/shard_map/all_to_all | solution.py:27
  76.4 19.8 %all_to_all.72 = bf16[8,28,256]{2,1,0:T(8,128)(2,1)S(1)} all-to-all(bf16[8,28,256]{2,1,0:T(8,128)(2,1)S(1)} %broadcast_in_dim.40), channel_id=1, replica_groups=mesh['zh'=8,'zl'=2,'x'=4,'y'=4,'core'=2] {'zh'}, dimensions={0} | all-to-all | bytes 229376 | tf_op jit(solution)/shard_map/all_to_all | solution.py:27
  96.2 0.3 fusion.1
  96.5 18.6 %all_to_all.73 = bf16[64,8,512]{2,1,0:T(8,128)(2,1)S(1)} all-to-all(bf16[64,8,512]{2,1,0:T(8,128)(2,1)S(1)} %fusion.1), channel_id=1, replica_groups=mesh['zh'=8,'zl'=2,'x'=4,'y'=4,'core'=2] {'zl','x','y','core'}, dimensions={0} | all-to-all | bytes 1048576 | tf_op jit(solution)/shard_map/all_to_all | solution.py:27
  115.3 12.0 %all_to_all.74 = bf16[32,24,256]{2,1,0:T(8,128)(2,1)S(1)} all-to-all(bf16[32,24,256]{2,1,0:T(8,128)(2,1)S(1)} %broadcast_in_dim.41), channel_id=1, replica_groups=mesh['zh'=8,'zl'=2,'x'=4,'y'=4,'core'=2] {'zl','x','y'}, dimensions={0} | all-to-all | bytes 786432 | tf_op jit(solution)/shard_map/all_to_all | solution.py:27
  127.3 4.4 %collective-permute-start.1 = (bf16[32,24,256]{2,1,0:T(8,128)(2,1)S(1)}, bf16[32,24,256]{2,1,0:T(8,128)(2,1)S(1)}, u32[]{:S(2)}, u32[]{:S(2)}) collective-permute-start(bf16[32,24,256]{2,1,0:T(8,128)(2,1)S(1)} %all_to_all.74), channel_id=1, source_target_pairs={{0,1},{1,0},{2,3},{3,2},{4,5},{5,4},{6,7},{7,6},{8,9},{9,8},{10,11... | collective-permute-start | bytes 1179656 | tf_op jit(solution)/shard_map/ppermute | solution.py:45
  131.7 1.3 collective-permute-done.1
  133.3 0.3 convolution_convert_fusion.2
  133.9 0.3 multiply_reduce_fusion.2
  134.3 16.0 %all_to_all.75 = bf16[8,14,512]{2,1,0:T(8,128)(2,1)S(1)} all-to-all(bf16[8,14,512]{2,1,0:T(8,128)(2,1)S(1)} %reshape.141), channel_id=1, replica_groups=mesh['zh'=8,'zl'=2,'x'=4,'y'=4,'core'=2] {'zh'}, dimensions={0} | all-to-all | bytes 229376 | tf_op jit(solution)/shard_map/all_to_all | solution.py:27
  150.7 16.4 %all_to_all.76 = bf16[8,16,256]{2,1,0:T(8,128)(2,1)S(1)} all-to-all(bf16[8,16,256]{2,1,0:T(8,128)(2,1)S(1)} %broadcast_in_dim.44), channel_id=1, replica_groups=mesh['zh'=8,'zl'=2,'x'=4,'y'=4,'core'=2] {'zh'}, dimensions={0} | all-to-all | bytes 131072 | tf_op jit(solution)/shard_map/all_to_all | solution.py:27
  167.4 0.3 fusion.3
  167.9 0.4 pad_maximum_fusion
  168.3 16.9 %all_to_all.77 = bf16[64,9,2,128]{3,2,1,0:T(2,128)(2,1)S(1)} all-to-all(bf16[64,9,2,128]{3,2,1,0:T(2,128)(2,1)S(1)} %pad_maximum_fusion), channel_id=1, replica_groups=mesh['zh'=8,'zl'=2,'x'=4,'y'=4,'core'=2] {'zl','x','y','core'}, dimensions={0} | all-to-all | bytes 589824 | tf_op jit(solution)/shard_map/all_to_all | solution.py:27
  185.7 13.8 %all_to_all.78 = bf16[64,8,256]{2,1,0:T(8,128)(2,1)S(1)} all-to-all(bf16[64,8,256]{2,1,0:T(8,128)(2,1)S(1)} %broadcast_in_dim.47), channel_id=1, replica_groups=mesh['zh'=8,'zl'=2,'x'=4,'y'=4,'core'=2] {'zl','x','y','core'}, dimensions={0} | all-to-all | bytes 524288 | tf_op jit(solution)/shard_map/all_to_all | solution.py:27
  199.5 0.2 fusion.28
  199.9 0.3 multiply_reduce_fusion
  200.5 14.3 %all_to_all.79 = bf16[8,14,256]{2,1,0:T(8,128)(2,1)S(1)} all-to-all(bf16[8,14,256]{2,1,0:T(8,128)(2,1)S(1)} %reshape.147), channel_id=1, replica_groups=mesh['zh'=8,'zl'=2,'x'=4,'y'=4,'core'=2] {'zh'}, dimensions={0} | all-to-all | bytes 114688 | tf_op jit(solution)/shard_map/all_to_all | solution.py:27
  215.5 16.2 %all_to_all.80 = bf16[8,32,256]{2,1,0:T(8,128)(2,1)S(1)} all-to-all(bf16[8,32,256]{2,1,0:T(8,128)(2,1)S(1)} %broadcast_in_dim.105), channel_id=1, replica_groups=mesh['zh'=8,'zl'=2,'x'=4,'y'=4,'core'=2] {'zh'}, dimensions={0} | all-to-all | bytes 262144 | tf_op jit(solution)/shard_map/all_to_all | solution.py:27
  232.7 9.3 %all_to_all.81 = bf16[8,196,128]{2,1,0:T(8,128)(2,1)S(1)} all-to-all(bf16[8,196,128]{2,1,0:T(8,128)(2,1)S(1)} %fusion.23), channel_id=1, replica_groups=mesh['zh'=8,'zl'=2,'x'=4,'y'=4,'core'=2] {'zl','x'}, dimensions={0} | all-to-all | bytes 802816 | tf_op jit(solution)/shard_map/all_to_all | solution.py:27
  242.1 0.3 copy.87
  242.4 0.3 reshape.154
  242.7 11.5 %all_to_all.82 = f32[8,2,128]{2,1,0:T(2,128)S(1)} all-to-all(f32[8,2,128]{2,1,0:T(2,128)S(1)} %broadcast_in_dim.107), channel_id=1, replica_groups=mesh['zh'=8,'zl'=2,'x'=4,'y'=4,'core'=2] {'y','core'}, dimensions={0} | all-to-all | bytes 16384 | tf_op jit(solution)/shard_map/all_to_all | solution.py:27
  254.3 0.2 convolution_multiply_fusion
  254.5 0.5 slice.209
  255.0 0.9 fusion.37
  (104 shorter events, 5.5 us)
Async XLA Ops:
  4.0 6.2 %copy-start.1 = (bf16[4,512]{1,0:T(4,128)(2,1)S(1)}, bf16[4,512]{1,0:T(4,128)(2,1)}, u32[]{:S(2)}) copy-start(bf16[4,512]{1,0:T(4,128)(2,1)} %get-tuple-element.254) | copy-start | bytes 12292
  4.1 12.0 %copy-start = (bf16[256,64]{0,1:T(8,128)(2,1)S(1)}, bf16[256,64]{0,1:T(8,128)(2,1)}, u32[]{:S(2)}) copy-start(bf16[256,64]{0,1:T(8,128)(2,1)} %param.11) | copy-start | bytes 98308
  4.1 14.5 %all-to-all-start = ((bf16[8,6,64,112]{3,2,1,0:T(8,128)(2,1)}), bf16[8,6,64,112]{3,2,1,0:T(8,128)(2,1)S(1)}, u32[]{:S(2)}, u32[]{:S(2)}) async-start(bf16[8,6,64,112]{3,2,1,0:T(8,128)(2,1)} %get-tuple-element.255), calls=%async_computation | async-start | bytes 1572864 | tf_op jit(solution)/shard_map/all_to_all | solution.py:27
  10.3 8.6 %collective-permute-start = (bf16[4,512]{1,0:T(4,128)(2,1)S(1)}, bf16[4,512]{1,0:T(4,128)(2,1)S(1)}, u32[]{:S(2)}, u32[]{:S(2)}) collective-permute-start(bf16[4,512]{1,0:T(4,128)(2,1)S(1)} %copy-done.1), channel_id=1, source_target_pairs={{0,0},{1,64},{2,128},{3,192},{4,256},{5,320},{6,384},{7,448},{64,1... | collective-permute-start | bytes 12296 | tf_op jit(solution)/shard_map/ppermute | solution.py:134
  127.3 5.8 %collective-permute-start.1 = (bf16[32,24,256]{2,1,0:T(8,128)(2,1)S(1)}, bf16[32,24,256]{2,1,0:T(8,128)(2,1)S(1)}, u32[]{:S(2)}, u32[]{:S(2)}) collective-permute-start(bf16[32,24,256]{2,1,0:T(8,128)(2,1)S(1)} %all_to_all.74), channel_id=1, source_target_pairs={{0,1},{1,0},{2,3},{3,2},{4,5},{5,4},{6,7},{7,6},{8,9},{9,8},{10,11... | collective-permute-start | bytes 1179656 | tf_op jit(solution)/shard_map/ppermute | solution.py:45

commit v10 on v9

--- a/solution.py
+++ b/solution.py
@@ -213,10 +213,13 @@
             v = jnp.sum(v, axis=0, keepdims=True)
             return jnp.pad(v, ((0, 0), (0, tokens - v.shape[1])))
 
+        def wide_lanes(v):
+            return jnp.sum(jnp.sum(v, axis=1).reshape(-1, tokens), axis=0, keepdims=True)
+
         def terms(*values):
             return jnp.concatenate([t for v in values for t in two_terms(v)])
 
-        live["square"] = lanes(hv_down * hv_down)
+        live["square"] = wide_lanes(hv_down * hv_down)
         got, live = alone(back.reshape(nz, sub, 2 * tokens), "zh", live)
         got = jnp.sum(got.astype(F32), axis=0)
         live["back"] = got[:, :tokens]
@@ -249,19 +252,17 @@
         square = jnp.sum(both[:, sub:].astype(F32), axis=(0, 1))[None]
 
         half = tokens // 2
+        live["square"] = terms(square[:, :half] + square[:, half:])
         out = dot(live["down"], tan_hidden, 1, 0)
         out = (out + dot(live["hv_down_b"], live["hidden"], 1, 0)).astype(BF)
-        out = out.reshape(nr, rows, 2, half)
-        scal = terms(square[:, :half] + square[:, half:])
-        scal = jnp.broadcast_to(scal[None, None], (nr, 1, 2, half))
-        got, live = alone(jnp.concatenate([out, scal], axis=1), REST, live)
-        got, square = got[:, :rows].astype(F32), got[:, rows:].astype(F32)
-        square = jnp.sum(square, axis=(0, 1, 2))[None]
+        got, live = alone(out.reshape(nr, rows, tokens), REST, live)
+        tan_resid = (jnp.sum(got.astype(F32), axis=0) / tokens).astype(BF)
+        packed = tan_resid.reshape(rows, 2, half)
+        packed = jnp.concatenate([packed, live.pop("square")[None]])
+        both, live = gather(packed, REST, nr, live)
+        tan_resid = both[:, :rows].reshape(dz, tokens)
+        square = jnp.sum(both[:, rows:].astype(F32), axis=(0, 1, 2))[None]
         live["scale"] = 1.0 / jnp.sqrt(total(square, tokens) / count + 1e-6)
-        got = jnp.sum(got, axis=0).reshape(rows, tokens)
-        tan_resid = (got / tokens).astype(BF)
-        tan_resid, live = gather(tan_resid, REST, nr, live)
-        tan_resid = tan_resid.reshape(dz, tokens)
 
         resid = live.pop("resid")
         back = dot(live.pop("down"), tan_resid, 0, 0)
@@ -270,8 +271,8 @@
         hv_down2 = dot(resid, live.pop("tan_hidden"), 1, 1)
         hv_down2 = hv_down2 + dot(tan_resid, live.pop("hidden"), 1, 1)
         hv_down2 = hv_down2 * scale[:, :ff]
-        live["inner"] = lanes((live.pop("hv_down") * scale[:, :ff]) * hv_down2)
-        live["square"] = lanes(hv_down2 * hv_down2)
+        live["inner"] = wide_lanes((live.pop("hv_down") * scale[:, :ff]) * hv_down2)
+        live["square"] = wide_lanes(hv_down2 * hv_down2)
         live["hv_down"] = hv_down2.astype(BF)
         live["scale"] = scale
         got, live = alone(back.reshape(nz, sub, tokens), "zh", live)

time: 257 us -> 256 us (level)
  no operation moved by 1% of the time
where the time goes in v10:
time: 256 us
  blocking collectives  221 us (86%)
  starting transfers between devices  16.4 us (6%)
  matrix products  4.22 us (2%)
  waiting for transfers between devices  3.58 us (1%)
  Pallas kernels  3.41 us (1%)
  local copies, waits for them, and re-layouts  3.22 us (1%)
    all_to_all x13, blocking collectives, exchange(): return lax.all_to_all(v, axes, split_axis=0, concat_axis=0, tiled=True)  221 us
    all_to_all x1, starting transfers between devices, exchange(): return lax.all_to_all(v, axes, split_axis=0, concat_axis=0, tiled=True)  6.22 us
    ppermute x1, starting transfers between devices, body(): chosen = lax.ppermute(picked, ('zh', 'y', 'core'), swap)  5.74 us
  transfers between devices with their start and end apart: 3, of which 2 were waited for; matrix products, arithmetic and copies ran while one was open for 0% of the time, Pallas kernels for 0%

profile of v10, /device:TPU:1, one launch (start us, length us, event | category | flops | bytes accessed | tf_op | source)
XLA Modules:
  0.0 255.7 jit_solution(16656011520836286643)
XLA Ops:
  0.6 3.4 %shard_map.120 = (bf16[4,512]{1,0:T(4,128)(2,1)}, bf16[8,6,64,112]{3,2,1,0:T(8,128)(2,1)}) custom-call(s32[4]{0:T(128)} %picks.1, bf16[1024,512]{1,0:T(8,128)(2,1)} %pool.1, bf16[64,896]{1,0:T(8,128)(2,1)} %refs_0_.1, bf16[64,896]{1,0:T(8,128)(2,1)} %refs_1_.1, f32[64,896]{1,0:T(8,128)} %refs_2_.1, f32[64,896]{1,0:T(8,128)} %refs_3_.1, ...), custom_call_target="tpu_custom_call" | custom-call | bytes 2097152 | tf_op jit(solution)/shard_map/pallas_call | solution.py:96
  4.1 6.2 %all-to-all-start = ((bf16[8,6,64,112]{3,2,1,0:T(8,128)(2,1)}), bf16[8,6,64,112]{3,2,1,0:T(8,128)(2,1)S(1)}, u32[]{:S(2)}, u32[]{:S(2)}) async-start(bf16[8,6,64,112]{3,2,1,0:T(8,128)(2,1)} %get-tuple-element.255), calls=%async_computation | async-start | bytes 1572864 | tf_op jit(solution)/shard_map/all_to_all | solution.py:27
  10.3 5.7 %collective-permute-start = (bf16[4,512]{1,0:T(4,128)(2,1)S(1)}, bf16[4,512]{1,0:T(4,128)(2,1)S(1)}, u32[]{:S(2)}, u32[]{:S(2)}) collective-permute-start(bf16[4,512]{1,0:T(4,128)(2,1)S(1)} %copy-done.1), channel_id=1, source_target_pairs={{0,0},{1,64},{2,128},{3,192},{4,256},{5,320},{6,384},{7,448},{64,1... | collective-permute-start | bytes 12296 | tf_op jit(solution)/shard_map/ppermute | solution.py:134
  16.4 2.2 all-to-all-done
  19.0 32.3 %all_to_all.70 = bf16[64,4,512]{2,1,0:T(4,128)(2,1)S(1)} all-to-all(bf16[64,4,512]{2,1,0:T(4,128)(2,1)S(1)} %broadcast_in_dim.38), channel_id=1, replica_groups=mesh['zh'=8,'zl'=2,'x'=4,'y'=4,'core'=2] {'zl','x','y','core'}, dimensions={0} | all-to-all | bytes 524288 | tf_op jit(solution)/shard_map/all_to_all | solution.py:27
  51.5 0.3 convolution_convert_fusion.1
  52.3 23.9 %all_to_all.71 = bf16[8,64,256]{2,1,0:T(8,128)(2,1)S(1)} all-to-all(bf16[8,64,256]{2,1,0:T(8,128)(2,1)S(1)} %copy.119), channel_id=1, replica_groups=mesh['zh'=8,'zl'=2,'x'=4,'y'=4,'core'=2] {'zh'}, dimensions={0} | all-to-all | bytes 524288 | tf_op jit(solution)/shard_map/all_to_all | solution.py:27
  76.4 19.8 %all_to_all.72 = bf16[8,28,256]{2,1,0:T(8,128)(2,1)S(1)} all-to-all(bf16[8,28,256]{2,1,0:T(8,128)(2,1)S(1)} %broadcast_in_dim.40), channel_id=1, replica_groups=mesh['zh'=8,'zl'=2,'x'=4,'y'=4,'core'=2] {'zh'}, dimensions={0} | all-to-all | bytes 229376 | tf_op jit(solution)/shard_map/all_to_all | solution.py:27
  96.2 0.3 fusion.1
  96.5 18.6 %all_to_all.73 = bf16[64,8,512]{2,1,0:T(8,128)(2,1)S(1)} all-to-all(bf16[64,8,512]{2,1,0:T(8,128)(2,1)S(1)} %fusion.1), channel_id=1, replica_groups=mesh['zh'=8,'zl'=2,'x'=4,'y'=4,'core'=2] {'zl','x','y','core'}, dimensions={0} | all-to-all | bytes 1048576 | tf_op jit(solution)/shard_map/all_to_all | solution.py:27
  115.3 12.0 %all_to_all.74 = bf16[32,24,256]{2,1,0:T(8,128)(2,1)S(1)} all-to-all(bf16[32,24,256]{2,1,0:T(8,128)(2,1)S(1)} %broadcast_in_dim.41), channel_id=1, replica_groups=mesh['zh'=8,'zl'=2,'x'=4,'y'=4,'core'=2] {'zl','x','y'}, dimensions={0} | all-to-all | bytes 786432 | tf_op jit(solution)/shard_map/all_to_all | solution.py:27
  127.3 4.4 %collective-permute-start.1 = (bf16[32,24,256]{2,1,0:T(8,128)(2,1)S(1)}, bf16[32,24,256]{2,1,0:T(8,128)(2,1)S(1)}, u32[]{:S(2)}, u32[]{:S(2)}) collective-permute-start(bf16[32,24,256]{2,1,0:T(8,128)(2,1)S(1)} %all_to_all.74), channel_id=1, source_target_pairs={{0,1},{1,0},{2,3},{3,2},{4,5},{5,4},{6,7},{7,6},{8,9},{9,8},{10,11... | collective-permute-start | bytes 1179656 | tf_op jit(solution)/shard_map/ppermute | solution.py:45
  131.7 1.3 collective-permute-done.1
  133.3 0.3 convolution_convert_fusion.2
  133.9 0.2 multiply_reduce_fusion.2
  134.2 15.9 %all_to_all.75 = bf16[8,14,512]{2,1,0:T(8,128)(2,1)S(1)} all-to-all(bf16[8,14,512]{2,1,0:T(8,128)(2,1)S(1)} %reshape.143), channel_id=1, replica_groups=mesh['zh'=8,'zl'=2,'x'=4,'y'=4,'core'=2] {'zh'}, dimensions={0} | all-to-all | bytes 229376 | tf_op jit(solution)/shard_map/all_to_all | solution.py:27
  150.6 16.5 %all_to_all.76 = bf16[8,16,256]{2,1,0:T(8,128)(2,1)S(1)} all-to-all(bf16[8,16,256]{2,1,0:T(8,128)(2,1)S(1)} %broadcast_in_dim.44), channel_id=1, replica_groups=mesh['zh'=8,'zl'=2,'x'=4,'y'=4,'core'=2] {'zh'}, dimensions={0} | all-to-all | bytes 131072 | tf_op jit(solution)/shard_map/all_to_all | solution.py:27
  167.4 0.2 fusion.3
  167.6 16.6 %all_to_all.77 = bf16[64,8,256]{2,1,0:T(8,128)(2,1)S(1)} all-to-all(bf16[64,8,256]{2,1,0:T(8,128)(2,1)S(1)} %fusion.3), channel_id=1, replica_groups=mesh['zh'=8,'zl'=2,'x'=4,'y'=4,'core'=2] {'zl','x','y','core'}, dimensions={0} | all-to-all | bytes 524288 | tf_op jit(solution)/shard_map/all_to_all | solution.py:27
  184.6 14.1 %all_to_all.78 = bf16[64,9,2,128]{3,2,1,0:T(2,128)(2,1)S(1)} all-to-all(bf16[64,9,2,128]{3,2,1,0:T(2,128)(2,1)S(1)} %broadcast_in_dim.47), channel_id=1, replica_groups=mesh['zh'=8,'zl'=2,'x'=4,'y'=4,'core'=2] {'zl','x','y','core'}, dimensions={0} | all-to-all | bytes 589824 | tf_op jit(solution)/shard_map/all_to_all | solution.py:27
  198.8 0.2 fusion.27
  199.4 0.2 fusion.100
  199.7 0.3 multiply_reduce_fusion
  200.0 14.3 %all_to_all.79 = bf16[8,14,256]{2,1,0:T(8,128)(2,1)S(1)} all-to-all(bf16[8,14,256]{2,1,0:T(8,128)(2,1)S(1)} %reshape.150), channel_id=1, replica_groups=mesh['zh'=8,'zl'=2,'x'=4,'y'=4,'core'=2] {'zh'}, dimensions={0} | all-to-all | bytes 114688 | tf_op jit(solution)/shard_map/all_to_all | solution.py:27
  214.9 16.3 %all_to_all.80 = bf16[8,32,256]{2,1,0:T(8,128)(2,1)S(1)} all-to-all(bf16[8,32,256]{2,1,0:T(8,128)(2,1)S(1)} %broadcast_in_dim.102), channel_id=1, replica_groups=mesh['zh'=8,'zl'=2,'x'=4,'y'=4,'core'=2] {'zh'}, dimensions={0} | all-to-all | bytes 262144 | tf_op jit(solution)/shard_map/all_to_all | solution.py:27
  232.2 9.3 %all_to_all.81 = bf16[8,196,128]{2,1,0:T(8,128)(2,1)S(1)} all-to-all(bf16[8,196,128]{2,1,0:T(8,128)(2,1)S(1)} %fusion.23), channel_id=1, replica_groups=mesh['zh'=8,'zl'=2,'x'=4,'y'=4,'core'=2] {'zl','x'}, dimensions={0} | all-to-all | bytes 802816 | tf_op jit(solution)/shard_map/all_to_all | solution.py:27
  241.6 0.3 copy.128
  241.9 0.3 reshape.159
  242.2 11.8 %all_to_all.82 = f32[8,2,128]{2,1,0:T(2,128)S(1)} all-to-all(f32[8,2,128]{2,1,0:T(2,128)S(1)} %broadcast_in_dim.104), channel_id=1, replica_groups=mesh['zh'=8,'zl'=2,'x'=4,'y'=4,'core'=2] {'y','core'}, dimensions={0} | all-to-all | bytes 16384 | tf_op jit(solution)/shard_map/all_to_all | solution.py:27
  254.0 0.2 convolution_multiply_fusion
  254.3 0.5 slice.211
  254.8 0.9 fusion.35
  (108 shorter events, 5.3 us)
Async XLA Ops:
  4.0 6.2 %copy-start.1 = (bf16[4,512]{1,0:T(4,128)(2,1)S(1)}, bf16[4,512]{1,0:T(4,128)(2,1)}, u32[]{:S(2)}) copy-start(bf16[4,512]{1,0:T(4,128)(2,1)} %get-tuple-element.254) | copy-start | bytes 12292
  4.1 12.0 %copy-start = (bf16[256,64]{0,1:T(8,128)(2,1)S(1)}, bf16[256,64]{0,1:T(8,128)(2,1)}, u32[]{:S(2)}) copy-start(bf16[256,64]{0,1:T(8,128)(2,1)} %param.11) | copy-start | bytes 98308
  4.1 14.5 %all-to-all-start = ((bf16[8,6,64,112]{3,2,1,0:T(8,128)(2,1)}), bf16[8,6,64,112]{3,2,1,0:T(8,128)(2,1)S(1)}, u32[]{:S(2)}, u32[]{:S(2)}) async-start(bf16[8,6,64,112]{3,2,1,0:T(8,128)(2,1)} %get-tuple-element.255), calls=%async_computation | async-start | bytes 1572864 | tf_op jit(solution)/shard_map/all_to_all | solution.py:27
  10.3 8.6 %collective-permute-start = (bf16[4,512]{1,0:T(4,128)(2,1)S(1)}, bf16[4,512]{1,0:T(4,128)(2,1)S(1)}, u32[]{:S(2)}, u32[]{:S(2)}) collective-permute-start(bf16[4,512]{1,0:T(4,128)(2,1)S(1)} %copy-done.1), channel_id=1, source_target_pairs={{0,0},{1,64},{2,128},{3,192},{4,256},{5,320},{6,384},{7,448},{64,1... | collective-permute-start | bytes 12296 | tf_op jit(solution)/shard_map/ppermute | solution.py:134
  127.3 5.8 %collective-permute-start.1 = (bf16[32,24,256]{2,1,0:T(8,128)(2,1)S(1)}, bf16[32,24,256]{2,1,0:T(8,128)(2,1)S(1)}, u32[]{:S(2)}, u32[]{:S(2)}) collective-permute-start(bf16[32,24,256]{2,1,0:T(8,128)(2,1)S(1)} %all_to_all.74), channel_id=1, source_target_pairs={{0,1},{1,0},{2,3},{3,2},{4,5},{5,4},{6,7},{7,6},{8,9},{9,8},{10,11... | collective-permute-start | bytes 1179656 | tf_op jit(solution)/shard_map/ppermute | solution.py:45

commit v11 on v10

--- a/solution.py
+++ b/solution.py
@@ -286,8 +286,9 @@
         square = lanes(by_gram(delta) * wide) + live.pop("square")
         del live["gram"], live["sums"], live["back"]
         both, live = gather(jnp.concatenate([delta, terms(inner, square)]), "zh", nz, live)
-        delta_gate = both[:, :sub].reshape(ff, tokens)
-        delta_up = both[:, sub : 2 * sub].reshape(ff, tokens)
+        delta = both[:, : 2 * sub].reshape(nz, 2, sub, tokens).transpose(1, 0, 2, 3)
+        hv = dot(delta.reshape(2 * ff, tokens), live["inputs"], 1, 0).astype(BF)
+        hv = hv.reshape(2, ff, dz).transpose(0, 2, 1)
         sums = both[:, 2 * sub :].reshape(nz, 2, 2, tokens).astype(F32)
         sums = jnp.sum(sums, axis=(0, 2))
         if tokens > LANES:
@@ -298,8 +299,8 @@
         hv = [
             jnp.pad(v.reshape(nx, d_dev, ff), ((0, 0), (0, 0), (0, LANES - ff)))
             for v in (
-                dot(live["inputs"], delta_gate, 0, 1).astype(BF),
-                dot(live["inputs"], delta_up, 0, 1).astype(BF),
+                hv[0],
+                hv[1],
                 live["hv_down"],
             )
         ]

time: 256 us -> 256 us (level)
  no operation moved by 1% of the time
where the time goes in v11:
time: 256 us
  blocking collectives  221 us (86%)
  starting transfers between devices  16.4 us (6%)
  matrix products  4.08 us (2%)
  waiting for transfers between devices  3.58 us (1%)
  Pallas kernels  3.41 us (1%)
  local copies, waits for them, and re-layouts  3.25 us (1%)
    all_to_all x13, blocking collectives, exchange(): return lax.all_to_all(v, axes, split_axis=0, concat_axis=0, tiled=True)  221 us
    all_to_all x1, starting transfers between devices, exchange(): return lax.all_to_all(v, axes, split_axis=0, concat_axis=0, tiled=True)  6.22 us
    ppermute x1, starting transfers between devices, body(): chosen = lax.ppermute(picked, ('zh', 'y', 'core'), swap)  5.74 us
  transfers between devices with their start and end apart: 3, of which 2 were waited for; matrix products, arithmetic and copies ran while one was open for 0% of the time, Pallas kernels for 0%

profile of v11, /device:TPU:1, one launch (start us, length us, event | category | flops | bytes accessed | tf_op | source)
XLA Modules:
  0.0 255.6 jit_solution(13021123497988172781)
XLA Ops:
  0.6 3.4 %shard_map.120 = (bf16[4,512]{1,0:T(4,128)(2,1)}, bf16[8,6,64,112]{3,2,1,0:T(8,128)(2,1)}) custom-call(s32[4]{0:T(128)} %picks.1, bf16[1024,512]{1,0:T(8,128)(2,1)} %pool.1, bf16[64,896]{1,0:T(8,128)(2,1)} %refs_0_.1, bf16[64,896]{1,0:T(8,128)(2,1)} %refs_1_.1, f32[64,896]{1,0:T(8,128)} %refs_2_.1, f32[64,896]{1,0:T(8,128)} %refs_3_.1, ...), custom_call_target="tpu_custom_call" | custom-call | bytes 2097152 | tf_op jit(solution)/shard_map/pallas_call | solution.py:96
  4.1 6.2 %all-to-all-start = ((bf16[8,6,64,112]{3,2,1,0:T(8,128)(2,1)}), bf16[8,6,64,112]{3,2,1,0:T(8,128)(2,1)S(1)}, u32[]{:S(2)}, u32[]{:S(2)}) async-start(bf16[8,6,64,112]{3,2,1,0:T(8,128)(2,1)} %get-tuple-element.255), calls=%async_computation | async-start | bytes 1572864 | tf_op jit(solution)/shard_map/all_to_all | solution.py:27
  10.3 5.7 %collective-permute-start = (bf16[4,512]{1,0:T(4,128)(2,1)S(1)}, bf16[4,512]{1,0:T(4,128)(2,1)S(1)}, u32[]{:S(2)}, u32[]{:S(2)}) collective-permute-start(bf16[4,512]{1,0:T(4,128)(2,1)S(1)} %copy-done.1), channel_id=1, source_target_pairs={{0,0},{1,64},{2,128},{3,192},{4,256},{5,320},{6,384},{7,448},{64,1... | collective-permute-start | bytes 12296 | tf_op jit(solution)/shard_map/ppermute | solution.py:134
  16.4 2.2 all-to-all-done
  19.0 32.3 %all_to_all.70 = bf16[64,4,512]{2,1,0:T(4,128)(2,1)S(1)} all-to-all(bf16[64,4,512]{2,1,0:T(4,128)(2,1)S(1)} %broadcast_in_dim.38), channel_id=1, replica_groups=mesh['zh'=8,'zl'=2,'x'=4,'y'=4,'core'=2] {'zl','x','y','core'}, dimensions={0} | all-to-all | bytes 524288 | tf_op jit(solution)/shard_map/all_to_all | solution.py:27
  51.5 0.3 convolution_convert_fusion.2
  52.3 23.9 %all_to_all.71 = bf16[8,64,256]{2,1,0:T(8,128)(2,1)S(1)} all-to-all(bf16[8,64,256]{2,1,0:T(8,128)(2,1)S(1)} %copy.123), channel_id=1, replica_groups=mesh['zh'=8,'zl'=2,'x'=4,'y'=4,'core'=2] {'zh'}, dimensions={0} | all-to-all | bytes 524288 | tf_op jit(solution)/shard_map/all_to_all | solution.py:27
  76.4 19.8 %all_to_all.72 = bf16[8,28,256]{2,1,0:T(8,128)(2,1)S(1)} all-to-all(bf16[8,28,256]{2,1,0:T(8,128)(2,1)S(1)} %broadcast_in_dim.40), channel_id=1, replica_groups=mesh['zh'=8,'zl'=2,'x'=4,'y'=4,'core'=2] {'zh'}, dimensions={0} | all-to-all | bytes 229376 | tf_op jit(solution)/shard_map/all_to_all | solution.py:27
  96.2 0.3 fusion.1
  96.5 18.6 %all_to_all.73 = bf16[64,8,512]{2,1,0:T(8,128)(2,1)S(1)} all-to-all(bf16[64,8,512]{2,1,0:T(8,128)(2,1)S(1)} %fusion.1), channel_id=1, replica_groups=mesh['zh'=8,'zl'=2,'x'=4,'y'=4,'core'=2] {'zl','x','y','core'}, dimensions={0} | all-to-all | bytes 1048576 | tf_op jit(solution)/shard_map/all_to_all | solution.py:27
  115.3 12.0 %all_to_all.74 = bf16[32,24,256]{2,1,0:T(8,128)(2,1)S(1)} all-to-all(bf16[32,24,256]{2,1,0:T(8,128)(2,1)S(1)} %broadcast_in_dim.41), channel_id=1, replica_groups=mesh['zh'=8,'zl'=2,'x'=4,'y'=4,'core'=2] {'zl','x','y'}, dimensions={0} | all-to-all | bytes 786432 | tf_op jit(solution)/shard_map/all_to_all | solution.py:27
  127.3 4.4 %collective-permute-start.1 = (bf16[32,24,256]{2,1,0:T(8,128)(2,1)S(1)}, bf16[32,24,256]{2,1,0:T(8,128)(2,1)S(1)}, u32[]{:S(2)}, u32[]{:S(2)}) collective-permute-start(bf16[32,24,256]{2,1,0:T(8,128)(2,1)S(1)} %all_to_all.74), channel_id=1, source_target_pairs={{0,1},{1,0},{2,3},{3,2},{4,5},{5,4},{6,7},{7,6},{8,9},{9,8},{10,11... | collective-permute-start | bytes 1179656 | tf_op jit(solution)/shard_map/ppermute | solution.py:45
  131.7 1.3 collective-permute-done.1
  133.3 0.3 convolution_convert_fusion.3
  133.9 0.2 multiply_reduce_fusion.2
  134.2 15.9 %all_to_all.75 = bf16[8,14,512]{2,1,0:T(8,128)(2,1)S(1)} all-to-all(bf16[8,14,512]{2,1,0:T(8,128)(2,1)S(1)} %reshape.140), channel_id=1, replica_groups=mesh['zh'=8,'zl'=2,'x'=4,'y'=4,'core'=2] {'zh'}, dimensions={0} | all-to-all | bytes 229376 | tf_op jit(solution)/shard_map/all_to_all | solution.py:27
  150.6 16.5 %all_to_all.76 = bf16[8,16,256]{2,1,0:T(8,128)(2,1)S(1)} all-to-all(bf16[8,16,256]{2,1,0:T(8,128)(2,1)S(1)} %broadcast_in_dim.44), channel_id=1, replica_groups=mesh['zh'=8,'zl'=2,'x'=4,'y'=4,'core'=2] {'zh'}, dimensions={0} | all-to-all | bytes 131072 | tf_op jit(solution)/shard_map/all_to_all | solution.py:27
  167.4 0.2 fusion.3
  167.6 16.6 %all_to_all.77 = bf16[64,8,256]{2,1,0:T(8,128)(2,1)S(1)} all-to-all(bf16[64,8,256]{2,1,0:T(8,128)(2,1)S(1)} %fusion.3), channel_id=1, replica_groups=mesh['zh'=8,'zl'=2,'x'=4,'y'=4,'core'=2] {'zl','x','y','core'}, dimensions={0} | all-to-all | bytes 524288 | tf_op jit(solution)/shard_map/all_to_all | solution.py:27
  184.6 14.1 %all_to_all.78 = bf16[64,9,2,128]{3,2,1,0:T(2,128)(2,1)S(1)} all-to-all(bf16[64,9,2,128]{3,2,1,0:T(2,128)(2,1)S(1)} %broadcast_in_dim.47), channel_id=1, replica_groups=mesh['zh'=8,'zl'=2,'x'=4,'y'=4,'core'=2] {'zl','x','y','core'}, dimensions={0} | all-to-all | bytes 589824 | tf_op jit(solution)/shard_map/all_to_all | solution.py:27
  198.8 0.2 fusion.27
  199.4 0.2 fusion.100
  199.7 0.3 multiply_reduce_fusion
  200.0 14.3 %all_to_all.79 = bf16[8,14,256]{2,1,0:T(8,128)(2,1)S(1)} all-to-all(bf16[8,14,256]{2,1,0:T(8,128)(2,1)S(1)} %reshape.147), channel_id=1, replica_groups=mesh['zh'=8,'zl'=2,'x'=4,'y'=4,'core'=2] {'zh'}, dimensions={0} | all-to-all | bytes 114688 | tf_op jit(solution)/shard_map/all_to_all | solution.py:27
  214.9 16.3 %all_to_all.80 = bf16[8,32,256]{2,1,0:T(8,128)(2,1)S(1)} all-to-all(bf16[8,32,256]{2,1,0:T(8,128)(2,1)S(1)} %broadcast_in_dim.102), channel_id=1, replica_groups=mesh['zh'=8,'zl'=2,'x'=4,'y'=4,'core'=2] {'zh'}, dimensions={0} | all-to-all | bytes 262144 | tf_op jit(solution)/shard_map/all_to_all | solution.py:27
  232.1 9.3 %all_to_all.81 = bf16[8,196,128]{2,1,0:T(8,128)(2,1)S(1)} all-to-all(bf16[8,196,128]{2,1,0:T(8,128)(2,1)S(1)} %fusion.23), channel_id=1, replica_groups=mesh['zh'=8,'zl'=2,'x'=4,'y'=4,'core'=2] {'zl','x'}, dimensions={0} | all-to-all | bytes 802816 | tf_op jit(solution)/shard_map/all_to_all | solution.py:27
  241.5 0.3 copy.133
  241.8 0.3 reshape.155
  242.1 11.8 %all_to_all.82 = f32[8,2,128]{2,1,0:T(2,128)S(1)} all-to-all(f32[8,2,128]{2,1,0:T(2,128)S(1)} %broadcast_in_dim.104), channel_id=1, replica_groups=mesh['zh'=8,'zl'=2,'x'=4,'y'=4,'core'=2] {'y','core'}, dimensions={0} | all-to-all | bytes 16384 | tf_op jit(solution)/shard_map/all_to_all | solution.py:27
  253.9 0.2 convolution_multiply_fusion
  254.2 0.5 slice.218
  254.7 0.9 fusion.35
  (108 shorter events, 5.2 us)
Async XLA Ops:
  4.0 6.2 %copy-start.1 = (bf16[4,512]{1,0:T(4,128)(2,1)S(1)}, bf16[4,512]{1,0:T(4,128)(2,1)}, u32[]{:S(2)}) copy-start(bf16[4,512]{1,0:T(4,128)(2,1)} %get-tuple-element.254) | copy-start | bytes 12292
  4.1 12.0 %copy-start = (bf16[256,64]{0,1:T(8,128)(2,1)S(1)}, bf16[256,64]{0,1:T(8,128)(2,1)}, u32[]{:S(2)}) copy-start(bf16[256,64]{0,1:T(8,128)(2,1)} %param.11) | copy-start | bytes 98308
  4.1 14.5 %all-to-all-start = ((bf16[8,6,64,112]{3,2,1,0:T(8,128)(2,1)}), bf16[8,6,64,112]{3,2,1,0:T(8,128)(2,1)S(1)}, u32[]{:S(2)}, u32[]{:S(2)}) async-start(bf16[8,6,64,112]{3,2,1,0:T(8,128)(2,1)} %get-tuple-element.255), calls=%async_computation | async-start | bytes 1572864 | tf_op jit(solution)/shard_map/all_to_all | solution.py:27
  10.3 8.6 %collective-permute-start = (bf16[4,512]{1,0:T(4,128)(2,1)S(1)}, bf16[4,512]{1,0:T(4,128)(2,1)S(1)}, u32[]{:S(2)}, u32[]{:S(2)}) collective-permute-start(bf16[4,512]{1,0:T(4,128)(2,1)S(1)} %copy-done.1), channel_id=1, source_target_pairs={{0,0},{1,64},{2,128},{3,192},{4,256},{5,320},{6,384},{7,448},{64,1... | collective-permute-start | bytes 12296 | tf_op jit(solution)/shard_map/ppermute | solution.py:134
  127.3 5.8 %collective-permute-start.1 = (bf16[32,24,256]{2,1,0:T(8,128)(2,1)S(1)}, bf16[32,24,256]{2,1,0:T(8,128)(2,1)S(1)}, u32[]{:S(2)}, u32[]{:S(2)}) collective-permute-start(bf16[32,24,256]{2,1,0:T(8,128)(2,1)S(1)} %all_to_all.74), channel_id=1, source_target_pairs={{0,1},{1,0},{2,3},{3,2},{4,5},{5,4},{6,7},{7,6},{8,9},{9,8},{10,11... | collective-permute-start | bytes 1179656 | tf_op jit(solution)/shard_map/ppermute | solution.py:45
